TPU v7x, 32 devices: a whole 2x2x4 slice. The times are simulated.
32 devices in a mesh: dp: 2 (over y), context: 8 (over z, x), tensor: 2 (over core).
Axes of the slice: x: 2, y: 2, z: 4, core: 2. Of those that a mesh axis runs over, the one named last changes fastest.
Arguments:
- tokens: bfloat16 [2, 1024, 2304], P('dp', 'context'), may hold values from -6 to 6
- w_query: bfloat16 [2304, 2048], P(('dp', 'context'), 'tensor'), may hold values from -0.21875 to 0.21875
- w_key: bfloat16 [2304, 1024], P(('dp', 'context'), 'tensor'), may hold values from -0.21875 to 0.21875
- w_value: bfloat16 [2304, 1024], P(('dp', 'context'), 'tensor'), may hold values from -0.125 to 0.125
- w_out: bfloat16 [2304, 2048], P(('dp', 'context'), 'tensor'), may hold values from -0.125 to 0.125
- w_gate: bfloat16 [2304, 9216], P(('dp', 'context'), 'tensor'), may hold values from -0.125 to 0.125
- w_up: bfloat16 [2304, 9216], P(('dp', 'context'), 'tensor'), may hold values from -0.125 to 0.125
- w_down: bfloat16 [2304, 9216], P(('dp', 'context'), 'tensor'), may hold values from -0.0625 to 0.0625
- gain_attn_in: bfloat16 [2304], P(('dp', 'context')), may hold values from 0.5 to 1.5
- gain_attn_out: bfloat16 [2304], P(('dp', 'context')), may hold values from 0.5 to 1.5
- gain_ffw_in: bfloat16 [2304], P(('dp', 'context')), may hold values from 0.5 to 1.5
- gain_ffw_out: bfloat16 [2304], P(('dp', 'context')), may hold values from 0.5 to 1.5
- cotangent: float32 [2, 1024, 2304], P('dp', 'context'), may hold values from -6 to 6
Outputs:
- layer_output: bfloat16 [2, 1024, 2304], P('dp', 'context')
- input_grad: float32 [2, 1024, 2304], P('dp', 'context')
- grad_query: float32 [2304, 2048], P(('dp', 'context'), 'tensor')
- grad_key: float32 [2304, 1024], P(('dp', 'context'), 'tensor')
- grad_value: float32 [2304, 1024], P(('dp', 'context'), 'tensor')
- grad_out: float32 [2304, 2048], P(('dp', 'context'), 'tensor')
- grad_gate: float32 [2304, 9216], P(('dp', 'context'), 'tensor')
- grad_up: float32 [2304, 9216], P(('dp', 'context'), 'tensor')
- grad_down: float32 [2304, 9216], P(('dp', 'context'), 'tensor')
- grad_attn_in: float32 [2304], P(('dp', 'context'))
- grad_attn_out: float32 [2304], P(('dp', 'context'))
- grad_ffw_in: float32 [2304], P(('dp', 'context'))
- grad_ffw_out: float32 [2304], P(('dp', 'context'))
All inputs are finite; a program needn't handle non-finite values.
Results may differ from a plain program's by a relative error of at most 0.025.
Values may be sent and summed in bfloat16 or wider, within the bound.
No kernel may reach another device: no remote copies, remote signals or barrier semaphores. Data moves between devices by JAX's collectives and lax.ppermute only.
A program may use at most 576 MiB of HBM per device.

v0:
```python
import jax
import jax.numpy as jnp
from jax import lax
from jax.sharding import PartitionSpec as P

HEAD_DIM = 256


epsilon = 1e-06
softcap = 50.0
theta = 10000.0
floor_value = -1e30


def rms_norm(values, scaling):
    return values * lax.rsqrt(jnp.mean(values * values, axis=-1, keepdims=True) + epsilon) * scaling


def rotate(values, positions, direction):
    half_width = values.shape[-1] // 2
    exponent = jnp.arange(half_width, dtype=jnp.float32) * (-2.0 / values.shape[-1])
    angles = direction * positions.astype(jnp.float32)[:, None] * (theta**exponent)[None, :]
    cosine = jnp.cos(angles)[:, None, :]
    sine_part = jnp.sin(angles)[:, None, :]
    former = values[..., :half_width]
    latter = values[..., half_width:]
    return jnp.concatenate(
        [former * cosine - latter * sine_part, latter * cosine + former * sine_part], axis=-1
    )


def product(left_side, right_side):
    return jnp.dot(left_side, right_side, preferred_element_type=jnp.float32)


def product_right_t(left_side, right_side):
    return lax.dot_general(
        left_side, right_side, (((1,), (1,)), ((), ())), preferred_element_type=jnp.float32
    )


def tensor_total(partial_value):
    return lax.psum(partial_value.astype(jnp.bfloat16), "tensor").astype(jnp.float32)


def norm_back(values, scaling, upstream):
    outcome, pullback = jax.vjp(rms_norm, values, scaling)
    return pullback(upstream)


def geglu(gate_in, upward):
    return jax.nn.gelu(gate_in, approximate=True) * upward


def body(
    tokens,
    w_query,
    w_key,
    w_value,
    w_out,
    w_gate,
    w_up,
    w_down,
    gain_attn_in,
    gain_attn_out,
    gain_ffw_in,
    gain_ffw_out,
    cotangent,
):
    tok_count = tokens.shape[1]
    cycle_count = lax.axis_size("context")
    my_index = lax.axis_index("context")
    length = tok_count * cycle_count
    first_place = my_index * tok_count
    positions = first_place + jnp.arange(tok_count, dtype=jnp.int32)
    last_place = first_place + tok_count - 1
    score_scale = HEAD_DIM ** (-0.5)
    groups = w_key.shape[1] // HEAD_DIM
    repeat = w_query.shape[1] // w_key.shape[1]
    inputs = tokens[0].astype(jnp.float32)
    attn_set = (
        lax.all_gather(w_query, ("dp", "context"), axis=0, tiled=True),
        lax.all_gather(w_key, ("dp", "context"), axis=0, tiled=True),
        lax.all_gather(w_value, ("dp", "context"), axis=0, tiled=True),
        lax.all_gather(w_out, ("dp", "context"), axis=0, tiled=True),
        lax.all_gather(gain_attn_in, ("dp", "context"), axis=0, tiled=True),
        lax.all_gather(gain_attn_out, ("dp", "context"), axis=0, tiled=True),
    )
    full_query, full_key, full_value, full_out, full_gin, full_gmid = attn_set
    scale_in = full_gin.astype(jnp.float32)
    scale_mid = full_gmid.astype(jnp.float32)
    normed = rms_norm(inputs, scale_in)
    normed_low = normed.astype(jnp.bfloat16)
    query_rot = rotate(
        product(normed_low, full_query).reshape(tok_count, groups * repeat, HEAD_DIM),
        positions,
        1.0,
    )
    key_rot = rotate(
        product(normed_low, full_key).reshape(tok_count, groups, HEAD_DIM), positions, 1.0
    )
    queries = query_rot.reshape(tok_count, groups, repeat, HEAD_DIM).astype(jnp.bfloat16)
    key_rows = key_rot.reshape(tok_count, groups * HEAD_DIM).astype(jnp.bfloat16)
    value_rows = product(normed_low, full_value).astype(jnp.bfloat16)
    heads_shape = (groups, repeat, tok_count)
    initial = (
        jnp.full(heads_shape, floor_value, jnp.float32),
        jnp.zeros(heads_shape, jnp.float32),
        jnp.zeros(heads_shape + (HEAD_DIM,), jnp.float32),
    )
    pieces = (
        lax.all_gather(key_rows, "context", axis=0, tiled=True),
        lax.all_gather(value_rows, "context", axis=0, tiled=True),
    )

    def attend_piece(current):
        running_top, running_total, running_acc = current
        piece_keys, piece_values = pieces
        piece_rows = piece_keys.shape[0]
        key_heads = piece_keys.reshape(piece_rows, groups, HEAD_DIM)
        value_heads = piece_values.reshape(piece_rows, groups, HEAD_DIM)
        scores = (
            jnp.einsum("tgrd,ngd->grtn", queries, key_heads, preferred_element_type=jnp.float32)
            * score_scale
        )
        capped = softcap * jnp.tanh(scores / softcap)
        allowed = jnp.arange(piece_rows, dtype=jnp.int32)[None, :] <= positions[:, None]
        capped = jnp.where(allowed, capped, floor_value)
        new_top = jnp.maximum(running_top, jnp.max(capped, axis=-1))
        weights = jnp.where(allowed, jnp.exp(capped - new_top[..., None]), 0.0)
        new_total = jnp.sum(weights, axis=-1)
        new_acc = jnp.einsum(
            "grtn,ngd->grtd",
            weights.astype(jnp.bfloat16),
            value_heads,
            preferred_element_type=jnp.float32,
        )
        return (new_top, new_total, new_acc)

    def visit_pass_through(current):
        return current

    run_top, run_total, run_acc = lax.cond(
        jnp.int32(0) <= last_place, attend_piece, visit_pass_through, initial
    )
    attention = run_acc / run_total[..., None]
    log_total = run_top + jnp.log(run_total)
    mixed = jnp.transpose(attention, (2, 0, 1, 3)).reshape(tok_count, groups * repeat * HEAD_DIM)
    mixed_low = mixed.astype(jnp.bfloat16)
    projected = tensor_total(product_right_t(mixed_low, full_out))
    middle = inputs + rms_norm(projected, scale_mid)
    mlp_set = (
        lax.all_gather(w_gate, ("dp", "context"), axis=0, tiled=True),
        lax.all_gather(w_up, ("dp", "context"), axis=0, tiled=True),
        lax.all_gather(w_down, ("dp", "context"), axis=0, tiled=True),
        lax.all_gather(gain_ffw_in, ("dp", "context"), axis=0, tiled=True),
        lax.all_gather(gain_ffw_out, ("dp", "context"), axis=0, tiled=True),
    )
    full_gate, full_up, full_down, full_gpre, full_gout = mlp_set
    scale_pre = full_gpre.astype(jnp.float32)
    scale_out = full_gout.astype(jnp.float32)
    normed_two = rms_norm(middle, scale_pre)
    normed_two_low = normed_two.astype(jnp.bfloat16)
    gate_in = product(normed_two_low, full_gate)
    upward = product(normed_two_low, full_up)
    hidden_low = geglu(gate_in, upward).astype(jnp.bfloat16)
    branch = tensor_total(product_right_t(hidden_low, full_down))
    layer_output = (middle + rms_norm(branch, scale_out)).astype(jnp.bfloat16)
    upstream = cotangent[0]
    d_branch, grad_ffw_out = norm_back(branch, scale_out, upstream)
    d_branch_low = d_branch.astype(jnp.bfloat16)
    back_mlp = (
        lax.all_gather(w_gate, ("dp", "context"), axis=0, tiled=True),
        lax.all_gather(w_up, ("dp", "context"), axis=0, tiled=True),
        lax.all_gather(w_down, ("dp", "context"), axis=0, tiled=True),
        lax.all_gather(gain_ffw_in, ("dp", "context"), axis=0, tiled=True),
        lax.all_gather(gain_ffw_out, ("dp", "context"), axis=0, tiled=True),
    )
    back_gate, back_up, back_down, back_gpre, back_gout = back_mlp
    d_hidden = product(d_branch_low, back_down)
    geglu_out, geglu_pull = jax.vjp(geglu, gate_in, upward)
    d_gate, d_up = geglu_pull(d_hidden)
    d_gate_low = d_gate.astype(jnp.bfloat16)
    d_up_low = d_up.astype(jnp.bfloat16)
    d_normed_two = tensor_total(
        product_right_t(d_gate_low, back_gate) + product_right_t(d_up_low, back_up)
    )
    d_middle_norm, grad_ffw_in = norm_back(middle, scale_pre, d_normed_two)
    d_middle = upstream + d_middle_norm
    ffw_cols = (
        lax.all_to_all(
            normed_two_low.T, ("dp", "context"), split_axis=0, concat_axis=1, tiled=True
        ),
        lax.all_to_all(d_branch_low.T, ("dp", "context"), split_axis=0, concat_axis=1, tiled=True),
    )
    piece_gate = lax.all_gather(d_gate_low, ("dp", "context"), axis=0, tiled=True)
    piece_up = lax.all_gather(d_up_low, ("dp", "context"), axis=0, tiled=True)
    piece_hidden = lax.all_gather(hidden_low, ("dp", "context"), axis=0, tiled=True)
    normed_cols = ffw_cols[0]
    branch_cols = ffw_cols[1]
    grad_gate = product(normed_cols, piece_gate)
    grad_up = product(normed_cols, piece_up)
    grad_down = product(branch_cols, piece_hidden)
    d_projected, grad_attn_out = norm_back(projected, scale_mid, d_middle)
    d_projected_low = d_projected.astype(jnp.bfloat16)
    back_attn = (
        lax.all_gather(w_query, ("dp", "context"), axis=0, tiled=True),
        lax.all_gather(w_key, ("dp", "context"), axis=0, tiled=True),
        lax.all_gather(w_value, ("dp", "context"), axis=0, tiled=True),
        lax.all_gather(w_out, ("dp", "context"), axis=0, tiled=True),
        lax.all_gather(gain_attn_in, ("dp", "context"), axis=0, tiled=True),
        lax.all_gather(gain_attn_out, ("dp", "context"), axis=0, tiled=True),
    )
    back_query, back_key, back_value, back_out, back_gin, back_gmid = back_attn
    d_mixed_low = product(d_projected_low, back_out).astype(jnp.bfloat16)
    d_mixed_heads = d_mixed_low.reshape(tok_count, groups, repeat, HEAD_DIM)
    delta = jnp.sum(
        jnp.transpose(d_mixed_heads, (1, 2, 0, 3)).astype(jnp.float32) * attention, axis=-1
    )

    def block_grads(key_block, value_block, offset):
        span = key_block.shape[0]
        key_heads = key_block.reshape(span, groups, HEAD_DIM)
        value_heads = value_block.reshape(span, groups, HEAD_DIM)
        scores = (
            jnp.einsum("tgrd,ngd->grtn", queries, key_heads, preferred_element_type=jnp.float32)
            * score_scale
        )
        bent = jnp.tanh(scores / softcap)
        capped = softcap * bent
        allowed = (offset + jnp.arange(span, dtype=jnp.int32))[None, :] <= positions[:, None]
        probabilities = jnp.where(allowed, jnp.exp(capped - log_total[..., None]), 0.0)
        d_prob = jnp.einsum(
            "tgrd,ngd->grtn", d_mixed_heads, value_heads, preferred_element_type=jnp.float32
        )
        d_capped = probabilities * (d_prob - delta[..., None])
        d_scores = (d_capped * (1.0 - bent * bent)).astype(jnp.bfloat16)
        d_query_part = (
            jnp.einsum("grtn,ngd->grtd", d_scores, key_heads, preferred_element_type=jnp.float32)
            * score_scale
        )
        d_key_block = (
            jnp.einsum("grtn,tgrd->ngd", d_scores, queries, preferred_element_type=jnp.float32)
            * score_scale
        )
        d_value_block = jnp.einsum(
            "grtn,tgrd->ngd",
            probabilities.astype(jnp.bfloat16),
            d_mixed_heads,
            preferred_element_type=jnp.float32,
        )
        return (
            d_query_part,
            d_key_block.reshape(span, groups * HEAD_DIM),
            d_value_block.reshape(span, groups * HEAD_DIM),
        )

    def pass_through(current):
        return current

    query_zero = jnp.zeros(heads_shape + (HEAD_DIM,), jnp.float32)
    all_keys, all_values = (
        lax.all_gather(key_rows, "context", axis=0, tiled=True),
        lax.all_gather(value_rows, "context", axis=0, tiled=True),
    )
    block_span = min(length, 1024)
    block_count = length // block_span

    def key_step(block_index, carried):

        def visit_block(current):
            d_query_acc, d_key_all, d_value_all = current
            offset = block_index * block_span
            key_block = lax.dynamic_slice_in_dim(all_keys, offset, block_span, 0)
            value_block = lax.dynamic_slice_in_dim(all_values, offset, block_span, 0)
            d_query_part, d_key_block, d_value_block = block_grads(key_block, value_block, offset)
            d_key_all = lax.dynamic_update_slice_in_dim(d_key_all, d_key_block, offset, 0)
            d_value_all = lax.dynamic_update_slice_in_dim(d_value_all, d_value_block, offset, 0)
            return (d_query_acc + d_query_part, d_key_all, d_value_all)

        return lax.cond(block_index * block_span <= last_place, visit_block, pass_through, carried)

    starting = (
        query_zero,
        jnp.zeros((length, groups * HEAD_DIM), jnp.float32),
        jnp.zeros((length, groups * HEAD_DIM), jnp.float32),
    )
    d_query_acc, d_key_all, d_value_all = lax.fori_loop(0, block_count, key_step, starting)
    d_key_mine, d_value_mine = (
        lax.psum_scatter(
            d_key_all.astype(jnp.bfloat16), "context", scatter_dimension=0, tiled=True
        ).astype(jnp.float32),
        lax.psum_scatter(
            d_value_all.astype(jnp.bfloat16), "context", scatter_dimension=0, tiled=True
        ).astype(jnp.float32),
    )
    d_query_heads = jnp.transpose(d_query_acc, (2, 0, 1, 3)).reshape(
        tok_count, groups * repeat, HEAD_DIM
    )
    d_query_low = rotate(d_query_heads, positions, -1.0).reshape(tok_count, -1).astype(jnp.bfloat16)
    d_key_low = (
        rotate(d_key_mine.reshape(tok_count, groups, HEAD_DIM), positions, -1.0)
        .reshape(tok_count, -1)
        .astype(jnp.bfloat16)
    )
    d_value_low = d_value_mine.astype(jnp.bfloat16)
    d_normed = tensor_total(
        product_right_t(d_query_low, back_query)
        + product_right_t(d_key_low, back_key)
        + product_right_t(d_value_low, back_value)
    )
    d_input_norm, grad_attn_in = norm_back(inputs, scale_in, d_normed)
    input_grad = d_middle + d_input_norm
    attn_cols = (
        lax.all_to_all(normed_low.T, ("dp", "context"), split_axis=0, concat_axis=1, tiled=True),
        lax.all_to_all(
            d_projected_low.T, ("dp", "context"), split_axis=0, concat_axis=1, tiled=True
        ),
    )
    piece_query = lax.all_gather(d_query_low, ("dp", "context"), axis=0, tiled=True)
    piece_key = lax.all_gather(d_key_low, ("dp", "context"), axis=0, tiled=True)
    piece_value = lax.all_gather(d_value_low, ("dp", "context"), axis=0, tiled=True)
    piece_mixed = lax.all_gather(mixed_low, ("dp", "context"), axis=0, tiled=True)
    normed_cols = attn_cols[0]
    projected_cols = attn_cols[1]
    grad_query = product(normed_cols, piece_query)
    grad_key = product(normed_cols, piece_key)
    grad_value = product(normed_cols, piece_value)
    grad_out = product(projected_cols, piece_mixed)
    gain_set = (
        lax.psum_scatter(grad_attn_in, ("dp", "context"), scatter_dimension=0, tiled=True),
        lax.psum_scatter(grad_attn_out, ("dp", "context"), scatter_dimension=0, tiled=True),
        lax.psum_scatter(grad_ffw_in, ("dp", "context"), scatter_dimension=0, tiled=True),
        lax.psum_scatter(grad_ffw_out, ("dp", "context"), scatter_dimension=0, tiled=True),
    )
    return (
        layer_output[None],
        input_grad[None],
        grad_query,
        grad_key,
        grad_value,
        grad_out,
        grad_gate,
        grad_up,
        grad_down,
        gain_set[0],
        gain_set[1],
        gain_set[2],
        gain_set[3],
    )


def solution(mesh):
    return jax.shard_map(
        body,
        mesh=mesh,
        in_specs=(
            P("dp", "context", None),
            P(("dp", "context"), "tensor"),
            P(("dp", "context"), "tensor"),
            P(("dp", "context"), "tensor"),
            P(("dp", "context"), "tensor"),
            P(("dp", "context"), "tensor"),
            P(("dp", "context"), "tensor"),
            P(("dp", "context"), "tensor"),
            P(("dp", "context")),
            P(("dp", "context")),
            P(("dp", "context")),
            P(("dp", "context")),
            P("dp", "context", None),
        ),
        out_specs=(
            P("dp", "context", None),
            P("dp", "context", None),
            P(("dp", "context"), "tensor"),
            P(("dp", "context"), "tensor"),
            P(("dp", "context"), "tensor"),
            P(("dp", "context"), "tensor"),
            P(("dp", "context"), "tensor"),
            P(("dp", "context"), "tensor"),
            P(("dp", "context"), "tensor"),
            P(("dp", "context")),
            P(("dp", "context")),
            P(("dp", "context")),
            P(("dp", "context")),
        ),
        check_vma=False,
    )
```

profile of v0, /device:TPU:1, one launch (start us, length us, event | category | flops | bytes accessed | tf_op | source)
XLA Modules:
  0.0 2381.1 jit_solution(2969082921740081285)
XLA Ops:
  14.8 64.6 %all-reduce.9 = (bf16[2304]{0:T(1024)(128)(2,1)S(1)}, bf16[2304]{0:T(1024)(128)(2,1)S(1)}, bf16[2304]{0:T(1024)(128)(2,1)S(1)}, bf16[2304]{0:T(1024)(128)(2,1)S(1)}) all-reduce(bf16[2304]{0:T(1024)(128)(2,1)S(1)} %dynamic-update-slice.2, ...), channel_id=1, replica_groups=mesh['dp'=2,'context'=8,'tensor'=2] {'dp','context'}, use_global_device_ids=true, to_apply=%add.2 | all-reduce | flops 9216 | bytes 36864
  86.5 52.8 %all-gather.23.cloned.1.call-done = bf16[2304,512]{1,0:T(8,128)(2,1)} async-done(((bf16[144,512]{1,0:T(8,128)(2,1)}), bf16[2304,512]{1,0:T(8,128)(2,1)}) %all-gather.23.cloned.1.call-update) | async-done | bytes 2359312 | tf_op jit(solution)/shard_map/all_gather | solution.py:84
  142.8 78.3 %all-gather.21.cloned.1.call-done = bf16[2304,1024]{1,0:T(8,128)(2,1)} async-done(((bf16[144,1024]{1,0:T(8,128)(2,1)}), bf16[2304,1024]{1,0:T(8,128)(2,1)}) %all-gather.21.cloned.1.call-update) | async-done | bytes 4718608 | tf_op jit(solution)/shard_map/all_gather | solution.py:82
  232.6 27.6 %all-gather.19.cloned.1.call-done = bf16[1024,512]{0,1:T(8,128)(2,1)} async-done(((bf16[128,512]{0,1:T(8,128)(2,1)}), bf16[1024,512]{0,1:T(8,128)(2,1)}) %all-gather.19.cloned.1.call-update) | async-done | bytes 1048592 | tf_op jit(solution)/shard_map/all_gather | solution.py:112
  260.3 43.1 %all-gather.25.cloned.1.call-done = bf16[1024,512]{1,0:T(8,128)(2,1)} async-done(((bf16[128,512]{1,0:T(8,128)(2,1)}), bf16[1024,512]{1,0:T(8,128)(2,1)}) %all-gather.25.cloned.1.call-update) | async-done | bytes 1048592 | tf_op jit(solution)/shard_map/all_gather | solution.py:113
  313.2 72.1 %all-gather.27.cloned.1.call-done = bf16[2304,1024]{1,0:T(8,128)(2,1)} async-done(((bf16[144,1024]{1,0:T(8,128)(2,1)}), bf16[2304,1024]{1,0:T(8,128)(2,1)}) %all-gather.27.cloned.1.call-update) | async-done | bytes 4718608 | tf_op jit(solution)/shard_map/all_gather | solution.py:85
  392.8 16.2 all-reduce.15.cloned.1.call-done
  412.9 233.7 %all-gather.29.cloned.1.call-done = bf16[2304,4608]{1,0:T(8,128)(2,1)} async-done(((bf16[144,4608]{1,0:T(8,128)(2,1)}), bf16[2304,4608]{1,0:T(8,128)(2,1)}) %all-gather.29.cloned.1.call-update) | async-done | bytes 21233680 | tf_op jit(solution)/shard_map/all_gather | solution.py:153
  657.9 223.9 %all-gather.31.cloned.1.call-done = bf16[2304,4608]{1,0:T(8,128)(2,1)} async-done(((bf16[144,4608]{1,0:T(8,128)(2,1)}), bf16[2304,4608]{1,0:T(8,128)(2,1)}) %all-gather.31.cloned.1.call-update) | async-done | bytes 21233680 | tf_op jit(solution)/shard_map/all_gather | solution.py:154
  894.6 222.4 %all-gather.33.cloned.1.call-done = bf16[2304,4608]{1,0:T(8,128)(2,1)} async-done(((bf16[144,4608]{1,0:T(8,128)(2,1)}), bf16[2304,4608]{1,0:T(8,128)(2,1)}) %all-gather.33.cloned.1.call-update) | async-done | bytes 21233680 | tf_op jit(solution)/shard_map/all_gather | solution.py:155
  1129.8 17.2 all-reduce.17.cloned.1.call-done
  1151.3 13.7 multiply_convert_fusion
  1189.6 19.9 all-reduce.19.cloned.1.call-done
  1221.2 18.3 conditional.3
  1248.8 55.8 %reduce-scatter.7.cloned.1.call-done = bf16[128,512]{1,0:T(8,128)(2,1)} async-done(((bf16[1024,512]{1,0:T(8,128)(2,1)}), bf16[128,512]{1,0:T(8,128)(2,1)}) %reduce-scatter.7.cloned.1.call-update) | async-done | bytes 131088
  1309.3 61.6 %reduce-scatter.9.cloned.1.call-done = bf16[128,512]{1,0:T(8,128)(2,1)} async-done(((bf16[1024,512]{1,0:T(8,128)(2,1)}), bf16[128,512]{1,0:T(8,128)(2,1)}) %reduce-scatter.9.cloned.1.call-update) | async-done | bytes 131088
  1408.3 14.2 all-to-all-done
  1428.8 74.3 %all-gather.41.cloned.1.call-done = bf16[2048,1024]{0,1:T(8,128)(2,1)} async-done(((bf16[128,1024]{0,1:T(8,128)(2,1)}), bf16[2048,1024]{0,1:T(8,128)(2,1)}) %all-gather.41.cloned.1.call-update) | async-done | bytes 4194320 | tf_op jit(solution)/shard_map/all_gather | solution.py:323
  1507.6 61.8 %all-reduce.8 = (f32[2304]{0:T(1024)S(1)}, f32[2304]{0:T(1024)S(1)}, f32[2304]{0:T(1024)S(1)}, f32[2304]{0:T(1024)S(1)}) all-reduce(f32[2304]{0:T(1024)S(1)} %copy-done.30, f32[2304]{0:T(1024)S(1)} %copy-done.29, f32[2304]{0:T(1024)S(1)} %copy-done.31, ...), channel_id=4, replica_groups=mesh['dp'=2,'context'=8,'tensor'=2] {'dp','context'}, use_global_device_ids=true, to_apply=%region_22.23.clone | all-reduce | flops 9216 | bytes 73728
  1575.1 57.7 %all-gather.37.cloned.1.call-done = bf16[2048,512]{0,1:T(8,128)(2,1)} async-done(((bf16[128,512]{0,1:T(8,128)(2,1)}), bf16[2048,512]{0,1:T(8,128)(2,1)}) %all-gather.37.cloned.1.call-update) | async-done | bytes 2097168 | tf_op jit(solution)/shard_map/all_gather | solution.py:321
  1640.2 85.0 %all-gather.35.cloned.1.call-done = bf16[2048,1024]{0,1:T(8,128)(2,1)} async-done(((bf16[128,1024]{0,1:T(8,128)(2,1)}), bf16[2048,1024]{0,1:T(8,128)(2,1)}) %all-gather.35.cloned.1.call-update) | async-done | bytes 4194320 | tf_op jit(solution)/shard_map/all_gather | solution.py:320
  1729.7 207.8 %all-gather.47.cloned.1.call-done = bf16[2048,4608]{1,0:T(8,128)(2,1)} async-done(((bf16[128,4608]{1,0:T(8,128)(2,1)}), bf16[2048,4608]{1,0:T(8,128)(2,1)}) %all-gather.47.cloned.1.call-update) | async-done | bytes 18874384 | tf_op jit(solution)/shard_map/all_gather | solution.py:198
  1948.3 202.3 %all-gather.45.cloned.1.call-done = bf16[2048,4608]{1,0:T(8,128)(2,1)} async-done(((bf16[128,4608]{1,0:T(8,128)(2,1)}), bf16[2048,4608]{1,0:T(8,128)(2,1)}) %all-gather.45.cloned.1.call-update) | async-done | bytes 18874384 | tf_op jit(solution)/shard_map/all_gather | solution.py:197
  2161.4 201.7 %all-gather.43.cloned.1.call-done = bf16[2048,4608]{1,0:T(8,128)(2,1)} async-done(((bf16[128,4608]{1,0:T(8,128)(2,1)}), bf16[2048,4608]{1,0:T(8,128)(2,1)}) %all-gather.43.cloned.1.call-update) | async-done | bytes 18874384 | tf_op jit(solution)/shard_map/all_gather | solution.py:196
  (251 shorter events, 264.8 us)
Async XLA Ops:
  7.2 74.6 %all-gather.17.cloned.1.call-start = ((), (), s32[]{:S(2)}) async-start(), calls=%async_computation.6 | async-start | bytes 2506752 | tf_op jit(solution)/shard_map/all_gather | solution.py:83
  7.9 131.4 %all-gather.23.cloned.1.call-start = ((), (), s32[]{:S(2)}) async-start(), calls=%async_computation.9 | async-start | bytes 2506752 | tf_op jit(solution)/shard_map/all_gather | solution.py:84
  8.7 212.5 %all-gather.21.cloned.1.call-start = ((), (), s32[]{:S(2)}) async-start(), calls=%async_computation.8 | async-start | bytes 5013504 | tf_op jit(solution)/shard_map/all_gather | solution.py:82
  9.4 250.9 %all-gather.19.cloned.1.call-start = ((), (), s32[]{:S(2)}) async-start(), calls=%async_computation.7 | async-start | bytes 1179648 | tf_op jit(solution)/shard_map/all_gather | solution.py:112
  86.5 216.8 %all-gather.25.cloned.1.call-start = ((), (), s32[]{:S(2)}) async-start(), calls=%async_computation.10 | async-start | bytes 1179648 | tf_op jit(solution)/shard_map/all_gather | solution.py:113
  142.2 243.1 %all-gather.27.cloned.1.call-start = ((), (), s32[]{:S(2)}) async-start(), calls=%async_computation.11 | async-start | bytes 5013504 | tf_op jit(solution)/shard_map/all_gather | solution.py:85
  142.8 266.3 %all-reduce.15.cloned.1.call-start = ((), (), s32[]{:S(2)}) async-start(), calls=%async_computation.12 | async-start | bytes 1179648 | tf_op jit(solution)/shard_map/psum | solution.py:43
  390.2 256.4 %all-gather.29.cloned.1.call-start = ((), (), s32[]{:S(2)}) async-start(), calls=%async_computation.13 | async-start | bytes 22560768 | tf_op jit(solution)/shard_map/all_gather | solution.py:153
  391.0 490.9 %all-gather.31.cloned.1.call-start = ((), (), s32[]{:S(2)}) async-start(), calls=%async_computation.14 | async-start | bytes 22560768 | tf_op jit(solution)/shard_map/all_gather | solution.py:154
  391.7 725.4 %all-gather.33.cloned.1.call-start = ((), (), s32[]{:S(2)}) async-start(), calls=%async_computation.15 | async-start | bytes 22560768 | tf_op jit(solution)/shard_map/all_gather | solution.py:155
  392.3 754.7 %all-reduce.17.cloned.1.call-start = ((), (), s32[]{:S(2)}) async-start(), calls=%async_computation.16 | async-start | bytes 1179648 | tf_op jit(solution)/shard_map/psum | solution.py:43
  1129.0 80.5 %all-reduce.19.cloned.1.call-start = ((), (), s32[]{:S(2)}) async-start(), calls=%async_computation.17 | async-start | bytes 1179648 | tf_op jit(solution)/shard_map/psum | solution.py:43
  1189.3 115.3 %reduce-scatter.7.cloned.1.call-start = ((), (), s32[]{:S(2)}) async-start(), calls=%async_computation.26 | async-start | bytes 1179648
  1241.7 129.2 %reduce-scatter.9.cloned.1.call-start = ((), (), s32[]{:S(2)}) async-start(), calls=%async_computation.27 | async-start | bytes 1179648
  1244.1 150.6 %all-reduce.21.cloned.1.call-start = ((), (), s32[]{:S(2)}) async-start(), calls=%async_computation.18 | async-start | bytes 1179648 | tf_op jit(solution)/shard_map/psum | solution.py:43
  1374.7 128.3 %all-gather.41.cloned.1.call-start = ((), (), s32[]{:S(2)}) async-start(), calls=%async_computation.22 | async-start | bytes 4456448 | tf_op jit(solution)/shard_map/all_gather | solution.py:323
  1375.3 196.6 %all-gather.39.cloned.1.call-start = ((), (), s32[]{:S(2)}) async-start(), calls=%async_computation.21 | async-start | bytes 2228224 | tf_op jit(solution)/shard_map/all_gather | solution.py:322
  1376.1 256.7 %all-gather.37.cloned.1.call-start = ((), (), s32[]{:S(2)}) async-start(), calls=%async_computation.20 | async-start | bytes 2228224 | tf_op jit(solution)/shard_map/all_gather | solution.py:321
  1376.7 348.5 %all-gather.35.cloned.1.call-start = ((), (), s32[]{:S(2)}) async-start(), calls=%async_computation.19 | async-start | bytes 4456448 | tf_op jit(solution)/shard_map/all_gather | solution.py:320
  1377.5 560.0 %all-gather.47.cloned.1.call-start = ((), (), s32[]{:S(2)}) async-start(), calls=%async_computation.25 | async-start | bytes 20054016 | tf_op jit(solution)/shard_map/all_gather | solution.py:198
  1378.1 772.5 %all-gather.45.cloned.1.call-start = ((), (), s32[]{:S(2)}) async-start(), calls=%async_computation.24 | async-start | bytes 20054016 | tf_op jit(solution)/shard_map/all_gather | solution.py:197
  1378.8 984.2 %all-gather.43.cloned.1.call-start = ((), (), s32[]{:S(2)}) async-start(), calls=%async_computation.23 | async-start | bytes 20054016 | tf_op jit(solution)/shard_map/all_gather | solution.py:196
  1422.5 213.5 %all-to-all-start.3 = ((bf16[16,144,128]{2,1,0:T(8,128)(2,1)}), bf16[16,144,128]{2,1,0:T(8,128)(2,1)S(1)}, u32[]{:S(2)}, u32[]{:S(2)}) async-start(bf16[16,144,128]{2,1,0:T(8,128)(2,1)} %bitcast.52), calls=%async_computation.3 | async-start | bytes 1179648 | tf_op jit(solution)/shard_map/all_to_all | solution.py:194
  1636.0 312.3 %all-to-all-start.2 = ((bf16[16,144,128]{2,1,0:T(8,128)(2,1)}), bf16[16,144,128]{2,1,0:T(8,128)(2,1)S(1)}, u32[]{:S(2)}, u32[]{:S(2)}) async-start(bf16[16,144,128]{2,1,0:T(8,128)(2,1)} %bitcast.49), calls=%async_computation.2 | async-start | bytes 1179648 | tf_op jit(solution)/shard_map/all_to_all | solution.py:191
  (47 other events, 2162.6 us)
Sparse Core Ops, SparseCore 0:
  10.8 64.1 all-gather.16
  77.7 61.5 all-gather.22
  142.1 79.0 all-gather.20
  223.7 36.5 all-gather.18
  262.8 40.4 all-gather.24
  305.9 79.3 all-gather.26
  390.3 18.6 all-reduce.14
  412.2 234.3 all-gather.28
  649.7 232.1 all-gather.30
  884.9 232.1 all-gather.32
  1129.1 17.8 all-reduce.16
  1189.4 20.0 all-reduce.18
  1241.8 62.6 reduce-scatter.6
  1308.4 62.4 reduce-scatter.8
  1374.8 19.7 all-reduce.20
  1397.8 105.2 all-gather.40
  1506.2 63.8 all-gather.38
  1572.6 60.1 all-gather.36
  1635.5 89.6 all-gather.34
  1727.8 209.6 all-gather.46
  1940.9 209.6 all-gather.44
  2153.3 209.6 all-gather.42
where the time goes:
time: 2390 us; the launch traced here: 2380 us
  waiting for transfers between devices  1990 us (83%)
  matrix products  164 us (7%)
  blocking collectives  126 us (5%)
  local copies, waits for them, and re-layouts  36.8 us (2%)
  other arithmetic  29.7 us (1%)
    all_gather x1, waiting for transfers between devices, body(): lax.all_gather(w_gate, ('dp', 'context'), axis=0, tiled=True)  234 us
    all_gather x1, waiting for transfers between devices, body(): lax.all_gather(w_up, ('dp', 'context'), axis=0, tiled=True)  224 us
    all_gather x1, waiting for transfers between devices, body(): lax.all_gather(w_down, ('dp', 'context'), axis=0, tiled=True)  222 us
    all_gather x1, waiting for transfers between devices, body(): lax.all_gather(hidden_low, ('dp', 'context'), axis=0, tiled=True)  208 us
    all_gather x1, waiting for transfers between devices, body(): piece_up = lax.all_gather(d_up_low, ('dp', 'context'), axis=0, tiled=True)  202 us
    all_gather x1, waiting for transfers between devices, body(): lax.all_gather(d_gate_low, ('dp', 'context'), axis=0, tiled=True)  202 us
    unnamed x2, blocking collectives  126 us
    unnamed x24, waiting for transfers between devices  126 us
  transfers between devices with their start and end apart: 26, of which 21 were waited for; matrix products, arithmetic and copies ran while one was open for 5% of the time, Pallas kernels for 0%

commit v1 on v0

v1 whole, which is shorter than its diff:
```python
import jax
import jax.numpy as jnp
from jax import lax
from jax.sharding import PartitionSpec as P

HEAD_DIM = 256
LANES = 128

epsilon = 1e-06
softcap = 50.0
theta = 10000.0
floor_value = -1e30
low = jnp.bfloat16
wide = jnp.float32
chip_axes = ("dp", "context")


def product(left_side, right_side):
    return jnp.dot(left_side, right_side, preferred_element_type=wide)


def product_right_t(left_side, right_side):
    return lax.dot_general(left_side, right_side, (((1,), (1,)), ((), ())), preferred_element_type=wide)


def product_left_t(left_side, right_side):
    return lax.dot_general(left_side, right_side, (((0,), (0,)), ((), ())), preferred_element_type=wide)


def inverse_size(values):
    return lax.rsqrt(jnp.mean(values * values, axis=-1, keepdims=True) + epsilon)


def norm_back(unit, inverse, scaling, upstream):
    inner = upstream * scaling
    return inverse * (inner - unit * jnp.mean(inner * unit, axis=-1, keepdims=True))


def turn(values, cosine, sine_part):
    half_width = values.shape[-1] // 2
    former = values[..., :half_width]
    latter = values[..., half_width:]
    return jnp.concatenate(
        [former * cosine - latter * sine_part, latter * cosine + former * sine_part], axis=-1
    )


def geglu(gate_in, upward):
    return jax.nn.gelu(gate_in, approximate=True) * upward


class Slice:
    def __init__(self):
        self.dp = lax.axis_size("dp")
        self.context = lax.axis_size("context")
        self.ranks = self.context // 2
        self.chips = self.dp * self.context
        self.core = lax.axis_index("tensor")
        self.place = lax.axis_index("context")
        self.rank = self.place // 2
        self.side = self.place % 2
        self.me = lax.axis_index(chip_axes)

    def send(self, block, where):
        pairs = []
        for dp in range(self.dp):
            for rank in range(self.ranks):
                for side in range(2):
                    pairs.append(
                        (self.index(dp, rank, side), self.index(*where(dp, rank, side)))
                    )
        return lax.ppermute(block, chip_axes, pairs)

    def index(self, dp, rank, side):
        return (dp * self.ranks + rank % self.ranks) * 2 + side

    def across(self, block):
        return self.send(block, lambda dp, rank, side: (dp, rank, 1 - side))

    def over(self, block):
        return self.send(block, lambda dp, rank, side: (1 - dp, rank, side))

    def along(self, block, step):
        if step % self.ranks == 0:
            return block
        return self.send(block, lambda dp, rank, side: (dp, rank + step, side))

    def swap(self, block):
        return lax.ppermute(block, "tensor", [(0, 1), (1, 0)])

    def ordered(self, mine, other):
        first = self.core == 0
        return jnp.where(first, mine, other), jnp.where(first, other, mine)

    def exchange(self, pick):
        pieces = [pick(self.me)]
        for turn_by in range(1, self.chips):
            pairs = [(chip, chip ^ turn_by) for chip in range(self.chips)]
            pieces.append(lax.ppermute(pick(self.me ^ turn_by), chip_axes, pairs))
        result = jnp.zeros((self.chips,) + pieces[0].shape, pieces[0].dtype)
        for turn_by, piece in enumerate(pieces):
            result = lax.dynamic_update_index_in_dim(result, piece, self.me ^ turn_by, 0)
        return result

    def gather_plane(self, block, groups):
        moved = {step: self.along(block, step) for step in range(self.ranks)}
        gathered = []
        for group in groups:
            here = jnp.stack([moved[step] for step in group])
            gathered.append(jnp.stack([here, self.across(here)]))
        return gathered

    def gather_all(self, block, groups):
        moved = {step: self.along(block, step) for step in range(self.ranks)}
        cut = block.shape[0] // 2
        gathered = []
        for group in groups:
            here = jnp.stack([moved[step] for step in group])
            beside = self.across(here)
            above = self.over(here)
            corner = jnp.concatenate(
                [self.over(beside[:, :cut]), self.across(above[:, cut:])], axis=1
            )
            gathered.append(jnp.stack([here, beside, above, corner]))
        return gathered

    def scatter_plane(self, parts, groups):
        total = 0.0
        for part, group in zip(parts, groups, strict=True):
            here = part[0].astype(wide)
            if part.shape[0] == 2:
                here = here + self.across(part[1]).astype(wide)
            total = total + self.settle(here, group)
        return total

    def settle(self, here, group):
        total = 0.0
        for at, step in enumerate(group):
            piece = here[at]
            if step:
                piece = self.along(piece.astype(low), -step).astype(wide)
            total = total + piece
        return total

    def scatter_all(self, parts, groups):
        total = 0.0
        for part, group in zip(parts, groups, strict=True):
            cut = part.shape[2] // 2
            upper = part[:, :, :cut]
            lower = part[:, :, cut:]
            upper_two = upper[:2].astype(wide) + self.over(upper[2:]).astype(wide)
            lower_two = lower[0::2].astype(wide) + self.across(lower[1::2]).astype(wide)
            upper_one = upper_two[0] + self.across(upper_two[1].astype(low)).astype(wide)
            lower_one = lower_two[0] + self.over(lower_two[1].astype(low)).astype(wide)
            here = jnp.concatenate([upper_one, lower_one], axis=1)
            total = total + self.settle(here, group)
        return total


def body(
    tokens,
    w_query,
    w_key,
    w_value,
    w_out,
    w_gate,
    w_up,
    w_down,
    gain_attn_in,
    gain_attn_out,
    gain_ffw_in,
    gain_ffw_out,
    cotangent,
):
    net = Slice()
    core, chips = net.core, net.chips
    span = tokens.shape[1]
    width = tokens.shape[2]
    half = span // 2
    rows = w_query.shape[0]
    cut_rows = rows // 2
    heads = 2 * w_query.shape[1] // HEAD_DIM
    kv_heads = 2 * w_key.shape[1] // HEAD_DIM
    repeat = heads // kv_heads
    share = net.context // heads
    score_scale = HEAD_DIM ** (-0.5)
    plane_groups = (tuple(range(net.ranks)),)
    all_groups = (tuple(range(net.ranks)),)

    def own_half(array):
        return lax.dynamic_slice_in_dim(array, core * half, half, 0)

    own_tokens = own_half(tokens[0])
    upstream = own_half(cotangent[0])

    gains = jnp.stack([gain_attn_in, gain_attn_out, gain_ffw_in, gain_ffw_out])
    gains = lax.all_to_all(
        jnp.broadcast_to(gains[None], (chips,) + gains.shape), chip_axes, 0, 0, tiled=True
    )
    gains = jnp.transpose(gains, (1, 0, 2)).reshape(4, width).astype(wide)
    scale_in, scale_mid, scale_pre, scale_out = gains[0], gains[1], gains[2], gains[3]

    packed = jnp.concatenate([w_query, w_key, w_value, w_out], axis=1)
    mine = lax.dynamic_slice_in_dim(packed, core * cut_rows, cut_rows, 0)
    theirs = lax.dynamic_slice_in_dim(packed, (1 - core) * cut_rows, cut_rows, 0)
    first, second = net.ordered(mine, net.swap(theirs))
    edges = (0, w_query.shape[1])
    edges = edges + (edges[1] + w_key.shape[1], edges[1] + 2 * w_key.shape[1])
    edges = edges + (packed.shape[1],)

    def by_head(at):
        both = jnp.concatenate(
            [first[:, edges[at] : edges[at + 1]], second[:, edges[at] : edges[at + 1]]], axis=1
        )
        return jnp.transpose(both.reshape(cut_rows, -1, HEAD_DIM), (1, 0, 2))

    head_sets = jnp.concatenate(
        [
            by_head(0),
            jnp.repeat(by_head(1), repeat, axis=0),
            jnp.repeat(by_head(2), repeat, axis=0),
            by_head(3),
        ],
        axis=2,
    )

    def head_set_of(chip):
        return lax.dynamic_index_in_dim(
            head_sets, (chip % net.context) // share, 0, keepdims=False
        )

    part = net.exchange(head_set_of)
    attn_first, attn_second = net.ordered(part, net.swap(part))
    attn_weights = jnp.stack([attn_first, attn_second], axis=1).reshape(width, 4 * HEAD_DIM)
    w_qkv = attn_weights[:, : 3 * HEAD_DIM]
    w_out_head = attn_weights[:, 3 * HEAD_DIM :]

    units = w_gate.shape[1] // chips
    main = units // LANES * LANES
    rest = units - main
    rest_lanes = -(-3 * rest // LANES) * LANES

    def unit_sets(arrays):
        main_parts = [
            jnp.transpose(a[:, : chips * main].reshape(rows, chips, main), (1, 0, 2)) for a in arrays
        ]
        rest_parts = [
            jnp.transpose(a[:, chips * main :].reshape(rows, chips, rest), (1, 0, 2)) for a in arrays
        ]
        blank = jnp.zeros((chips, rows, rest_lanes - 3 * rest), low)
        return jnp.concatenate(main_parts + rest_parts + [blank], axis=2)

    sets = unit_sets([w_gate, w_up, w_down])
    mine = net.exchange(
        lambda chip: lax.dynamic_index_in_dim(sets, chip, 0, keepdims=False)
    ).reshape(width, -1)
    other = net.swap(mine)

    def units_of(at):
        start = 3 * main + at * rest
        return jnp.concatenate(
            [
                mine[:, at * main : (at + 1) * main],
                other[:, at * main : (at + 1) * main],
                mine[:, start : start + rest],
                other[:, start : start + rest],
            ],
            axis=1,
        )

    gate_units, up_units, down_units = units_of(0), units_of(1), units_of(2)

    if share == 1:
        asked = None
    else:
        asked = tuple(range(0, net.ranks, share // 2))
    own_inputs = own_tokens.astype(wide)
    inputs = jnp.concatenate(
        [g.reshape(-1, width) for g in net.gather_plane(own_tokens, plane_groups)]
    ).astype(wide)
    units_in = inputs * inverse_size(inputs)
    normed_low = (units_in * scale_in).astype(low)
    block_places = jnp.concatenate(
        [
            jnp.stack(
                [
                    jnp.stack([(net.rank - step) % net.ranks * 2 + side for step in group])
                    for side in (net.side, 1 - net.side)
                ]
            ).reshape(-1)
            for group in plane_groups
        ]
    )
    offsets = jnp.arange(half, dtype=jnp.int32)
    places = (block_places[:, None] * span + core * half + offsets[None, :]).reshape(-1)
    other_places = places + (1 - 2 * core) * half
    exponent = jnp.arange(HEAD_DIM // 2, dtype=wide) * (-2.0 / HEAD_DIM)
    angles = places.astype(wide)[:, None] * (theta**exponent)[None, :]
    cosine, sine_part = jnp.cos(angles), jnp.sin(angles)

    def asked_rows(array):
        if asked is None:
            return array
        blocks = array.reshape((2, net.ranks, half) + array.shape[1:])
        return jnp.concatenate([blocks[0, step] for step in asked])

    qkv = product(normed_low, w_qkv)
    queries = asked_rows(turn(qkv[:, :HEAD_DIM], cosine, sine_part).astype(low))
    keys = turn(qkv[:, HEAD_DIM : 2 * HEAD_DIM], cosine, sine_part).astype(low)
    values = qkv[:, 2 * HEAD_DIM :].astype(low)
    own_kv = jnp.concatenate([keys, values], axis=1)
    all_kv = jnp.concatenate([own_kv, net.swap(own_kv)])
    all_keys, all_values = all_kv[:, :HEAD_DIM], all_kv[:, HEAD_DIM:]
    key_places = jnp.concatenate([places, other_places])
    allowed = key_places[None, :] <= asked_rows(places)[:, None]
    scores = product_right_t(queries, all_keys) * score_scale
    bent = jnp.tanh(scores / softcap)
    capped = jnp.where(allowed, softcap * bent, floor_value)
    shifted = jnp.exp(capped - jnp.max(capped, axis=-1, keepdims=True))
    probabilities = shifted / jnp.sum(shifted, axis=-1, keepdims=True)
    probabilities_low = probabilities.astype(low)
    mixed_low = product(probabilities_low, all_values).astype(low)

    def plane_parts(array):
        array = array.astype(low)
        if asked is not None:
            return [array.reshape(1, len(asked), half, width)], (asked,)
        parts, start = [], 0
        for group in plane_groups:
            size = 2 * len(group) * half
            parts.append(array[start : start + size].reshape(2, len(group), half, width))
            start += size
        return parts, plane_groups

    projected = net.scatter_plane(*plane_parts(product_right_t(mixed_low, w_out_head)))

    inverse_mid = inverse_size(projected)
    unit_mid = projected * inverse_mid
    middle = own_inputs + unit_mid * scale_mid
    inverse_pre = inverse_size(middle)
    unit_pre = middle * inverse_pre
    normed_two_low = (unit_pre * scale_pre).astype(low)

    all_two = [g.reshape(-1, width) for g in net.gather_all(normed_two_low, all_groups)]
    gates = [product(rows_two, gate_units) for rows_two in all_two]
    ups = [product(rows_two, up_units) for rows_two in all_two]
    hiddens = [geglu(g, u).astype(low) for g, u in zip(gates, ups, strict=True)]

    def all_part(array, group):
        return array.astype(low).reshape(4, len(group), half, width)

    branch = net.scatter_all(
        [
            all_part(product_right_t(h, down_units), group)
            for h, group in zip(hiddens, all_groups, strict=True)
        ],
        all_groups,
    )
    inverse_out = inverse_size(branch)
    unit_out = branch * inverse_out
    own_output = (middle + unit_out * scale_out).astype(low)

    grad_ffw_out = jnp.sum(upstream * unit_out, axis=0)
    d_branch_low = norm_back(unit_out, inverse_out, scale_out, upstream).astype(low)
    all_branch = [g.reshape(-1, width) for g in net.gather_all(d_branch_low, all_groups)]
    d_gates, d_ups, d_twos = [], [], []
    for d_rows, gate_in, upward, group in zip(all_branch, gates, ups, all_groups, strict=True):
        d_hidden = product(d_rows, down_units)
        _, pull = jax.vjp(geglu, gate_in, upward)
        d_gate, d_up = pull(d_hidden)
        d_gates.append(d_gate.astype(low))
        d_ups.append(d_up.astype(low))
        d_twos.append(
            all_part(
                product_right_t(d_gates[-1], gate_units) + product_right_t(d_ups[-1], up_units),
                group,
            )
        )
    d_normed_two = net.scatter_all(d_twos, all_groups)
    grad_ffw_in = jnp.sum(d_normed_two * unit_pre, axis=0)
    d_middle = upstream + norm_back(unit_pre, inverse_pre, scale_pre, d_normed_two)
    grad_attn_out = jnp.sum(d_middle * unit_mid, axis=0)
    d_projected_low = norm_back(unit_mid, inverse_mid, scale_mid, d_middle).astype(low)

    all_two = jnp.concatenate(all_two)
    all_branch = jnp.concatenate(all_branch)
    unit_grads = [
        product_left_t(all_two, jnp.concatenate(d_gates)),
        product_left_t(all_two, jnp.concatenate(d_ups)),
        product_left_t(all_branch, jnp.concatenate(hiddens)),
    ]

    def side_of(at_other):
        mains = [g[:, at_other * main : (at_other + 1) * main] for g in unit_grads]
        starts = 2 * main + at_other * rest
        rests = [g[:, starts : starts + rest] for g in unit_grads]
        blank = jnp.zeros((width, rest_lanes - 3 * rest), wide)
        return jnp.concatenate(mains + rests + [blank], axis=1)

    grad_set = (side_of(0) + net.swap(side_of(1).astype(low)).astype(wide)).astype(low)
    grad_set = grad_set.reshape(chips, rows, -1)
    got = net.exchange(lambda chip: lax.dynamic_index_in_dim(grad_set, chip, 0, keepdims=False))

    def unit_grad(at):
        start = 3 * main + at * rest
        main_part = jnp.transpose(got[:, :, at * main : (at + 1) * main], (1, 0, 2))
        rest_part = jnp.transpose(got[:, :, start : start + rest], (1, 0, 2))
        return jnp.concatenate(
            [main_part.reshape(rows, chips * main), rest_part.reshape(rows, chips * rest)], axis=1
        ).astype(wide)

    grad_gate, grad_up, grad_down = unit_grad(0), unit_grad(1), unit_grad(2)

    d_projected_all = jnp.concatenate(
        [g.reshape(-1, width) for g in net.gather_plane(d_projected_low, plane_groups)]
    )
    d_projected_asked = asked_rows(d_projected_all)
    d_mixed_low = product(d_projected_asked, w_out_head).astype(low)
    d_prob = product_right_t(d_mixed_low, all_values)
    delta = jnp.sum(probabilities * d_prob, axis=-1, keepdims=True)
    d_capped = probabilities * (d_prob - delta)
    d_scores = (d_capped * (1.0 - bent * bent)).astype(low)
    d_queries = product(d_scores, all_keys) * score_scale
    d_keys = product_left_t(d_scores, queries) * score_scale
    d_values = product_left_t(probabilities_low, d_mixed_low)
    d_kv = jnp.concatenate([d_keys, d_values], axis=1)
    count = places.shape[0]
    d_kv = d_kv[:count] + net.swap(d_kv[count:].astype(low)).astype(wide)
    d_query_low = turn(d_queries, asked_rows(cosine), -asked_rows(sine_part)).astype(low)
    d_key_low = turn(d_kv[:, :HEAD_DIM], cosine, -sine_part).astype(low)
    d_kv_low = jnp.concatenate([d_key_low, d_kv[:, HEAD_DIM:].astype(low)], axis=1)
    if asked is None:
        d_qkv_low = jnp.concatenate([d_query_low, d_kv_low], axis=1)
    else:
        blocks = jnp.zeros((2, net.ranks, half, HEAD_DIM), low)
        d_query_low = blocks.at[0, jnp.array(asked)].set(
            d_query_low.reshape(len(asked), half, HEAD_DIM)
        )
        d_qkv_low = jnp.concatenate([d_query_low.reshape(-1, HEAD_DIM), d_kv_low], axis=1)
    d_normed_part = product_right_t(d_qkv_low, w_qkv)
    grad_attn_in = jnp.sum(d_normed_part * units_in, axis=0)
    every = d_normed_part.astype(low)
    parts, start = [], 0
    for group in plane_groups:
        size = 2 * len(group) * half
        parts.append(every[start : start + size].reshape(2, len(group), half, width))
        start += size
    d_normed = net.scatter_plane(parts, plane_groups)
    own_inverse = inverse_size(own_inputs)
    own_grad = d_middle + norm_back(own_inputs * own_inverse, own_inverse, scale_in, d_normed)

    head_grads = jnp.concatenate(
        [
            product_left_t(normed_low, d_qkv_low),
            product_left_t(d_projected_asked, mixed_low),
        ],
        axis=1,
    ).reshape(chips, 2, cut_rows, 4 * HEAD_DIM)
    kept = lax.dynamic_index_in_dim(head_grads, core, 1, keepdims=False)
    given = lax.dynamic_index_in_dim(head_grads, 1 - core, 1, keepdims=False)
    head_grads = (kept + net.swap(given.astype(low)).astype(wide)).astype(low)
    got = net.exchange(lambda chip: lax.dynamic_index_in_dim(head_grads, chip, 0, keepdims=False))
    got = got.astype(wide).reshape(net.dp, net.context, cut_rows, 4 * HEAD_DIM)

    def heads_total(at, count_of):
        piece = got[..., at * HEAD_DIM : (at + 1) * HEAD_DIM]
        piece = piece.reshape(net.dp, count_of, -1, cut_rows, HEAD_DIM).sum(axis=(0, 2))
        return jnp.transpose(piece, (1, 0, 2)).reshape(cut_rows, 2, -1)

    whole = jnp.concatenate(
        [
            heads_total(0, heads),
            heads_total(1, kv_heads),
            heads_total(2, kv_heads),
            heads_total(3, heads),
        ],
        axis=2,
    )
    kept = lax.dynamic_index_in_dim(whole, core, 1, keepdims=False)
    given = lax.dynamic_index_in_dim(whole, 1 - core, 1, keepdims=False)
    upper, lower = net.ordered(kept, net.swap(given.astype(low)).astype(wide))
    whole = jnp.concatenate([upper, lower])
    grad_query = whole[:, edges[0] : edges[1]]
    grad_key = whole[:, edges[1] : edges[2]]
    grad_value = whole[:, edges[2] : edges[3]]
    grad_out = whole[:, edges[3] : edges[4]]

    gain_grads = jnp.stack([grad_attn_in, grad_attn_out, grad_ffw_in, grad_ffw_out])
    gain_grads = gain_grads + net.swap(gain_grads)
    gain_grads = jnp.transpose(gain_grads.reshape(4, chips, rows), (1, 0, 2))
    gain_grads = lax.all_to_all(gain_grads, chip_axes, 0, 0, tiled=True).sum(axis=0)

    layer_output = jnp.concatenate(net.ordered(own_output, net.swap(own_output)))
    input_grad = jnp.concatenate(net.ordered(own_grad, net.swap(own_grad)))
    return (
        layer_output[None],
        input_grad[None],
        grad_query,
        grad_key,
        grad_value,
        grad_out,
        grad_gate,
        grad_up,
        grad_down,
        gain_grads[0],
        gain_grads[1],
        gain_grads[2],
        gain_grads[3],
    )


def solution(mesh):
    tokens_spec = P("dp", "context", None)
    weight_spec = P(("dp", "context"), "tensor")
    gain_spec = P(("dp", "context"))
    return jax.shard_map(
        body,
        mesh=mesh,
        in_specs=(tokens_spec,) + (weight_spec,) * 7 + (gain_spec,) * 4 + (tokens_spec,),
        out_specs=(tokens_spec,) * 2 + (weight_spec,) * 7 + (gain_spec,) * 4,
        check_vma=False,
    )
```

time: 2390 us -> 1050 us (0.44)
  waiting for transfers between devices: 1990 us -> 463 us
  starting transfers between devices: 21.6 us -> 256 us
  local copies, waits for them, and re-layouts: 36.8 us -> 177 us
  blocking collectives: 126 us -> 0 us
  matrix products: 164 us -> 63.7 us
  other arithmetic: 29.7 us -> 70 us
    all_gather x16 -> x0, waiting for transfers between devices: 1780 us -> none  [the longest x1 234 us: body(): lax.all_gather(w_gate, ('dp', 'context'), axis=0, tiled=True)]
    ppermute x0 -> x115, waiting for transfers between devices: none -> 463 us  [the longest x44 320 us: send(): return lax.ppermute(block, chip_axes, pairs)]
    ppermute x0 -> x115, starting transfers between devices: none -> 242 us  [the longest x60 123 us: exchange(): pieces.append(lax.ppermute(pick(self.me ^ turn_by), chip_axes, pairs))]
    unnamed x2 -> x0, blocking collectives: 126 us -> none
    unnamed x24 -> x0, waiting for transfers between devices: 126 us -> none
    dot_general x20 -> x14, matrix products: 110 us -> 37.7 us  [the longest x7 19.1 us: product(): return jnp.dot(left_side, right_side, preferred_element_type=wide)]
    psum x4 -> x0, waiting for transfers between devices: 62.8 us -> none  [tensor_total(): lax.psum(partial_value.astype(jnp.bfloat16), 'tensor').astype(jnp.float32)]
    dynamic_update_slice x0 -> x62, local copies, waits for them, and re-layouts: none -> 30.6 us  [exchange(): lax.dynamic_update_index_in_dim(result, piece, self.me ^ turn_by, 0)]
  transfers between devices with their start and end apart: 26 -> 117, of which waited for: 21 -> 53; matrix products, arithmetic and copies ran while one was open for 5% -> 23% of each run, Pallas kernels for 0% -> 0%
where the time goes in v1:
time: 1050 us; the launch traced here: 1030 us
  waiting for transfers between devices  463 us (44%)
  starting transfers between devices  256 us (24%)
  local copies, waits for them, and re-layouts  177 us (17%)
  other arithmetic  70 us (7%)
  matrix products  63.7 us (6%)
    ppermute x44, waiting for transfers between devices, send(): return lax.ppermute(block, chip_axes, pairs)  320 us
    ppermute x60, waiting for transfers between devices, exchange(): pieces.append(lax.ppermute(pick(self.me ^ turn_by), chip_axes, pairs))  142 us
    ppermute x60, starting transfers between devices, exchange(): pieces.append(lax.ppermute(pick(self.me ^ turn_by), chip_axes, pairs))  123 us
    ppermute x44, starting transfers between devices, send(): return lax.ppermute(block, chip_axes, pairs)  74.8 us
    ppermute x11, starting transfers between devices, swap(): return lax.ppermute(block, 'tensor', [(0, 1), (1, 0)])  43.8 us
    unnamed x298, local copies, waits for them, and re-layouts  40.8 us
    dynamic_update_slice x62, local copies, waits for them, and re-layouts, exchange(): lax.dynamic_update_index_in_dim(result, piece, self.me ^ turn_by, 0)  30.6 us
    dot_general x7, matrix products, product_right_t(): lax.dot_general(left_side, right_side, (((1,), (1,)), ((), ())), preferre...  26 us
  transfers between devices with their start and end apart: 117, of which 53 were waited for; matrix products, arithmetic and copies ran while one was open for 23% of the time, Pallas kernels for 0%

profile of v1, /device:TPU:1, one launch (start us, length us, event | category | flops | bytes accessed | tf_op | source)
XLA Modules:
  0.0 1033.8 jit_solution(4789253166399488923)
XLA Ops:
  24.1 18.3 %constant_dynamic-slice_fusion.1 = (bf16[1,144,896]{2,0,1:T(2,128)(2,1)S(1)}, bf16[1,144,896]{2,0,1:T(2,128)(2,1)S(1)}, bf16[1,144,896]{2,0,1:T(2,128)(2,1)S(1)}...) fusion(bf16[16,144,896]{2,0,1:T(8,128)(2,1)} %concatenate.111, ...), kind=kLoop, calls=%fused_computation.400 | loop fusion | bytes 8257600 | tf_op jit(solution)/shard_map/jit(dynamic_index_in_dim)/dynamic_slice | solution.py:255
  194.9 25.1 %collective-permute-start.20 = (bf16[16,72,1024]{2,1,0:T(8,128)(2,1)S(1)}, bf16[16,72,1024]{2,1,0:T(8,128)(2,1)}, u32[]{:S(2)}, u32[]{:S(2)}) collective-permute-start(bf16[16,72,1024]{2,1,0:T(8,128)(2,1)S(1)} %bitcast_dynamic-update-slice_fusion.45), channel_id=1, source_target_pairs={{0,1},{1,0},{2,3},{3,2},{4,5},{5,4},{6,7},{7,6},{8,9},{9,8},{10,11... | collective-permute-start | bytes 7077896 | tf_op jit(solution)/shard_map/ppermute | solution.py:89
  238.2 19.0 %collective-permute-done.3 = bf16[4,64,2304]{2,1,0:T(8,128)(2,1)S(1)} collective-permute-done((bf16[4,64,2304]{2,1,0:T(8,128)(2,1)S(1)}, bf16[4,64,2304]{2,1,0:T(8,128)(2,1)S(1)}, u32[]{:S(2)}, u32[]{:S(2)}) %collective-permute-start.3) | collective-permute-done | bytes 1179680 | tf_op jit(solution)/shard_map/ppermute | solution.py:72
  304.1 21.5 %collective-permute-done.22 = bf16[4,64,2304]{2,1,0:T(8,128)(2,1)S(1)} collective-permute-done((bf16[4,64,2304]{2,1,0:T(8,128)(2,1)S(1)}, bf16[4,64,2304]{2,1,0:T(8,128)(2,1)S(1)}, u32[]{:S(2)}, u32[]{:S(2)}) %collective-permute-start.22) | collective-permute-done | bytes 1179680 | tf_op jit(solution)/shard_map/ppermute | solution.py:72
  338.0 11.6 %collective-permute-done.24 = bf16[64,2304]{1,0:T(8,128)(2,1)S(1)} collective-permute-done((bf16[64,2304]{1,0:T(8,128)(2,1)S(1)}, bf16[64,2304]{1,0:T(8,128)(2,1)S(1)}, u32[]{:S(2)}, u32[]{:S(2)}) %collective-permute-start.24) | collective-permute-done | bytes 294944 | tf_op jit(solution)/shard_map/ppermute | solution.py:72
  359.3 14.5 %collective-permute-done.27 = bf16[64,2304]{1,0:T(8,128)(2,1)S(1)} collective-permute-done((bf16[64,2304]{1,0:T(8,128)(2,1)S(1)}, bf16[64,2304]{1,0:T(8,128)(2,1)S(1)}, u32[]{:S(2)}, u32[]{:S(2)}) %collective-permute-start.27) | collective-permute-done | bytes 294944 | tf_op jit(solution)/shard_map/ppermute | solution.py:72
  378.5 22.5 %collective-permute-done.29 = bf16[4,64,2304]{2,1,0:T(8,128)(2,1)S(1)} collective-permute-done((bf16[4,64,2304]{2,1,0:T(8,128)(2,1)S(1)}, bf16[4,64,2304]{2,1,0:T(8,128)(2,1)S(1)}, u32[]{:S(2)}, u32[]{:S(2)}) %collective-permute-start.29) | collective-permute-done | bytes 1179680 | tf_op jit(solution)/shard_map/ppermute | solution.py:72
  403.6 10.9 %collective-permute-done.31 = bf16[4,32,2304]{2,1,0:T(8,128)(2,1)S(1)} collective-permute-done((bf16[4,32,2304]{2,1,0:T(8,128)(2,1)S(1)}, bf16[4,32,2304]{2,1,0:T(8,128)(2,1)S(1)}, u32[]{:S(2)}, u32[]{:S(2)}) %collective-permute-start.31) | collective-permute-done | bytes 589856 | tf_op jit(solution)/shard_map/ppermute | solution.py:72
  431.1 23.3 %collective-permute-done.49 = bf16[2,4,32,2304]{3,2,1,0:T(8,128)(2,1)S(1)} collective-permute-done((bf16[2,4,32,2304]{3,2,1,0:T(8,128)(2,1)S(1)}, bf16[2,4,32,2304]{3,2,1,0:T(8,128)(2,1)S(1)}, u32[]{:S(2)}, u32[]{:S(2)}) %collective-permute-start.49) | collective-permute-done | bytes 1179680 | tf_op jit(solution)/shard_map/ppermute | solution.py:72
  456.6 11.4 %collective-permute-done.50 = bf16[4,32,2304]{2,1,0:T(8,128)(2,1)S(1)} collective-permute-done((bf16[4,32,2304]{2,1,0:T(8,128)(2,1)S(1)}, bf16[4,32,2304]{2,1,0:T(8,128)(2,1)S(1)}, u32[]{:S(2)}, u32[]{:S(2)}) %collective-permute-start.50) | collective-permute-done | bytes 589856 | tf_op jit(solution)/shard_map/ppermute | solution.py:72
  483.3 18.7 %collective-permute-done.54 = bf16[64,2304]{1,0:T(8,128)(2,1)} collective-permute-done((bf16[64,2304]{1,0:T(8,128)(2,1)}, bf16[64,2304]{1,0:T(8,128)(2,1)}, u32[]{:S(2)}, u32[]{:S(2)}) %collective-permute-start.54) | collective-permute-done | bytes 294944 | tf_op jit(solution)/shard_map/ppermute | solution.py:72
  513.0 15.8 %collective-permute-done.58 = bf16[64,2304]{1,0:T(8,128)(2,1)S(1)} collective-permute-done((bf16[64,2304]{1,0:T(8,128)(2,1)S(1)}, bf16[64,2304]{1,0:T(8,128)(2,1)S(1)}, u32[]{:S(2)}, u32[]{:S(2)}) %collective-permute-start.58) | collective-permute-done | bytes 294944 | tf_op jit(solution)/shard_map/ppermute | solution.py:72
  534.5 23.1 %collective-permute-done.60 = bf16[4,64,2304]{2,1,0:T(8,128)(2,1)} collective-permute-done((bf16[4,64,2304]{2,1,0:T(8,128)(2,1)}, bf16[4,64,2304]{2,1,0:T(8,128)(2,1)}, u32[]{:S(2)}, u32[]{:S(2)}) %collective-permute-start.60) | collective-permute-done | bytes 1179680 | tf_op jit(solution)/shard_map/ppermute | solution.py:72
  625.2 13.9 %collective-permute-done.64 = bf16[2,4,32,2304]{3,2,1,0:T(8,128)(2,1)S(1)} collective-permute-done((bf16[2,4,32,2304]{3,2,1,0:T(8,128)(2,1)S(1)}, bf16[2,4,32,2304]{3,2,1,0:T(8,128)(2,1)S(1)}, u32[]{:S(2)}, u32[]{:S(2)}) %collective-permute-start.64) | collective-permute-done | bytes 1179680 | tf_op jit(solution)/shard_map/ppermute | solution.py:72
  642.0 11.1 %collective-permute-done.65 = bf16[4,32,2304]{2,1,0:T(8,128)(2,1)S(1)} collective-permute-done((bf16[4,32,2304]{2,1,0:T(8,128)(2,1)S(1)}, bf16[4,32,2304]{2,1,0:T(8,128)(2,1)S(1)}, u32[]{:S(2)}, u32[]{:S(2)}) %collective-permute-start.65) | collective-permute-done | bytes 589856 | tf_op jit(solution)/shard_map/ppermute | solution.py:72
  663.5 20.0 %collective-permute-done.69 = bf16[64,2304]{1,0:T(8,128)(2,1)S(1)} collective-permute-done((bf16[64,2304]{1,0:T(8,128)(2,1)S(1)}, bf16[64,2304]{1,0:T(8,128)(2,1)S(1)}, u32[]{:S(2)}, u32[]{:S(2)}) %collective-permute-start.69) | collective-permute-done | bytes 294944 | tf_op jit(solution)/shard_map/ppermute | solution.py:72
  692.2 14.2 %collective-permute-done.72 = bf16[64,2304]{1,0:T(8,128)(2,1)S(1)} collective-permute-done((bf16[64,2304]{1,0:T(8,128)(2,1)S(1)}, bf16[64,2304]{1,0:T(8,128)(2,1)S(1)}, u32[]{:S(2)}, u32[]{:S(2)}) %collective-permute-start.72) | collective-permute-done | bytes 294944 | tf_op jit(solution)/shard_map/ppermute | solution.py:72
  709.1 24.3 %collective-permute-done.74 = bf16[4,64,2304]{2,1,0:T(8,128)(2,1)S(1)} collective-permute-done((bf16[4,64,2304]{2,1,0:T(8,128)(2,1)S(1)}, bf16[4,64,2304]{2,1,0:T(8,128)(2,1)S(1)}, u32[]{:S(2)}, u32[]{:S(2)}) %collective-permute-start.74) | collective-permute-done | bytes 1179680 | tf_op jit(solution)/shard_map/ppermute | solution.py:72
  836.2 10.3 collective-permute-done.103
  849.1 12.4 %collective-permute-start.108 = (bf16[144,896]{1,0:T(8,128)(2,1)S(1)}, bf16[144,896]{1,0:T(8,128)(2,1)S(1)}, u32[]{:S(2)}, u32[]{:S(2)}) collective-permute-start(bf16[144,896]{1,0:T(8,128)(2,1)S(1)} %copy-done.74), channel_id=1, source_target_pairs={{0,20},{2,22},{4,16},{6,18},{8,28},{10,30},{12,24},{14,26},{16,4},... | collective-permute-start | bytes 774152 | tf_op jit(solution)/shard_map/ppermute | solution.py:99
  880.7 18.9 %collective-permute-done.111 = bf16[144,896]{1,0:T(8,128)(2,1)S(1)} collective-permute-done((bf16[144,896]{1,0:T(8,128)(2,1)S(1)}, bf16[144,896]{1,0:T(8,128)(2,1)S(1)}, u32[]{:S(2)}, u32[]{:S(2)}) %collective-permute-start.111) | collective-permute-done | bytes 258080 | tf_op jit(solution)/shard_map/ppermute | solution.py:99
  916.3 13.8 %collective-permute-start.78 = (bf16[64,2304]{1,0:T(8,128)(2,1)}, bf16[64,2304]{1,0:T(8,128)(2,1)}, u32[]{:S(2)}, u32[]{:S(2)}) collective-permute-start(bf16[64,2304]{1,0:T(8,128)(2,1)} %get-tuple-element.133), channel_id=1, source_target_pairs={{0,8},{2,10},{4,12},{6,14},{8,0},{10,2},{12,4},{14,6},{16,24},{18,... | collective-permute-start | bytes 884744 | tf_op jit(solution)/shard_map/ppermute | solution.py:72
  937.2 17.0 %collective-permute-done.78 = bf16[64,2304]{1,0:T(8,128)(2,1)} collective-permute-done((bf16[64,2304]{1,0:T(8,128)(2,1)}, bf16[64,2304]{1,0:T(8,128)(2,1)}, u32[]{:S(2)}, u32[]{:S(2)}) %collective-permute-start.78) | collective-permute-done | bytes 294944 | tf_op jit(solution)/shard_map/ppermute | solution.py:72
  1006.0 11.1 %collective-permute-done.93 = bf16[72,1024]{1,0:T(8,128)(2,1)S(1)} collective-permute-done((bf16[72,1024]{1,0:T(8,128)(2,1)S(1)}, bf16[72,1024]{1,0:T(8,128)(2,1)S(1)}, u32[]{:S(2)}, u32[]{:S(2)}) %collective-permute-start.93) | collective-permute-done | bytes 147488 | tf_op jit(solution)/shard_map/ppermute | solution.py:99
  (793 shorter events, 626.8 us)
Async XLA Ops:
  2.3 189.7 %collective-permute-start = (bf16[64,2304]{1,0:T(8,128)(2,1)S(1)}, bf16[64,2304]{1,0:T(8,128)(2,1)}, u32[]{:S(2)}, u32[]{:S(2)}) collective-permute-start(bf16[64,2304]{1,0:T(8,128)(2,1)S(1)} %bitcast.565), channel_id=1, source_target_pairs={{0,4},{2,6},{4,8},{6,10},{8,12},{10,14},{12,0},{14,2},{16,20},{18,... | collective-permute-start | bytes 884744 | tf_op jit(solution)/shard_map/ppermute | solution.py:72
  4.4 187.7 %collective-permute-start.1 = (bf16[64,2304]{1,0:T(8,128)(2,1)S(1)}, bf16[64,2304]{1,0:T(8,128)(2,1)}, u32[]{:S(2)}, u32[]{:S(2)}) collective-permute-start(bf16[64,2304]{1,0:T(8,128)(2,1)S(1)} %bitcast.566), channel_id=1, source_target_pairs={{0,8},{2,10},{4,12},{6,14},{8,0},{10,2},{12,4},{14,6},{16,24},{18,... | collective-permute-start | bytes 884744 | tf_op jit(solution)/shard_map/ppermute | solution.py:72
  6.8 188.1 %collective-permute-start.2 = (bf16[64,2304]{1,0:T(8,128)(2,1)S(1)}, bf16[64,2304]{1,0:T(8,128)(2,1)}, u32[]{:S(2)}, u32[]{:S(2)}) collective-permute-start(bf16[64,2304]{1,0:T(8,128)(2,1)S(1)} %bitcast.567), channel_id=1, source_target_pairs={{0,12},{2,14},{4,0},{6,2},{8,4},{10,6},{12,8},{14,10},{16,28},{18,... | collective-permute-start | bytes 884744 | tf_op jit(solution)/shard_map/ppermute | solution.py:72
  43.2 35.2 %collective-permute-start.33 = (bf16[144,896]{1,0:T(8,128)(2,1)}, bf16[144,896]{1,0:T(8,128)(2,1)}, u32[]{:S(2)}, u32[]{:S(2)}) collective-permute-start(bf16[144,896]{1,0:T(8,128)(2,1)} %bitcast.544), channel_id=1, source_target_pairs={{0,2},{2,0},{4,6},{6,4},{8,10},{10,8},{12,14},{14,12},{16,18},{18,... | collective-permute-start | bytes 774152 | tf_op jit(solution)/shard_map/ppermute | solution.py:99
  45.1 37.0 %collective-permute-start.34 = (bf16[144,896]{1,0:T(8,128)(2,1)}, bf16[144,896]{1,0:T(8,128)(2,1)}, u32[]{:S(2)}, u32[]{:S(2)}) collective-permute-start(bf16[144,896]{1,0:T(8,128)(2,1)} %bitcast.543), channel_id=1, source_target_pairs={{0,4},{2,6},{4,0},{6,2},{8,12},{10,14},{12,8},{14,10},{16,20},{18,... | collective-permute-start | bytes 774152 | tf_op jit(solution)/shard_map/ppermute | solution.py:99
  82.2 139.1 %collective-permute-start.35 = (bf16[144,896]{1,0:T(8,128)(2,1)}, bf16[144,896]{1,0:T(8,128)(2,1)}, u32[]{:S(2)}, u32[]{:S(2)}) collective-permute-start(bf16[144,896]{1,0:T(8,128)(2,1)} %bitcast.542), channel_id=1, source_target_pairs={{0,6},{2,4},{4,2},{6,0},{8,14},{10,12},{12,10},{14,8},{16,22},{18,... | collective-permute-start | bytes 774152 | tf_op jit(solution)/shard_map/ppermute | solution.py:99
  187.0 36.9 %collective-permute-start.36 = (bf16[144,896]{1,0:T(8,128)(2,1)S(1)}, bf16[144,896]{1,0:T(8,128)(2,1)S(1)}, u32[]{:S(2)}, u32[]{:S(2)}) collective-permute-start(bf16[144,896]{1,0:T(8,128)(2,1)S(1)} %bitcast.645), channel_id=1, source_target_pairs={{0,8},{2,10},{4,12},{6,14},{8,0},{10,2},{12,4},{14,6},{16,24},{18,... | collective-permute-start | bytes 774152 | tf_op jit(solution)/shard_map/ppermute | solution.py:99
  192.0 34.7 %collective-permute-start.37 = (bf16[144,896]{1,0:T(8,128)(2,1)S(1)}, bf16[144,896]{1,0:T(8,128)(2,1)S(1)}, u32[]{:S(2)}, u32[]{:S(2)}) collective-permute-start(bf16[144,896]{1,0:T(8,128)(2,1)S(1)} %bitcast.644), channel_id=1, source_target_pairs={{0,10},{2,8},{4,14},{6,12},{8,2},{10,0},{12,6},{14,4},{16,26},{18,... | collective-permute-start | bytes 774152 | tf_op jit(solution)/shard_map/ppermute | solution.py:99
  192.1 35.3 %collective-permute-start.38 = (bf16[144,896]{1,0:T(8,128)(2,1)S(1)}, bf16[144,896]{1,0:T(8,128)(2,1)S(1)}, u32[]{:S(2)}, u32[]{:S(2)}) collective-permute-start(bf16[144,896]{1,0:T(8,128)(2,1)S(1)} %bitcast.643), channel_id=1, source_target_pairs={{0,12},{2,14},{4,8},{6,10},{8,4},{10,6},{12,0},{14,2},{16,28},{18,... | collective-permute-start | bytes 774152 | tf_op jit(solution)/shard_map/ppermute | solution.py:99
  194.9 67.9 %collective-permute-start.20 = (bf16[16,72,1024]{2,1,0:T(8,128)(2,1)S(1)}, bf16[16,72,1024]{2,1,0:T(8,128)(2,1)}, u32[]{:S(2)}, u32[]{:S(2)}) collective-permute-start(bf16[16,72,1024]{2,1,0:T(8,128)(2,1)S(1)} %bitcast_dynamic-update-slice_fusion.45), channel_id=1, source_target_pairs={{0,1},{1,0},{2,3},{3,2},{4,5},{5,4},{6,7},{7,6},{8,9},{9,8},{10,11... | collective-permute-start | bytes 7077896 | tf_op jit(solution)/shard_map/ppermute | solution.py:89
  221.3 36.0 %collective-permute-start.3 = (bf16[4,64,2304]{2,1,0:T(8,128)(2,1)S(1)}, bf16[4,64,2304]{2,1,0:T(8,128)(2,1)S(1)}, u32[]{:S(2)}, u32[]{:S(2)}) collective-permute-start(bf16[4,64,2304]{2,1,0:T(8,128)(2,1)S(1)} %get-tuple-element.166), channel_id=1, source_target_pairs={{0,2},{2,0},{4,6},{6,4},{8,10},{10,8},{12,14},{14,12},{16,18},{18,... | collective-permute-start | bytes 3538952 | tf_op jit(solution)/shard_map/ppermute | solution.py:72
  226.7 44.5 %collective-permute-start.40 = (bf16[144,896]{1,0:T(8,128)(2,1)}, bf16[144,896]{1,0:T(8,128)(2,1)}, u32[]{:S(2)}, u32[]{:S(2)}) collective-permute-start(bf16[144,896]{1,0:T(8,128)(2,1)} %bitcast.537), channel_id=1, source_target_pairs={{0,16},{2,18},{4,20},{6,22},{8,24},{10,26},{12,28},{14,30},{16,0},... | collective-permute-start | bytes 774152 | tf_op jit(solution)/shard_map/ppermute | solution.py:99
  227.4 47.3 %collective-permute-start.41 = (bf16[144,896]{1,0:T(8,128)(2,1)}, bf16[144,896]{1,0:T(8,128)(2,1)}, u32[]{:S(2)}, u32[]{:S(2)}) collective-permute-start(bf16[144,896]{1,0:T(8,128)(2,1)} %bitcast.536), channel_id=1, source_target_pairs={{0,18},{2,16},{4,22},{6,20},{8,26},{10,24},{12,30},{14,28},{16,2},... | collective-permute-start | bytes 774152 | tf_op jit(solution)/shard_map/ppermute | solution.py:99
  231.9 46.0 %collective-permute-start.42 = (bf16[144,896]{1,0:T(8,128)(2,1)}, bf16[144,896]{1,0:T(8,128)(2,1)}, u32[]{:S(2)}, u32[]{:S(2)}) collective-permute-start(bf16[144,896]{1,0:T(8,128)(2,1)} %bitcast.535), channel_id=1, source_target_pairs={{0,20},{2,22},{4,16},{6,18},{8,28},{10,30},{12,24},{14,26},{16,4},... | collective-permute-start | bytes 774152 | tf_op jit(solution)/shard_map/ppermute | solution.py:99
  257.2 30.7 %collective-permute-start.43 = (bf16[144,896]{1,0:T(8,128)(2,1)}, bf16[144,896]{1,0:T(8,128)(2,1)}, u32[]{:S(2)}, u32[]{:S(2)}) collective-permute-start(bf16[144,896]{1,0:T(8,128)(2,1)} %bitcast.534), channel_id=1, source_target_pairs={{0,22},{2,20},{4,18},{6,16},{8,30},{10,28},{12,26},{14,24},{16,6},... | collective-permute-start | bytes 774152 | tf_op jit(solution)/shard_map/ppermute | solution.py:99
  288.0 37.7 %collective-permute-start.22 = (bf16[4,64,2304]{2,1,0:T(8,128)(2,1)S(1)}, bf16[4,64,2304]{2,1,0:T(8,128)(2,1)S(1)}, u32[]{:S(2)}, u32[]{:S(2)}) collective-permute-start(bf16[4,64,2304]{2,1,0:T(8,128)(2,1)S(1)} %bitcast.617), channel_id=1, source_target_pairs={{0,2},{2,0},{4,6},{6,4},{8,10},{10,8},{12,14},{14,12},{16,18},{18,... | collective-permute-start | bytes 3538952 | tf_op jit(solution)/shard_map/ppermute | solution.py:72
  303.5 74.7 %collective-permute-start.48 = (bf16[2304,896]{1,0:T(8,128)(2,1)}, bf16[2304,896]{1,0:T(8,128)(2,1)S(1)}, u32[]{:S(2)}, u32[]{:S(2)}) collective-permute-start(bf16[2304,896]{1,0:T(8,128)(2,1)} %bitcast.80), channel_id=1, source_target_pairs={{0,1},{1,0},{2,3},{3,2},{4,5},{5,4},{6,7},{7,6},{8,9},{9,8},{10,11... | collective-permute-start | bytes 12386312 | tf_op jit(solution)/shard_map/ppermute | solution.py:89
  530.4 30.0 %collective-permute-start.56 = (bf16[64,2304]{1,0:T(8,128)(2,1)}, bf16[64,2304]{1,0:T(8,128)(2,1)}, u32[]{:S(2)}, u32[]{:S(2)}) collective-permute-start(bf16[64,2304]{1,0:T(8,128)(2,1)} %get-tuple-element.168), channel_id=1, source_target_pairs={{0,1},{1,0},{2,3},{3,2},{4,5},{5,4},{6,7},{7,6},{8,9},{9,8},{10,11... | collective-permute-start | bytes 884744 | tf_op jit(solution)/shard_map/ppermute | solution.py:89
  622.0 165.9 %collective-permute-start.98 = (bf16[2304,896]{0,1:T(8,128)(2,1)}, bf16[2304,896]{0,1:T(8,128)(2,1)}, u32[]{:S(2)}, u32[]{:S(2)}) collective-permute-start(bf16[2304,896]{0,1:T(8,128)(2,1)} %broadcast_dynamic-update-slice_fusion.1), channel_id=1, source_target_pairs={{0,1},{1,0},{2,3},{3,2},{4,5},{5,4},{6,7},{7,6},{8,9},{9,8},{10,11... | collective-permute-start | bytes 12386312 | tf_op jit(solution)/shard_map/ppermute | solution.py:89
  776.5 185.6 %collective-permute-start.81 = (bf16[16,72,1024]{2,1,0:T(8,128)(2,1)}, bf16[16,72,1024]{2,1,0:T(8,128)(2,1)}, u32[]{:S(2)}, u32[]{:S(2)}) collective-permute-start(bf16[16,72,1024]{2,1,0:T(8,128)(2,1)} %fusion.14), channel_id=1, source_target_pairs={{0,1},{1,0},{2,3},{3,2},{4,5},{5,4},{6,7},{7,6},{8,9},{9,8},{10,11... | collective-permute-start | bytes 7077896 | tf_op jit(solution)/shard_map/ppermute | solution.py:89
  777.8 33.4 %all-to-all-start.1 = ((f32[16,4,144]{2,1,0:T(4,128)}), f32[16,4,144]{2,1,0:T(4,128)S(1)}, u32[]{:S(2)}, u32[]{:S(2)}) async-start(f32[16,4,144]{2,1,0:T(4,128)} %copy.182), calls=%async_computation.1 | async-start | bytes 131072 | tf_op jit(solution)/shard_map/all_to_all | solution.py:491
  808.5 104.9 %collective-permute-start.76 = (bf16[4,64,2304]{2,1,0:T(8,128)(2,1)}, bf16[4,64,2304]{2,1,0:T(8,128)(2,1)}, u32[]{:S(2)}, u32[]{:S(2)}) collective-permute-start(bf16[4,64,2304]{2,1,0:T(8,128)(2,1)} %bitcast.118), channel_id=1, source_target_pairs={{0,2},{2,0},{4,6},{6,4},{8,10},{10,8},{12,14},{14,12},{16,18},{18,... | collective-permute-start | bytes 3538952 | tf_op jit(solution)/shard_map/ppermute | solution.py:72
  817.0 29.5 %collective-permute-start.103 = (bf16[144,896]{1,0:T(8,128)(2,1)}, bf16[144,896]{1,0:T(8,128)(2,1)S(1)}, u32[]{:S(2)}, u32[]{:S(2)}) collective-permute-start(bf16[144,896]{1,0:T(8,128)(2,1)} %get-tuple-element.59), channel_id=1, source_target_pairs={{0,10},{2,8},{4,14},{6,12},{8,2},{10,0},{12,6},{14,4},{16,26},{18,... | collective-permute-start | bytes 774152 | tf_op jit(solution)/shard_map/ppermute | solution.py:99
  916.3 37.9 %collective-permute-start.78 = (bf16[64,2304]{1,0:T(8,128)(2,1)}, bf16[64,2304]{1,0:T(8,128)(2,1)}, u32[]{:S(2)}, u32[]{:S(2)}) collective-permute-start(bf16[64,2304]{1,0:T(8,128)(2,1)} %get-tuple-element.133), channel_id=1, source_target_pairs={{0,8},{2,10},{4,12},{6,14},{8,0},{10,2},{12,4},{14,6},{16,24},{18,... | collective-permute-start | bytes 884744 | tf_op jit(solution)/shard_map/ppermute | solution.py:72
  (219 other events, 3716.1 us)

commit v2 on v1

v2 whole, which is shorter than its diff:
```python
import jax
import jax.numpy as jnp
from jax import lax
from jax.experimental import pallas as pl
from jax.experimental.pallas import tpu as pltpu
from jax.sharding import PartitionSpec as P

HEAD_DIM = 256

epsilon = 1e-06
softcap = 50.0
theta = 10000.0
floor_value = -1e30
low = jnp.bfloat16
wide = jnp.float32
chip_axes = ("dp", "context")


def product(left_side, right_side):
    return jnp.dot(left_side, right_side, preferred_element_type=wide)


def product_right_t(left_side, right_side):
    return lax.dot_general(left_side, right_side, (((1,), (1,)), ((), ())), preferred_element_type=wide)


def product_left_t(left_side, right_side):
    return lax.dot_general(left_side, right_side, (((0,), (0,)), ((), ())), preferred_element_type=wide)


def inverse_size(values):
    return lax.rsqrt(jnp.mean(values * values, axis=-1, keepdims=True) + epsilon)


def norm_back(unit, inverse, scaling, upstream):
    inner = upstream * scaling
    return inverse * (inner - unit * jnp.mean(inner * unit, axis=-1, keepdims=True))


def turn(values, cosine, sine_part):
    half_width = values.shape[-1] // 2
    former = values[..., :half_width]
    latter = values[..., half_width:]
    return jnp.concatenate(
        [former * cosine - latter * sine_part, latter * cosine + former * sine_part], axis=-1
    )


def geglu(gate_in, upward):
    return jax.nn.gelu(gate_in, approximate=True) * upward


def pick(array, at, axis):
    return lax.dynamic_index_in_dim(array, at, axis, keepdims=False)


def hold(*trees):
    return lax.optimization_barrier(trees)


def placed(line, core, sources, rows):
    blocks, lanes = sources[0].shape[0], sources[0].shape[2]
    if rows % 16:
        ins = [source[:, :rows] for source in sources]
        lines = [
            jnp.stack([jnp.where(line == 0, a, b), jnp.where(line == 0, b, a)])
            for a, b in (ins[:2], ins[2:])
        ]
        return jnp.where(core == 0, lines[0], lines[1]), jnp.where(core == 0, lines[1], lines[0])

    def kernel(place_ref, *refs):
        ins, outs = refs[:4], refs[4:]
        for put in range(2):
            for at in range(2):
                chosen = (place_ref[0] ^ at) + 2 * (place_ref[1] ^ put)
                for number in range(4):

                    @pl.when(chosen == number)
                    def _(put=put, at=at, number=number):
                        outs[put][at] = ins[number][:, :rows]

    return pl.pallas_call(
        kernel,
        in_specs=[pl.BlockSpec(memory_space=pltpu.SMEM)] + [pl.BlockSpec(memory_space=pltpu.VMEM)] * 4,
        out_specs=[pl.BlockSpec(memory_space=pltpu.VMEM)] * 2,
        out_shape=[jax.ShapeDtypeStruct((2, blocks, rows, lanes), low)] * 2,
        compiler_params=pltpu.CompilerParams(vmem_limit_bytes=32 * 2**20),
        cost_estimate=pl.CostEstimate(
            flops=0, transcendentals=0, bytes_accessed=16 * blocks * rows * lanes
        ),
    )(jnp.stack([line, core]).astype(jnp.int32), *sources)


class Slice:
    def __init__(self):
        self.dp = lax.axis_size("dp")
        self.context = lax.axis_size("context")
        self.ranks = self.context // 2
        self.chips = self.dp * self.context
        self.core = lax.axis_index("tensor")
        self.place = lax.axis_index("context")
        self.rank = self.place // 2
        self.side = self.place % 2
        self.line = lax.axis_index("dp")

    def send(self, block, where):
        pairs = []
        for dp in range(self.dp):
            for rank in range(self.ranks):
                for side in range(2):
                    pairs.append(
                        (self.index(dp, rank, side), self.index(*where(dp, rank, side)))
                    )
        return lax.ppermute(block, chip_axes, pairs)

    def index(self, dp, rank, side):
        return (dp * self.ranks + rank % self.ranks) * 2 + side

    def across(self, block):
        return self.send(block, lambda dp, rank, side: (dp, rank, 1 - side))

    def over(self, block):
        return self.send(block, lambda dp, rank, side: (1 - dp, rank, side))

    def along(self, block, step):
        if step % self.ranks == 0:
            return block
        return self.send(block, lambda dp, rank, side: (dp, rank + step, side))

    def swap(self, block):
        return lax.ppermute(block, "tensor", [(0, 1), (1, 0)])

    def ordered(self, mine, other):
        first = self.core == 0
        return jnp.where(first, mine, other), jnp.where(first, other, mine)

    def moves(self, block):
        return [self.along(block, step) for step in range(self.ranks)]

    def returned(self, blocks):
        total = 0.0
        for step, block in enumerate(blocks):
            if step:
                block = self.along(block.astype(low), -step)
            total = total + block.astype(wide)
        return total

    def to_ranks(self, array):
        groups = [[rank * 2 + side for rank in range(self.ranks)] for side in range(2)]
        return lax.all_to_all(array, "context", 0, 0, tiled=True, axis_index_groups=groups)

    def square(self):
        return [
            [self.index(dp, rank, side) for dp in range(self.dp) for side in range(2)]
            for rank in range(self.ranks)
        ]

    def weights_in(self, array):
        ranks, rows, units = array.shape
        whole = lax.all_gather(array, chip_axes, axis=0, tiled=False, axis_index_groups=self.square())
        return whole.reshape(self.dp, 2, ranks, rows, units)

    def by_model_row(self, whole):
        return jnp.transpose(whole, (0, 2, 1, 3, 4)).reshape(-1, whole.shape[-1])

    def grads_out(self, grad, rows):
        units = grad.shape[1]
        parts = grad.astype(low).reshape(self.dp, self.ranks, 2, rows, units)
        parts = jnp.transpose(parts, (0, 2, 1, 3, 4)).reshape(-1, units)
        total = lax.psum_scatter(
            parts, chip_axes, scatter_dimension=0, tiled=True, axis_index_groups=self.square()
        )
        return total.reshape(self.ranks, rows, units)


def body(
    tokens,
    w_query,
    w_key,
    w_value,
    w_out,
    w_gate,
    w_up,
    w_down,
    gain_attn_in,
    gain_attn_out,
    gain_ffw_in,
    gain_ffw_out,
    cotangent,
):
    net = Slice()
    core, chips, ranks = net.core, net.chips, net.ranks
    span = tokens.shape[1]
    width = tokens.shape[2]
    half = span // 2
    rows = w_query.shape[0]
    heads = 2 * w_query.shape[1] // HEAD_DIM
    kv_heads = 2 * w_key.shape[1] // HEAD_DIM
    repeat = heads // kv_heads
    share = net.context // heads
    score_scale = HEAD_DIM ** (-0.5)
    units = w_gate.shape[1] // ranks
    q_cols, k_cols = w_query.shape[1], w_key.shape[1]
    is_front = core == 0

    own_tokens = lax.dynamic_slice_in_dim(tokens[0], core * half, half, 0)
    upstream = lax.dynamic_slice_in_dim(cotangent[0], core * half, half, 0)

    front = jnp.concatenate([w_query, w_key], axis=1)
    back = jnp.concatenate([w_out, w_value], axis=1)
    mine = jnp.where(is_front, front, back)
    theirs = net.swap(jnp.where(is_front, back, front))
    low_heads, high_heads = net.ordered(mine, theirs)

    def by_head(begin, end):
        both = jnp.concatenate([low_heads[:, begin:end], high_heads[:, begin:end]], axis=1)
        return jnp.transpose(both.reshape(rows, -1, HEAD_DIM), (1, 0, 2))

    gain_row = jnp.concatenate([gain_attn_in, gain_attn_out, gain_ffw_in, gain_ffw_out])
    gain_lanes = -(-4 * rows // (2 * HEAD_DIM))
    gain_row = jnp.pad(gain_row, (0, gain_lanes * 2 * HEAD_DIM - 4 * rows))
    gain_row = jnp.broadcast_to(
        gain_row.reshape(1, gain_lanes, 2 * HEAD_DIM), (heads, gain_lanes, 2 * HEAD_DIM)
    )
    head_sets = jnp.concatenate(
        [
            jnp.concatenate(
                [by_head(0, q_cols), jnp.repeat(by_head(q_cols, q_cols + k_cols), repeat, axis=0)],
                axis=2,
            ),
            gain_row,
        ],
        axis=1,
    )
    head_sets = jnp.repeat(head_sets, share, axis=0)
    part = lax.all_to_all(head_sets, "context", 0, 0, tiled=True)
    token_blocks = jnp.stack(net.moves(own_tokens))

    def by_rank(w):
        return jnp.transpose(w.reshape(rows, ranks, units), (1, 0, 2))

    gate_set, up_set, down_set = by_rank(w_gate), by_rank(w_up), by_rank(w_down)
    part, token_blocks, gate_set, up_set, down_set = hold(
        part, token_blocks, gate_set, up_set, down_set
    )
    token_blocks = jnp.stack([token_blocks, net.across(token_blocks)])
    part_line = net.over(part)
    gate_set = net.to_ranks(gate_set)
    token_blocks, part, part_line, gate_set, up_set = hold(
        token_blocks, part, part_line, gate_set, up_set
    )
    gate_units = net.weights_in(gate_set)
    up_set = net.to_ranks(up_set)

    part_core, part_both = net.swap(part), net.swap(part_line)
    front_weights, back_weights = placed(
        net.line, core, [part, part_line, part_core, part_both], rows
    )
    front_weights = front_weights.reshape(width, 2 * HEAD_DIM)
    back_weights = back_weights.reshape(width, 2 * HEAD_DIM)
    first_line = net.line == 0
    gain_own, gain_other = part[:, rows:], part_line[:, rows:]
    gain_rows = jnp.concatenate(
        [jnp.where(first_line, gain_own, gain_other), jnp.where(first_line, gain_other, gain_own)]
    ).reshape(chips, -1)
    gains = gain_rows[:, : 4 * rows].reshape(chips, 4, rows)
    gains = jnp.transpose(gains, (1, 0, 2)).reshape(4, width).astype(wide)
    scale_in, scale_mid, scale_pre, scale_out = gains[0], gains[1], gains[2], gains[3]
    w_out_head = back_weights[:, :HEAD_DIM]
    w_value_head = back_weights[:, HEAD_DIM:]

    own_inputs = own_tokens.astype(wide)
    inputs = token_blocks.reshape(-1, width).astype(wide)
    units_in = inputs * inverse_size(inputs)
    normed_low = (units_in * scale_in).astype(low)
    block_places = jnp.concatenate(
        [(net.rank - jnp.arange(ranks)) % ranks * 2 + side for side in (net.side, 1 - net.side)]
    )
    offsets = jnp.arange(half, dtype=jnp.int32)
    places = (block_places[:, None] * span + core * half + offsets[None, :]).reshape(-1)
    other_places = places + (1 - 2 * core) * half
    exponent = jnp.arange(HEAD_DIM // 2, dtype=wide) * (-2.0 / HEAD_DIM)
    angles = places.astype(wide)[:, None] * (theta**exponent)[None, :]
    cosine, sine_part = jnp.cos(angles), jnp.sin(angles)
    asked = tuple(range(0, ranks, max(share // 2, 1)))

    def asked_rows(array):
        if share == 1:
            return array
        blocks = array.reshape((2, ranks, half) + array.shape[1:])
        return jnp.concatenate([blocks[0, step] for step in asked])

    query_key = product(normed_low, front_weights)
    queries = asked_rows(turn(query_key[:, :HEAD_DIM], cosine, sine_part).astype(low))
    keys = turn(query_key[:, HEAD_DIM:], cosine, sine_part).astype(low)
    values = product(normed_low, w_value_head).astype(low)
    own_kv = jnp.concatenate([keys, values], axis=1)
    all_kv = jnp.concatenate([own_kv, net.swap(own_kv)])
    all_keys, all_values = all_kv[:, :HEAD_DIM], all_kv[:, HEAD_DIM:]
    key_places = jnp.concatenate([places, other_places])
    allowed = key_places[None, :] <= asked_rows(places)[:, None]
    scores = product_right_t(queries, all_keys) * score_scale
    bent = jnp.tanh(scores / softcap)
    capped = jnp.where(allowed, softcap * bent, floor_value)
    shifted = jnp.exp(capped - jnp.max(capped, axis=-1, keepdims=True))
    probabilities = shifted / jnp.sum(shifted, axis=-1, keepdims=True)
    probabilities_low = probabilities.astype(low)
    mixed_low = product(probabilities_low, all_values).astype(low)
    out_parts = product_right_t(mixed_low, w_out_head).astype(low)
    out_parts, up_set, down_set = hold(out_parts, up_set, down_set)
    up_units = net.weights_in(up_set)
    down_set = net.to_ranks(down_set)
    if share == 1:
        out_parts = out_parts.reshape(2, ranks, half, width)
        out_parts = out_parts[0].astype(wide) + net.across(out_parts[1]).astype(wide)
    else:
        out_parts = out_parts.reshape(len(asked), half, width).astype(wide)
    projected = 0.0
    for at, step in enumerate(asked):
        block = out_parts[at]
        if step:
            block = net.along(block.astype(low), -step).astype(wide)
        projected = projected + block

    projected, down_set = hold(projected, down_set)
    down_units = net.weights_in(down_set)

    inverse_mid = inverse_size(projected)
    unit_mid = projected * inverse_mid
    middle = own_inputs + unit_mid * scale_mid
    inverse_pre = inverse_size(middle)
    unit_pre = middle * inverse_pre
    normed_two_low = (unit_pre * scale_pre).astype(low)
    two_blocks = jnp.stack(net.moves(normed_two_low)).reshape(-1, width)
    two_blocks, gate_units, up_units = hold(two_blocks, gate_units, up_units)
    pair_units = jnp.concatenate([net.by_model_row(gate_units), net.by_model_row(up_units)], axis=1)

    all_two = jnp.concatenate([two_blocks, net.swap(two_blocks)])
    pair = product(all_two, pair_units)
    gate_in, upward = pair[:, :units], pair[:, units:]
    hidden_low = geglu(gate_in, upward).astype(low)
    hidden_low, down_units = hold(hidden_low, down_units)
    down_units = net.by_model_row(down_units)

    def core_total(part):
        count = ranks * half
        part = part.astype(low)
        return part[:count].astype(wide) + net.swap(part[count:]).astype(wide)

    def line_total(own):
        return net.returned(list(own.reshape(ranks, half, width)))

    branch = line_total(core_total(product_right_t(hidden_low, down_units)))
    inverse_out = inverse_size(branch)
    unit_out = branch * inverse_out
    own_output = (middle + unit_out * scale_out).astype(low)

    grad_ffw_out = jnp.sum(upstream * unit_out, axis=0)
    d_branch_low = norm_back(unit_out, inverse_out, scale_out, upstream).astype(low)
    branch_blocks = jnp.stack(net.moves(d_branch_low)).reshape(-1, width)
    all_branch = jnp.concatenate([branch_blocks, net.swap(branch_blocks)])

    down_grad = product_left_t(all_branch, hidden_low).astype(low)
    down_grad, all_branch = hold(down_grad, all_branch)
    down_grad = net.grads_out(down_grad, rows)
    d_hidden = product(all_branch, down_units)
    _, pull = jax.vjp(geglu, gate_in, upward)
    d_gate, d_up = pull(d_hidden)
    d_pair_low = jnp.concatenate([d_gate.astype(low), d_up.astype(low)], axis=1)
    d_two = core_total(product_right_t(d_pair_low, pair_units))
    d_normed_two = line_total(d_two)
    d_normed_two, d_pair_low, all_two = hold(d_normed_two, d_pair_low, all_two)
    pair_grad = product_left_t(all_two, d_pair_low).astype(low)
    gate_grad = net.grads_out(pair_grad[:, :units], rows)
    up_grad = pair_grad[:, units:]
    gate_grad, up_grad = hold(gate_grad, up_grad)
    up_grad = net.grads_out(up_grad, rows)
    grad_ffw_in = jnp.sum(d_normed_two * unit_pre, axis=0)
    d_middle = upstream + norm_back(unit_pre, inverse_pre, scale_pre, d_normed_two)
    grad_attn_out = jnp.sum(d_middle * unit_mid, axis=0)
    d_projected_low = norm_back(unit_mid, inverse_mid, scale_mid, d_middle).astype(low)
    d_projected_all = jnp.stack(net.moves(d_projected_low))
    d_projected_all, down_grad = hold(d_projected_all, down_grad)
    down_grad = net.to_ranks(down_grad)
    d_projected_all = jnp.stack([d_projected_all, net.across(d_projected_all)]).reshape(-1, width)
    d_projected_asked = asked_rows(d_projected_all)
    d_mixed_low = product(d_projected_asked, w_out_head).astype(low)
    d_prob = product_right_t(d_mixed_low, all_values)
    delta = jnp.sum(probabilities * d_prob, axis=-1, keepdims=True)
    d_capped = probabilities * (d_prob - delta)
    d_scores = (d_capped * (1.0 - bent * bent)).astype(low)
    d_queries = product(d_scores, all_keys) * score_scale
    d_keys = product_left_t(d_scores, queries) * score_scale
    d_values = product_left_t(probabilities_low, d_mixed_low)
    d_kv = jnp.concatenate([d_keys, d_values], axis=1)
    count = places.shape[0]
    d_kv = d_kv[:count] + net.swap(d_kv[count:].astype(low)).astype(wide)
    d_query_low = turn(d_queries, asked_rows(cosine), -asked_rows(sine_part)).astype(low)
    d_key_low = turn(d_kv[:, :HEAD_DIM], cosine, -sine_part).astype(low)
    if share != 1:
        blocks = jnp.zeros((2, ranks, half, HEAD_DIM), low)
        d_query_low = blocks.at[0, jnp.array(asked)].set(
            d_query_low.reshape(len(asked), half, HEAD_DIM)
        )
        d_query_low = d_query_low.reshape(-1, HEAD_DIM)
    d_value_low = d_kv[:, HEAD_DIM:].astype(low)
    d_front_low = jnp.concatenate([d_query_low, d_key_low], axis=1)
    d_normed_part = product_right_t(d_front_low, front_weights)
    d_normed_part = d_normed_part + product_right_t(d_value_low, w_value_head)
    grad_attn_in = jnp.sum(d_normed_part * units_in, axis=0)
    d_normed_low = d_normed_part.astype(low).reshape(2, ranks, half, width)
    gate_grad, down_grad, d_normed_low, d_front_low, d_value_low = hold(
        gate_grad, down_grad, d_normed_low, d_front_low, d_value_low
    )
    gate_grad = net.to_ranks(gate_grad)
    d_normed = d_normed_low[0].astype(wide) + net.across(d_normed_low[1]).astype(wide)
    d_normed, gate_grad = hold(d_normed, gate_grad)
    front_grads = product_left_t(normed_low, d_front_low)
    back_grads = jnp.concatenate(
        [
            product_left_t(d_projected_asked, mixed_low),
            product_left_t(normed_low, d_value_low),
        ],
        axis=1,
    )
    given = jnp.where(is_front, back_grads, front_grads).astype(low)
    kept = jnp.where(is_front, front_grads, back_grads)
    kept = (kept + net.swap(given).astype(wide)).astype(low)
    kept = kept.reshape(net.dp, net.context, rows, 2 * HEAD_DIM)
    d_normed = net.returned(list(d_normed))

    def line_sum(array):
        return pick(array, net.line, 0).astype(wide) + net.over(pick(array, 1 - net.line, 0)).astype(wide)

    gain_grads = jnp.stack([grad_attn_in, grad_attn_out, grad_ffw_in, grad_ffw_out])
    gain_grads = gain_grads + net.swap(gain_grads)
    gain_grads = jnp.transpose(gain_grads.reshape(4, net.dp, net.context, rows), (1, 2, 0, 3))
    gain_grads = line_sum(gain_grads.reshape(net.dp, net.context, 4 * rows))
    gain_grads = jnp.pad(gain_grads, ((0, 0), (0, gain_lanes * 2 * HEAD_DIM - 4 * rows)))
    gain_grads = gain_grads.reshape(net.context, gain_lanes, 2 * HEAD_DIM)
    gain_high = gain_grads.astype(low)
    gain_low = (gain_grads - gain_high.astype(wide)).astype(low)
    head_grads = jnp.concatenate([line_sum(kept).astype(low), gain_high, gain_low], axis=1)
    own_inverse = inverse_size(own_inputs)
    own_grad = d_middle + norm_back(own_inputs * own_inverse, own_inverse, scale_in, d_normed)
    layer_output = jnp.concatenate(net.ordered(own_output, net.swap(own_output)))
    input_grad = jnp.concatenate(net.ordered(own_grad, net.swap(own_grad)))
    got = lax.all_to_all(head_grads, "context", 0, 0, tiled=True)
    got, up_grad = hold(got, up_grad)
    up_grad = net.to_ranks(up_grad)
    got = got.astype(wide)
    gain_got = got[:, rows:].reshape(net.context, 2, -1).sum(axis=(0, 1))
    gain_got = gain_got[: 4 * rows].reshape(4, rows)

    def heads_total(at, count_of):
        piece = got[:, :rows, at * HEAD_DIM : (at + 1) * HEAD_DIM]
        piece = piece.reshape(count_of, -1, rows, HEAD_DIM).sum(axis=1)
        return jnp.transpose(piece, (1, 0, 2)).reshape(rows, 2, -1)

    total = jnp.concatenate([heads_total(0, heads), heads_total(1, kv_heads)], axis=2)
    kept = pick(total, core, 1)
    given = pick(total, 1 - core, 1)
    front, back = net.ordered(kept, net.swap(given.astype(low)).astype(wide))
    grad_query, grad_key = front[:, :q_cols], front[:, q_cols:]
    grad_out, grad_value = back[:, :q_cols], back[:, q_cols:]

    def by_units(pieces):
        return jnp.transpose(pieces, (1, 0, 2)).reshape(rows, ranks * units).astype(wide)

    return (
        layer_output[None],
        input_grad[None],
        grad_query,
        grad_key,
        grad_value,
        grad_out,
        by_units(gate_grad),
        by_units(up_grad),
        by_units(down_grad),
        gain_got[0],
        gain_got[1],
        gain_got[2],
        gain_got[3],
    )


def solution(mesh):
    tokens_spec = P("dp", "context", None)
    weight_spec = P(("dp", "context"), "tensor")
    gain_spec = P(("dp", "context"))
    return jax.shard_map(
        body,
        mesh=mesh,
        in_specs=(tokens_spec,) + (weight_spec,) * 7 + (gain_spec,) * 4 + (tokens_spec,),
        out_specs=(tokens_spec,) * 2 + (weight_spec,) * 7 + (gain_spec,) * 4,
        check_vma=False,
    )
```

time: 1050 us -> 764 us (0.73)
  starting transfers between devices: 256 us -> 113 us
  local copies, waits for them, and re-layouts: 177 us -> 102 us
  waiting for transfers between devices: 463 us -> 388 us
  between operations: 4.1 us -> 15.9 us
    ppermute x60 -> x0, waiting for transfers between devices: 142 us -> none  [exchange(): pieces.append(lax.ppermute(pick(self.me ^ turn_by), chip_axes, pairs))]
    ppermute x60 -> x0, starting transfers between devices: 123 us -> none  [exchange(): pieces.append(lax.ppermute(pick(self.me ^ turn_by), chip_axes, pairs))]
    all_to_all x2 -> x8, waiting for transfers between devices: 0.01 us -> 57.9 us  [the longest x6 36.7 us: to_ranks(): lax.all_to_all(array, 'context', 0, 0, tiled=True, axis_index_groups=groups)]
    dynamic_update_slice x62 -> x0, local copies, waits for them, and re-layouts: 30.6 us -> none  [exchange(): lax.dynamic_update_index_in_dim(result, piece, self.me ^ turn_by, 0)]
    dynamic_slice x4 -> x1, local copies, waits for them, and re-layouts: 27.8 us -> 2.24 us  [pick(): return lax.dynamic_index_in_dim(array, at, axis, keepdims=False)]
    ppermute x11 -> x14, starting transfers between devices: 43.8 us -> 20.3 us  [swap(): return lax.ppermute(block, 'tensor', [(0, 1), (1, 0)])]
    all_to_all x2 -> x8, starting transfers between devices: 14.5 us -> 37.3 us  [the longest x6 25.7 us: to_ranks(): lax.all_to_all(array, 'context', 0, 0, tiled=True, axis_index_groups=groups)]
    unnamed x298 -> x164, local copies, waits for them, and re-layouts: 40.8 us -> 18.1 us
  transfers between devices with their start and end apart: 117 -> 59, of which waited for: 53 -> 32; matrix products, arithmetic and copies ran while one was open for 23% -> 25% of each run, Pallas kernels for 0% -> 0%
where the time goes in v2:
time: 764 us; the launch traced here: 753 us
  waiting for transfers between devices  388 us (51%)
  starting transfers between devices  113 us (15%)
  local copies, waits for them, and re-layouts  102 us (13%)
  other arithmetic  69.3 us (9%)
  matrix products  62.9 us (8%)
  between operations  15.9 us (2%)
    ppermute x31, waiting for transfers between devices, send(): return lax.ppermute(block, chip_axes, pairs)  300 us
    ppermute x31, starting transfers between devices, send(): return lax.ppermute(block, chip_axes, pairs)  54.7 us
    all_to_all x6, waiting for transfers between devices, to_ranks(): lax.all_to_all(array, 'context', 0, 0, tiled=True, axis_index_groups=groups)  36.7 us
    all_to_all x6, starting transfers between devices, to_ranks(): lax.all_to_all(array, 'context', 0, 0, tiled=True, axis_index_groups=groups)  25.7 us
    dot_general x7, matrix products, product(): return jnp.dot(left_side, right_side, preferred_element_type=wide)  21.9 us
    all_to_all x1, waiting for transfers between devices, body(): got = lax.all_to_all(head_grads, 'context', 0, 0, tiled=True)  21.2 us
    all_gather x3, waiting for transfers between devices, weights_in(): lax.all_gather(array, chip_axes, axis=0, tiled=False, axis_index_groups=s...  20.9 us
    dot_general x7, matrix products, product_right_t(): lax.dot_general(left_side, right_side, (((1,), (1,)), ((), ())), preferre...  20.8 us
  transfers between devices with their start and end apart: 59, of which 32 were waited for; matrix products, arithmetic and copies ran while one was open for 25% of the time, Pallas kernels for 0%

profile of v2, /device:TPU:1, one launch (start us, length us, event | category | flops | bytes accessed | tf_op | source)
XLA Modules:
  0.0 752.5 jit_solution(14069308901975487003)
XLA Ops:
  34.8 12.9 %collective-permute-done.3 = bf16[64,2304]{1,0:T(8,128)(2,1)S(1)} collective-permute-done((bf16[64,2304]{1,0:T(8,128)(2,1)S(1)}, bf16[64,2304]{1,0:T(8,128)(2,1)S(1)}, u32[]{:S(2)}, u32[]{:S(2)}) %collective-permute-start.3) | collective-permute-done | bytes 294944 | tf_op jit(solution)/shard_map/ppermute | solution.py:114
  47.7 27.6 %collective-permute-done.2 = bf16[64,2304]{1,0:T(8,128)(2,1)S(1)} collective-permute-done((bf16[64,2304]{1,0:T(8,128)(2,1)S(1)}, bf16[64,2304]{1,0:T(8,128)(2,1)S(1)}, u32[]{:S(2)}, u32[]{:S(2)}) %collective-permute-start.2) | collective-permute-done | bytes 294944 | tf_op jit(solution)/shard_map/ppermute | solution.py:114
  85.2 23.4 %collective-permute-done.4 = bf16[4,64,2304]{2,1,0:T(8,128)(2,1)S(1)} collective-permute-done((bf16[4,64,2304]{2,1,0:T(8,128)(2,1)}, bf16[4,64,2304]{2,1,0:T(8,128)(2,1)S(1)}, u32[]{:S(2)}, u32[]{:S(2)}) %collective-permute-start.4) | collective-permute-done | bytes 1179680 | tf_op jit(solution)/shard_map/ppermute | solution.py:114
  148.1 23.0 %all-to-all-done.2 = bf16[4,144,1152]{2,1,0:T(8,128)(2,1)} async-done(((bf16[4,144,1152]{2,1,0:T(8,128)(2,1)}), bf16[4,144,1152]{2,1,0:T(8,128)(2,1)}, u32[]{:S(2)}, u32[]{:S(2)}) %all-to-all-start.2) | async-done | bytes 1327136 | tf_op jit(solution)/shard_map/all_to_all | solution.py:150
  180.6 29.7 %collective-permute-done.9 = bf16[4,64,2304]{2,1,0:T(8,128)(2,1)} collective-permute-done((bf16[4,64,2304]{2,1,0:T(8,128)(2,1)}, bf16[4,64,2304]{2,1,0:T(8,128)(2,1)}, u32[]{:S(2)}, u32[]{:S(2)}) %collective-permute-start.9) | collective-permute-done | bytes 1179680 | tf_op jit(solution)/shard_map/ppermute | solution.py:114
  220.7 15.8 %collective-permute-done.11 = bf16[64,2304]{1,0:T(8,128)(2,1)S(1)} collective-permute-done((bf16[64,2304]{1,0:T(8,128)(2,1)S(1)}, bf16[64,2304]{1,0:T(8,128)(2,1)S(1)}, u32[]{:S(2)}, u32[]{:S(2)}) %collective-permute-start.11) | collective-permute-done | bytes 294944 | tf_op jit(solution)/shard_map/ppermute | solution.py:114
  254.4 19.8 %collective-permute-done.14 = bf16[64,2304]{1,0:T(8,128)(2,1)S(1)} collective-permute-done((bf16[64,2304]{1,0:T(8,128)(2,1)S(1)}, bf16[64,2304]{1,0:T(8,128)(2,1)S(1)}, u32[]{:S(2)}, u32[]{:S(2)}) %collective-permute-start.14) | collective-permute-done | bytes 294944 | tf_op jit(solution)/shard_map/ppermute | solution.py:114
  283.0 7.9 %fusion.1 = f32[512,2304]{1,0:T(8,128)} fusion(bf16[512,2304]{1,0:T(8,128)(2,1)S(1)} %constant_dynamic-update-slice_fusion.4, bf16[2304,1152]{1,0:T(8,128)(2,1)S(1)} %bitcast.212, bf16[2304,1152]{1,0:T(8,128)(2,1)S(1)} %bitcast.214), kind=kOutput, calls=%fused_computation.4 | convolution fusion | flops 5457051648 | bytes 17694720 | tf_op jit(solution)/shard_map/dot_general | solution.py:20
  295.1 20.9 %all-gather.11.cloned.1.call-done = bf16[16,144,1152]{2,1,0:T(8,128)(2,1)} async-done(((bf16[4,144,1152]{2,1,0:T(8,128)(2,1)}), bf16[16,144,1152]{2,1,0:T(8,128)(2,1)}) %all-gather.11.cloned.1.call-update) | async-done | bytes 5308432 | tf_op jit(solution)/shard_map/all_gather | solution.py:160
  338.9 13.3 %collective-permute-done.19 = bf16[64,2304]{1,0:T(8,128)(2,1)} collective-permute-done((bf16[64,2304]{1,0:T(8,128)(2,1)}, bf16[64,2304]{1,0:T(8,128)(2,1)}, u32[]{:S(2)}, u32[]{:S(2)}) %collective-permute-start.19) | collective-permute-done | bytes 294944 | tf_op jit(solution)/shard_map/ppermute | solution.py:114
  369.8 19.8 %collective-permute-done.23 = bf16[64,2304]{1,0:T(8,128)(2,1)S(1)} collective-permute-done((bf16[64,2304]{1,0:T(8,128)(2,1)S(1)}, bf16[64,2304]{1,0:T(8,128)(2,1)S(1)}, u32[]{:S(2)}, u32[]{:S(2)}) %collective-permute-start.23) | collective-permute-done | bytes 294944 | tf_op jit(solution)/shard_map/ppermute | solution.py:114
  401.5 9.3 %fusion.9 = (bf16[512,1152]{1,0:T(8,128)(2,1)S(1)}, bf16[512,1152]{1,0:T(8,128)(2,1)S(1)}) fusion(f32[512,2304]{1,0:T(8,128)} %fusion.1, bf16[512,2304]{1,0:T(8,128)(2,1)} %pad_maximum_fusion.7, bf16[2304,1152]{1,0:T(8,128)(2,1)} %bitcast.218), kind=kOutput, calls=%fused_computation.28 | convolution fusion | flops 2732064768 | bytes 14745600 | tf_op jit(solution)/shard_map/dot_general | solution.py:20
  410.9 9.4 %fusion.2 = bf16[512,2304]{1,0:T(8,128)(2,1)S(1)} fusion(bf16[2304,1152]{1,0:T(8,128)(2,1)} %bitcast.213, bf16[2304,1152]{1,0:T(8,128)(2,1)} %bitcast.215, bf16[512,1152]{1,0:T(8,128)(2,1)S(1)} %get-tuple-element.115, bf16[512,1152]{1,0:T(8,128)(2,1)S(1)} %get-tuple-element.114), kind=kOutput, calls=%fused_computation.16 | convolution fusion | flops 5462949888 | bytes 15335424 | tf_op jit(solution)/shard_map/dot_general | solution.py:24
  434.0 11.8 %collective-permute-done.28 = bf16[64,2304]{1,0:T(8,128)(2,1)S(1)} collective-permute-done((bf16[64,2304]{1,0:T(8,128)(2,1)S(1)}, bf16[64,2304]{1,0:T(8,128)(2,1)S(1)}, u32[]{:S(2)}, u32[]{:S(2)}) %collective-permute-start.28) | collective-permute-done | bytes 294944 | tf_op jit(solution)/shard_map/ppermute | solution.py:114
  446.7 8.3 %convolution_convert_fusion = bf16[2304,2304]{1,0:T(8,128)(2,1)} fusion(bf16[512,2304]{1,0:T(8,128)(2,1)S(1)} %copy-done.43, bf16[512,2304]{1,0:T(8,128)(2,1)S(1)} %pad_maximum_fusion.8), kind=kOutput, calls=%fused_computation | convolution fusion | flops 5441126400 | bytes 15335424 | tf_op jit(solution)/shard_map/dot_general | solution.py:28
  455.0 9.1 %fusion.101 = (bf16[2304,1152]{1,0:T(8,128)(2,1)}, bf16[2304,1152]{1,0:T(8,128)(2,1)}) fusion(bf16[2304,2304]{1,0:T(8,128)(2,1)} %convolution_convert_fusion), kind=kLoop, calls=%fused_computation.250 | loop fusion | bytes 21233664 | tf_op jit(solution)/shard_map/slice | solution.py:375
  487.3 19.7 %collective-permute-done.31 = bf16[64,2304]{1,0:T(8,128)(2,1)S(1)} collective-permute-done((bf16[64,2304]{1,0:T(8,128)(2,1)S(1)}, bf16[64,2304]{1,0:T(8,128)(2,1)S(1)}, u32[]{:S(2)}, u32[]{:S(2)}) %collective-permute-start.31) | collective-permute-done | bytes 294944 | tf_op jit(solution)/shard_map/ppermute | solution.py:114
  521.3 19.4 %collective-permute-done.33 = bf16[4,64,2304]{2,1,0:T(8,128)(2,1)} collective-permute-done((bf16[4,64,2304]{2,1,0:T(8,128)(2,1)S(1)}, bf16[4,64,2304]{2,1,0:T(8,128)(2,1)}, u32[]{:S(2)}, u32[]{:S(2)}) %collective-permute-start.33) | collective-permute-done | bytes 1179680 | tf_op jit(solution)/shard_map/ppermute | solution.py:114
  548.9 6.8 collective-permute-start.34
  595.6 29.5 %collective-permute-done.35 = bf16[4,64,2304]{2,1,0:T(8,128)(2,1)} collective-permute-done((bf16[4,64,2304]{2,1,0:T(8,128)(2,1)}, bf16[4,64,2304]{2,1,0:T(8,128)(2,1)}, u32[]{:S(2)}, u32[]{:S(2)}) %collective-permute-start.35) | collective-permute-done | bytes 1179680 | tf_op jit(solution)/shard_map/ppermute | solution.py:114
  644.8 15.2 %collective-permute-done.37 = bf16[64,2304]{1,0:T(8,128)(2,1)S(1)} collective-permute-done((bf16[64,2304]{1,0:T(8,128)(2,1)S(1)}, bf16[64,2304]{1,0:T(8,128)(2,1)S(1)}, u32[]{:S(2)}, u32[]{:S(2)}) %collective-permute-start.37) | collective-permute-done | bytes 294944 | tf_op jit(solution)/shard_map/ppermute | solution.py:114
  660.9 8.7 %collective-permute-done.41 = bf16[8,144,512]{2,1,0:T(8,128)(2,1)S(1)} collective-permute-done((bf16[8,144,512]{2,1,0:T(8,128)(2,1)S(1)}, bf16[8,144,512]{2,1,0:T(8,128)(2,1)S(1)}, u32[]{:S(2)}, u32[]{:S(2)}) %collective-permute-start.41) | collective-permute-done | bytes 1179680 | tf_op jit(solution)/shard_map/ppermute | solution.py:114
  683.7 21.2 %all-to-all-done.6 = bf16[8,148,512]{2,1,0:T(8,128)(2,1)} async-done(((bf16[8,148,512]{2,1,0:T(8,128)(2,1)}), bf16[8,148,512]{2,1,0:T(8,128)(2,1)}, u32[]{:S(2)}, u32[]{:S(2)}) %all-to-all-start.6) | async-done | bytes 1212448 | tf_op jit(solution)/shard_map/all_to_all | solution.py:448
  731.7 10.6 %all-to-all-done.7 = bf16[4,144,1152]{2,1,0:T(8,128)(2,1)} async-done(((bf16[4,144,1152]{2,1,0:T(8,128)(2,1)}), bf16[4,144,1152]{2,1,0:T(8,128)(2,1)}, u32[]{:S(2)}, u32[]{:S(2)}) %all-to-all-start.7) | async-done | bytes 1327136 | tf_op jit(solution)/shard_map/all_to_all | solution.py:150
  (447 shorter events, 343.4 us)
Async XLA Ops:
  13.9 63.5 %all-to-all-start = ((bf16[8,146,512]{2,1,0:T(8,128)(2,1)}), bf16[8,146,512]{2,1,0:T(8,128)(2,1)S(1)}, u32[]{:S(2)}, u32[]{:S(2)}) async-start(bf16[8,146,512]{2,1,0:T(8,128)(2,1)} %pad_maximum_fusion.10), calls=%async_computation | async-start | bytes 2490368 | tf_op jit(solution)/shard_map/all_to_all | solution.py:236
  24.5 50.8 %collective-permute-start.2 = (bf16[64,2304]{1,0:T(8,128)(2,1)S(1)}, bf16[64,2304]{1,0:T(8,128)(2,1)S(1)}, u32[]{:S(2)}, u32[]{:S(2)}) collective-permute-start(bf16[64,2304]{1,0:T(8,128)(2,1)S(1)} %bitcast.209), channel_id=1, source_target_pairs={{0,8},{2,10},{4,12},{6,14},{8,0},{10,2},{12,4},{14,6},{16,24},{18,... | collective-permute-start | bytes 884744 | tf_op jit(solution)/shard_map/ppermute | solution.py:114
  24.5 50.8 %collective-permute-start.1 = (bf16[64,2304]{1,0:T(8,128)(2,1)S(1)}, bf16[64,2304]{1,0:T(8,128)(2,1)}, u32[]{:S(2)}, u32[]{:S(2)}) collective-permute-start(bf16[64,2304]{1,0:T(8,128)(2,1)S(1)} %bitcast.210), channel_id=1, source_target_pairs={{0,4},{2,6},{4,8},{6,10},{8,12},{10,14},{12,0},{14,2},{16,20},{18,... | collective-permute-start | bytes 884744 | tf_op jit(solution)/shard_map/ppermute | solution.py:114
  78.7 34.7 %all-to-all-start.1 = ((bf16[4,144,1152]{2,1,0:T(8,128)(2,1)}), bf16[4,144,1152]{2,1,0:T(8,128)(2,1)S(1)}, u32[]{:S(2)}, u32[]{:S(2)}) async-start(bf16[4,144,1152]{2,1,0:T(8,128)(2,1)} %copy.125), calls=%async_computation.1 | async-start | bytes 2654208 | tf_op jit(solution)/shard_map/all_to_all | solution.py:150
  82.2 193.1 %all-gather.7.cloned.1.call-start = ((), (), s32[]{:S(2)}) async-start(), calls=%async_computation.14 | async-start | bytes 6635520 | tf_op jit(solution)/shard_map/all_gather | solution.py:160
  135.4 35.7 %all-to-all-start.2 = ((bf16[4,144,1152]{2,1,0:T(8,128)(2,1)}), bf16[4,144,1152]{2,1,0:T(8,128)(2,1)}, u32[]{:S(2)}, u32[]{:S(2)}) async-start(bf16[4,144,1152]{2,1,0:T(8,128)(2,1)} %copy.131), calls=%async_computation.2 | async-start | bytes 2654208 | tf_op jit(solution)/shard_map/all_to_all | solution.py:150
  139.7 135.6 %all-gather.9.cloned.1.call-start = ((), (), s32[]{:S(2)}) async-start(), calls=%async_computation.15 | async-start | bytes 6635520 | tf_op jit(solution)/shard_map/all_gather | solution.py:160
  174.1 36.2 %collective-permute-start.9 = (bf16[4,64,2304]{2,1,0:T(8,128)(2,1)}, bf16[4,64,2304]{2,1,0:T(8,128)(2,1)}, u32[]{:S(2)}, u32[]{:S(2)}) collective-permute-start(bf16[4,64,2304]{2,1,0:T(8,128)(2,1)} %bitcast.20), channel_id=1, source_target_pairs={{0,2},{2,0},{4,6},{6,4},{8,10},{10,8},{12,14},{14,12},{16,18},{18,... | collective-permute-start | bytes 3538952 | tf_op jit(solution)/shard_map/ppermute | solution.py:114
  176.3 60.4 %all-to-all-start.3 = ((bf16[4,144,1152]{2,1,0:T(8,128)(2,1)}), bf16[4,144,1152]{2,1,0:T(8,128)(2,1)}, u32[]{:S(2)}, u32[]{:S(2)}) async-start(bf16[4,144,1152]{2,1,0:T(8,128)(2,1)} %copy.132), calls=%async_computation.3 | async-start | bytes 2654208 | tf_op jit(solution)/shard_map/all_to_all | solution.py:150
  180.6 135.4 %all-gather.11.cloned.1.call-start = ((), (), s32[]{:S(2)}) async-start(), calls=%async_computation.16 | async-start | bytes 6635520 | tf_op jit(solution)/shard_map/all_gather | solution.py:160
  236.7 270.5 %reduce-scatter.6.cloned.1.call-start = ((), (), s32[]{:S(2)}) async-start(), calls=%async_computation.12 | async-start | bytes 6635520 | tf_op jit(solution)/shard_map/reduce_scatter | solution.py:170
  245.8 28.4 %collective-permute-start.14 = (bf16[64,2304]{1,0:T(8,128)(2,1)S(1)}, bf16[64,2304]{1,0:T(8,128)(2,1)S(1)}, u32[]{:S(2)}, u32[]{:S(2)}) collective-permute-start(bf16[64,2304]{1,0:T(8,128)(2,1)S(1)} %multiply_convert_fusion.7), channel_id=1, source_target_pairs={{0,8},{2,10},{4,12},{6,14},{8,0},{10,2},{12,4},{14,6},{16,24},{18,... | collective-permute-start | bytes 884744 | tf_op jit(solution)/shard_map/ppermute | solution.py:114
  363.0 26.6 %collective-permute-start.23 = (bf16[64,2304]{1,0:T(8,128)(2,1)S(1)}, bf16[64,2304]{1,0:T(8,128)(2,1)S(1)}, u32[]{:S(2)}, u32[]{:S(2)}) collective-permute-start(bf16[64,2304]{1,0:T(8,128)(2,1)S(1)} %get-tuple-element.152), channel_id=1, source_target_pairs={{0,8},{2,10},{4,12},{6,14},{8,0},{10,2},{12,4},{14,6},{16,24},{18,... | collective-permute-start | bytes 884744 | tf_op jit(solution)/shard_map/ppermute | solution.py:114
  401.5 157.7 %reduce-scatter.4.cloned.1.call-start = ((), (), s32[]{:S(2)}) async-start(), calls=%async_computation.11 | async-start | bytes 6635520 | tf_op jit(solution)/shard_map/reduce_scatter | solution.py:170
  480.3 26.7 %collective-permute-start.31 = (bf16[64,2304]{1,0:T(8,128)(2,1)S(1)}, bf16[64,2304]{1,0:T(8,128)(2,1)S(1)}, u32[]{:S(2)}, u32[]{:S(2)}) collective-permute-start(bf16[64,2304]{1,0:T(8,128)(2,1)S(1)} %multiply_convert_fusion.5), channel_id=1, source_target_pairs={{0,8},{2,10},{4,12},{6,14},{8,0},{10,2},{12,4},{14,6},{16,24},{18,... | collective-permute-start | bytes 884744 | tf_op jit(solution)/shard_map/ppermute | solution.py:114
  507.2 33.5 %collective-permute-start.33 = (bf16[4,64,2304]{2,1,0:T(8,128)(2,1)S(1)}, bf16[4,64,2304]{2,1,0:T(8,128)(2,1)}, u32[]{:S(2)}, u32[]{:S(2)}) collective-permute-start(bf16[4,64,2304]{2,1,0:T(8,128)(2,1)S(1)} %pad_maximum_fusion.15), channel_id=1, source_target_pairs={{0,2},{2,0},{4,6},{6,4},{8,10},{10,8},{12,14},{14,12},{16,18},{18,... | collective-permute-start | bytes 3538952 | tf_op jit(solution)/shard_map/ppermute | solution.py:114
  516.7 57.3 %all-to-all-start.4 = ((bf16[4,144,1152]{2,1,0:T(8,128)(2,1)}), bf16[4,144,1152]{2,1,0:T(8,128)(2,1)}, u32[]{:S(2)}, u32[]{:S(2)}) async-start(bf16[4,144,1152]{2,1,0:T(8,128)(2,1)} %bitcast.243), calls=%async_computation.6 | async-start | bytes 2654208 | tf_op jit(solution)/shard_map/all_to_all | solution.py:150
  521.0 183.8 %reduce-scatter.8.cloned.1.call-start = ((), (), s32[]{:S(2)}) async-start(), calls=%async_computation.13 | async-start | bytes 6635520 | tf_op jit(solution)/shard_map/reduce_scatter | solution.py:170
  576.5 48.6 %collective-permute-start.35 = (bf16[4,64,2304]{2,1,0:T(8,128)(2,1)}, bf16[4,64,2304]{2,1,0:T(8,128)(2,1)}, u32[]{:S(2)}, u32[]{:S(2)}) collective-permute-start(bf16[4,64,2304]{2,1,0:T(8,128)(2,1)} %slice_bitcast_fusion.1), channel_id=1, source_target_pairs={{0,2},{2,0},{4,6},{6,4},{8,10},{10,8},{12,14},{14,12},{16,18},{18,... | collective-permute-start | bytes 3538952 | tf_op jit(solution)/shard_map/ppermute | solution.py:114
  578.6 49.8 %all-to-all-start.5 = ((bf16[4,144,1152]{2,1,0:T(8,128)(2,1)}), bf16[4,144,1152]{2,1,0:T(8,128)(2,1)}, u32[]{:S(2)}, u32[]{:S(2)}) async-start(bf16[4,144,1152]{2,1,0:T(8,128)(2,1)} %bitcast.244), calls=%async_computation.7 | async-start | bytes 2654208 | tf_op jit(solution)/shard_map/all_to_all | solution.py:150
  589.5 41.4 %collective-permute-start.40 = (bf16[2304,512]{1,0:T(8,128)(2,1)}, bf16[2304,512]{1,0:T(8,128)(2,1)}, u32[]{:S(2)}, u32[]{:S(2)}) collective-permute-start(bf16[2304,512]{1,0:T(8,128)(2,1)} %get-tuple-element.171), channel_id=1, source_target_pairs={{0,1},{1,0},{2,3},{3,2},{4,5},{5,4},{6,7},{7,6},{8,9},{9,8},{10,11... | collective-permute-start | bytes 7077896 | tf_op jit(solution)/shard_map/ppermute | solution.py:131
  635.2 34.5 %collective-permute-start.41 = (bf16[8,144,512]{2,1,0:T(8,128)(2,1)S(1)}, bf16[8,144,512]{2,1,0:T(8,128)(2,1)S(1)}, u32[]{:S(2)}, u32[]{:S(2)}) collective-permute-start(bf16[8,144,512]{2,1,0:T(8,128)(2,1)S(1)} %dynamic-slice_bitcast_fusion), channel_id=1, source_target_pairs={{0,16},{2,18},{4,20},{6,22},{8,24},{10,26},{12,28},{14,30},{16,0},... | collective-permute-start | bytes 3538952 | tf_op jit(solution)/shard_map/ppermute | solution.py:114
  671.2 33.6 %all-to-all-start.6 = ((bf16[8,148,512]{2,1,0:T(8,128)(2,1)}), bf16[8,148,512]{2,1,0:T(8,128)(2,1)}, u32[]{:S(2)}, u32[]{:S(2)}) async-start(bf16[8,148,512]{2,1,0:T(8,128)(2,1)} %pad_maximum_fusion.11), calls=%async_computation.8 | async-start | bytes 2490368 | tf_op jit(solution)/shard_map/all_to_all | solution.py:448
  706.5 35.8 %all-to-all-start.7 = ((bf16[4,144,1152]{2,1,0:T(8,128)(2,1)}), bf16[4,144,1152]{2,1,0:T(8,128)(2,1)}, u32[]{:S(2)}, u32[]{:S(2)}) async-start(bf16[4,144,1152]{2,1,0:T(8,128)(2,1)} %bitcast.242), calls=%async_computation.10 | async-start | bytes 2654208 | tf_op jit(solution)/shard_map/all_to_all | solution.py:150
  (114 other events, 1158.7 us)
Sparse Core Ops, SparseCore 0:
  114.6 61.8 all-gather.6
  178.3 73.7 all-gather.8
  254.0 61.9 all-gather.10
  401.6 59.1 reduce-scatter.5
  469.6 81.8 reduce-scatter.3
  564.7 87.9 reduce-scatter.7

commit v3 on v2

v3 whole, which is shorter than its diff:
```python
import jax
import jax.numpy as jnp
from jax import lax
from jax.experimental import pallas as pl
from jax.experimental.pallas import tpu as pltpu
from jax.sharding import PartitionSpec as P

HEAD_DIM = 256
LANES = 128
LANES = 128

epsilon = 1e-06
softcap = 50.0
theta = 10000.0
floor_value = -1e30
low = jnp.bfloat16
wide = jnp.float32
chip_axes = ("dp", "context")
all_axes = ("dp", "context", "tensor")


def product(left_side, right_side):
    return jnp.dot(left_side, right_side, preferred_element_type=wide)


def product_right_t(left_side, right_side):
    return lax.dot_general(left_side, right_side, (((1,), (1,)), ((), ())), preferred_element_type=wide)


def product_left_t(left_side, right_side):
    return lax.dot_general(left_side, right_side, (((0,), (0,)), ((), ())), preferred_element_type=wide)


def inverse_size(values):
    return lax.rsqrt(jnp.mean(values * values, axis=-1, keepdims=True) + epsilon)


def norm_back(unit, inverse, scaling, upstream):
    inner = upstream * scaling
    return inverse * (inner - unit * jnp.mean(inner * unit, axis=-1, keepdims=True))


def turn(values, cosine, sine_part):
    half_width = values.shape[-1] // 2
    former = values[..., :half_width]
    latter = values[..., half_width:]
    return jnp.concatenate(
        [former * cosine - latter * sine_part, latter * cosine + former * sine_part], axis=-1
    )


def geglu(gate_in, upward):
    return jax.nn.gelu(gate_in, approximate=True) * upward


def pick(array, at, axis):
    return lax.dynamic_index_in_dim(array, at, axis, keepdims=False)


def hold(*trees):
    return lax.optimization_barrier(trees)


def assembled(place, ranks, rows, upper, lower, others):
    count, units = len(others), others[0].shape[3]
    parts = upper.shape[3], lower.shape[3]

    def kernel(place_ref, upper_ref, lower_ref, *refs):
        out, own = refs[-1], place_ref[2]
        for at in range(count):
            begin = at * units
            out[0, own, 0, :, begin : begin + parts[0]] = upper_ref[0, at]
            out[0, own, 0, :, begin + parts[0] : begin + units] = lower_ref[0, at]
            for step in range(1, ranks):
                out[0, (own + step) % ranks, 0, :, begin : begin + units] = refs[at][0, step - 1]

    def relative(line, side, place):
        return ((line ^ place[0]) * 2 + (side ^ place[1]), 0, 0, 0)

    whole = pl.pallas_call(
        kernel,
        grid_spec=pltpu.PrefetchScalarGridSpec(
            num_scalar_prefetch=1,
            grid=(2, 2),
            in_specs=[
                pl.BlockSpec((1, count, rows, parts[0]), relative),
                pl.BlockSpec((1, count, rows, parts[1]), relative),
            ]
            + [
                pl.BlockSpec(
                    (1, ranks - 1, rows, units), lambda line, side, place: (line * 2 + side, 0, 0, 0)
                )
            ]
            * count,
            out_specs=pl.BlockSpec(
                (1, ranks, 1, rows, count * units), lambda line, side, place: (line, 0, side, 0, 0)
            ),
        ),
        out_shape=jax.ShapeDtypeStruct((2, ranks, 2, rows, count * units), low),
        compiler_params=pltpu.CompilerParams(vmem_limit_bytes=32 * 2**20),
        cost_estimate=pl.CostEstimate(
            flops=0, transcendentals=0, bytes_accessed=16 * ranks * rows * count * units
        ),
    )(place, upper, lower, *others)
    return whole.reshape(-1, count * units)


class Slice:
    def __init__(self):
        self.dp = lax.axis_size("dp")
        self.context = lax.axis_size("context")
        self.ranks = self.context // 2
        self.chips = self.dp * self.context
        self.core = lax.axis_index("tensor")
        self.place = lax.axis_index("context")
        self.rank = self.place // 2
        self.side = self.place % 2
        self.line = lax.axis_index("dp")

    def send(self, block, where):
        pairs = []
        for dp in range(self.dp):
            for rank in range(self.ranks):
                for side in range(2):
                    pairs.append(
                        (self.index(dp, rank, side), self.index(*where(dp, rank, side)))
                    )
        return lax.ppermute(block, chip_axes, pairs)

    def index(self, dp, rank, side):
        return (dp * self.ranks + rank % self.ranks) * 2 + side

    def across(self, block):
        return self.send(block, lambda dp, rank, side: (dp, rank, 1 - side))

    def over(self, block):
        return self.send(block, lambda dp, rank, side: (1 - dp, rank, side))

    def along(self, block, step):
        if step % self.ranks == 0:
            return block
        return self.send(block, lambda dp, rank, side: (dp, rank + step, side))

    def swap(self, block):
        return lax.ppermute(block, "tensor", [(0, 1), (1, 0)])

    def ordered(self, mine, other):
        first = self.core == 0
        return jnp.where(first, mine, other), jnp.where(first, other, mine)

    def moves(self, block):
        return [self.along(block, step) for step in range(self.ranks)]

    def returned(self, blocks):
        total = 0.0
        for step, block in enumerate(blocks):
            if step:
                block = self.along(block.astype(low), -step)
            total = total + block.astype(wide)
        return total

    def to_ranks(self, array):
        groups = [[rank * 2 + side for rank in range(self.ranks)] for side in range(2)]
        return lax.all_to_all(array, "context", 0, 0, tiled=True, axis_index_groups=groups)

    def square(self):
        return [
            [self.index(dp, rank, side) for dp in range(self.dp) for side in range(2)]
            for rank in range(self.ranks)
        ]

    def square_cores(self):
        return [[2 * chip + core for chip in chips for core in range(2)] for chips in self.square()]

    def heads_in(self, array):
        whole = lax.all_gather(
            array, all_axes, axis=0, tiled=False, axis_index_groups=self.square_cores()
        )
        return whole.reshape((self.dp, 2, 2) + array.shape)

    def heads_by_square(self, grads, rows):
        lanes = grads[0].shape[1]
        parts = [g.astype(low).reshape(self.dp, self.ranks, 2, rows, lanes) for g in grads]
        parts = [jnp.transpose(part, (0, 2, 1, 3, 4)) for part in parts]
        return jnp.stack(parts, axis=2).reshape(-1, lanes)

    def head_grads_out(self, parts, rows):
        total = lax.psum_scatter(
            parts,
            all_axes,
            scatter_dimension=0,
            tiled=True,
            axis_index_groups=self.square_cores(),
        )
        return total.reshape(self.ranks, rows, -1)

    def weights_in(self, array):
        ranks, rows, units = array.shape
        whole = lax.all_gather(array, chip_axes, axis=0, tiled=False, axis_index_groups=self.square())
        return whole.reshape(self.dp, 2, ranks, rows, units)

    def others_in(self, array):
        ranks = array.shape[0]
        around = jnp.concatenate([array, array[: ranks - 1]])
        around = lax.dynamic_slice_in_dim(around, self.rank + 1, ranks - 1, 0)
        return lax.all_gather(
            around, chip_axes, axis=0, tiled=False, axis_index_groups=self.square()
        )

    def by_model_row(self, whole):
        return jnp.transpose(whole, (0, 2, 1, 3, 4)).reshape(-1, whole.shape[-1])

    def by_square(self, grad, rows):
        parts = grad.astype(low).reshape(self.dp, self.ranks, 2, rows, -1)
        return jnp.transpose(parts, (0, 2, 1, 3, 4)).reshape(-1, grad.shape[1])

    def grads_out(self, parts, rows):
        total = lax.psum_scatter(
            parts, chip_axes, scatter_dimension=0, tiled=True, axis_index_groups=self.square()
        )
        return total.reshape(self.ranks, rows, -1)


def body(
    tokens,
    w_query,
    w_key,
    w_value,
    w_out,
    w_gate,
    w_up,
    w_down,
    gain_attn_in,
    gain_attn_out,
    gain_ffw_in,
    gain_ffw_out,
    cotangent,
):
    net = Slice()
    core, chips, ranks = net.core, net.chips, net.ranks
    span = tokens.shape[1]
    width = tokens.shape[2]
    half = span // 2
    rows = w_query.shape[0]
    heads = 2 * w_query.shape[1] // HEAD_DIM
    kv_heads = 2 * w_key.shape[1] // HEAD_DIM
    repeat = heads // kv_heads
    share = ranks // kv_heads
    score_scale = HEAD_DIM ** (-0.5)
    units = w_gate.shape[1] // ranks
    q_cols, k_cols = w_query.shape[1], w_key.shape[1]
    is_front = core == 0

    own_tokens = lax.dynamic_slice_in_dim(tokens[0], core * half, half, 0)
    upstream = lax.dynamic_slice_in_dim(cotangent[0], core * half, half, 0)

    front = jnp.concatenate([w_query, w_key], axis=1)
    back = jnp.concatenate([w_out, w_value], axis=1)
    mine = jnp.where(is_front, front, back)
    theirs = net.swap(jnp.where(is_front, back, front))
    low_heads, high_heads = net.ordered(mine, theirs)

    def by_group(begin, end):
        both = jnp.concatenate([low_heads[:, begin:end], high_heads[:, begin:end]], axis=1)
        return jnp.transpose(both.reshape(rows, kv_heads, -1), (1, 0, 2))

    lanes = (repeat + 1) * HEAD_DIM
    gain_row = jnp.concatenate([gain_attn_in, gain_attn_out, gain_ffw_in, gain_ffw_out])
    gain_row = jnp.pad(gain_row, (0, lanes - 4 * rows))
    head_sets = jnp.concatenate([by_group(0, q_cols), by_group(q_cols, q_cols + k_cols)], axis=2)
    head_sets = jnp.concatenate(
        [head_sets, jnp.broadcast_to(gain_row, (kv_heads, 1, lanes))], axis=1
    )
    part = net.to_ranks(jnp.repeat(head_sets, share, axis=0))

    def by_rank(w):
        return jnp.transpose(w.reshape(rows, ranks, units), (1, 0, 2))

    gate_set, up_set, down_set = by_rank(w_gate), by_rank(w_up), by_rank(w_down)
    token_blocks = jnp.stack(net.moves(own_tokens))

    by_parts = rows % 16 == 0 and units % LANES == 0
    if by_parts:
        own_units = jnp.stack(
            [lax.dynamic_slice_in_dim(w, net.rank * units, units, 1) for w in (w_gate, w_up, w_down)]
        )
        middle_lane = (units // LANES + 1) // 2 * LANES
        upper, lower = own_units[:, :, :middle_lane], own_units[:, :, middle_lane:]
        upper = jnp.stack([upper, net.across(upper)])
        lower = jnp.stack([lower, net.over(lower)])
        part, token_blocks, upper, lower, gate_set, up_set, down_set = hold(
            part, token_blocks, upper, lower, gate_set, up_set, down_set
        )
        upper = jnp.concatenate([upper, net.over(upper)])
        lower_side = net.across(lower)
        lower = jnp.stack([lower[0], lower_side[0], lower[1], lower_side[1]])
        place = jnp.stack([net.line, net.side, net.rank]).astype(jnp.int32)
    else:
        part, token_blocks, gate_set, up_set, down_set = hold(
            part, token_blocks, gate_set, up_set, down_set
        )
    weights_in = net.others_in if by_parts else net.weights_in

    gate_set = net.to_ranks(gate_set)
    head_all = net.heads_in(part)
    gate_units = weights_in(gate_set)
    gate_set, up_set = hold(gate_set, up_set)
    up_set = net.to_ranks(up_set)
    up_units = weights_in(up_set)
    up_set, down_set = hold(up_set, down_set)
    down_set = net.to_ranks(down_set)
    down_units = weights_in(down_set)

    own_inputs = own_tokens.astype(wide)
    block_places = (net.rank - jnp.arange(ranks)) % ranks * 2 * span
    offsets = jnp.arange(half, dtype=jnp.int32)
    line_places = (block_places[:, None] + offsets[None, :]).reshape(-1)
    places = line_places + net.side * span + core * half
    key_places = jnp.concatenate(
        [
            line_places + side * span + of * half
            for side in (net.side, 1 - net.side)
            for of in (core, 1 - core)
        ]
    )
    exponent = jnp.arange(HEAD_DIM // 2, dtype=wide) * (-2.0 / HEAD_DIM)
    angles = places.astype(wide)[:, None] * (theta**exponent)[None, :]
    cosine, sine_part = jnp.cos(angles), jnp.sin(angles)
    asked = tuple(range(0, ranks, share))

    def asked_rows(array):
        if share == 1:
            return array
        blocks = array.reshape((ranks, half) + array.shape[1:])
        return jnp.concatenate([blocks[step] for step in asked])

    def by_head(array):
        return jnp.concatenate(jnp.split(array, repeat, axis=1))

    def by_token(array):
        return jnp.concatenate(jnp.split(array, repeat), axis=1)

    cosine_heads = jnp.concatenate([asked_rows(cosine)] * repeat)
    sine_heads = jnp.concatenate([asked_rows(sine_part)] * repeat)
    head_cols = repeat * HEAD_DIM

    def attend(head_all, token_blocks):
        front_weights = net.by_model_row(head_all[:, :, 0, :, :rows])
        back_weights = net.by_model_row(head_all[:, :, 1, :, :rows])
        gains = jnp.transpose(head_all[:, :, 0, :, rows, : 4 * rows], (0, 2, 1, 3))
        gains = jnp.transpose(gains.reshape(chips, 4, rows), (1, 0, 2)).reshape(4, width).astype(wide)
        inputs = token_blocks.reshape(-1, width).astype(wide)
        normed_low = (inputs * inverse_size(inputs) * gains[0]).astype(low)
        query_key = product(normed_low, front_weights)
        queries = turn(by_head(asked_rows(query_key[:, :head_cols])), cosine_heads, sine_heads)
        queries = queries.astype(low)
        keys = turn(query_key[:, head_cols:], cosine, sine_part).astype(low)
        values = product(normed_low, back_weights[:, head_cols:]).astype(low)
        own_kv = jnp.concatenate([keys, values], axis=1)
        side_kv = jnp.stack([own_kv, net.swap(own_kv)])
        all_kv = jnp.concatenate([side_kv, net.across(side_kv)]).reshape(-1, 2 * HEAD_DIM)
        allowed = key_places[None, :] <= jnp.concatenate([asked_rows(places)] * repeat)[:, None]
        scores = product_right_t(queries, all_kv[:, :HEAD_DIM]) * score_scale
        bent = jnp.tanh(scores / softcap)
        capped = jnp.where(allowed, softcap * bent, floor_value)
        shifted = jnp.exp(capped - jnp.max(capped, axis=-1, keepdims=True))
        probabilities = shifted / jnp.sum(shifted, axis=-1, keepdims=True)
        mixed = product(probabilities.astype(low), all_kv[:, HEAD_DIM:])
        mixed_low = by_token(mixed.astype(low))
        out_parts = product_right_t(mixed_low, back_weights[:, :head_cols]).astype(low)
        return (
            front_weights,
            back_weights,
            gains,
            normed_low,
            queries,
            all_kv,
            probabilities,
            bent,
            mixed_low,
            out_parts,
        )

    (
        front_weights,
        back_weights,
        gains,
        normed_low,
        queries,
        all_kv,
        probabilities,
        bent,
        mixed_low,
        out_parts,
    ) = attend(head_all, token_blocks)
    scale_in, scale_mid, scale_pre, scale_out = gains[0], gains[1], gains[2], gains[3]
    w_out_head = back_weights[:, :head_cols]
    w_value_head = back_weights[:, head_cols:]
    all_keys, all_values = all_kv[:, :HEAD_DIM], all_kv[:, HEAD_DIM:]
    probabilities_low = probabilities.astype(low)
    inputs = token_blocks.reshape(-1, width).astype(wide)
    units_in = inputs * inverse_size(inputs)
    out_parts = out_parts.reshape(len(asked), half, width).astype(wide)
    projected = 0.0
    for at, step in enumerate(asked):
        block = out_parts[at]
        if step:
            block = net.along(block.astype(low), -step).astype(wide)
        projected = projected + block


    inverse_mid = inverse_size(projected)
    unit_mid = projected * inverse_mid
    middle = own_inputs + unit_mid * scale_mid
    inverse_pre = inverse_size(middle)
    unit_pre = middle * inverse_pre
    normed_two_low = (unit_pre * scale_pre).astype(low)
    two_blocks = jnp.stack(net.moves(normed_two_low)).reshape(-1, width)
    two_blocks, gate_units, up_units = hold(two_blocks, gate_units, up_units)
    if by_parts:
        pair_units = assembled(place, ranks, rows, upper[:, :2], lower[:, :2], [gate_units, up_units])
    else:
        pair_units = jnp.concatenate(
            [net.by_model_row(gate_units), net.by_model_row(up_units)], axis=1
        )

    all_two = jnp.concatenate([two_blocks, net.swap(two_blocks)])
    pair = product(all_two, pair_units)
    gate_in, upward = pair[:, :units], pair[:, units:]
    hidden_low = geglu(gate_in, upward).astype(low)
    hidden_low, down_units = hold(hidden_low, down_units)
    if by_parts:
        down_units = assembled(place, ranks, rows, upper[:, 2:], lower[:, 2:], [down_units])
    else:
        down_units = net.by_model_row(down_units)

    def core_total(part):
        count = ranks * half
        part = part.astype(low)
        return part[:count].astype(wide) + net.swap(part[count:]).astype(wide)

    def line_total(own):
        return net.returned(list(own.reshape(ranks, half, width)))

    branch = line_total(core_total(product_right_t(hidden_low, down_units)))
    inverse_out = inverse_size(branch)
    unit_out = branch * inverse_out
    own_output = (middle + unit_out * scale_out).astype(low)

    grad_ffw_out = jnp.sum(upstream * unit_out, axis=0)
    d_branch_low = norm_back(unit_out, inverse_out, scale_out, upstream).astype(low)
    branch_blocks = jnp.stack(net.moves(d_branch_low)).reshape(-1, width)
    all_branch = jnp.concatenate([branch_blocks, net.swap(branch_blocks)])

    down_grad = net.by_square(product_left_t(all_branch, hidden_low), rows)
    down_grad, all_branch = hold(down_grad, all_branch)
    down_grad = net.grads_out(down_grad, rows)
    d_hidden = product(all_branch, down_units)
    _, pull = jax.vjp(geglu, gate_in, upward)
    d_gate, d_up = pull(d_hidden)
    d_pair_low = jnp.concatenate([d_gate.astype(low), d_up.astype(low)], axis=1)
    d_two = core_total(product_right_t(d_pair_low, pair_units))
    d_normed_two = line_total(d_two)
    pair_grad = net.by_square(product_left_t(all_two, d_pair_low), rows)
    d_normed_two, pair_grad = hold(d_normed_two, pair_grad)
    pair_grad = net.grads_out(pair_grad, rows)
    grad_ffw_in = jnp.sum(d_normed_two * unit_pre, axis=0)
    d_middle = upstream + norm_back(unit_pre, inverse_pre, scale_pre, d_normed_two)
    grad_attn_out = jnp.sum(d_middle * unit_mid, axis=0)
    d_projected_low = norm_back(unit_mid, inverse_mid, scale_mid, d_middle).astype(low)
    d_projected_all = jnp.stack(net.moves(d_projected_low))
    d_projected_all, down_grad = hold(d_projected_all, down_grad)
    down_grad = net.to_ranks(down_grad)
    d_projected_asked = asked_rows(d_projected_all.reshape(-1, width))
    d_mixed_low = by_head(product(d_projected_asked, w_out_head).astype(low))
    d_prob = product_right_t(d_mixed_low, all_values)
    delta = jnp.sum(probabilities * d_prob, axis=-1, keepdims=True)
    d_capped = probabilities * (d_prob - delta)
    d_scores = (d_capped * (1.0 - bent * bent)).astype(low)
    d_queries = product(d_scores, all_keys) * score_scale
    d_keys = product_left_t(d_scores, queries) * score_scale
    d_values = product_left_t(probabilities_low, d_mixed_low)
    d_kv = jnp.concatenate([d_keys, d_values], axis=1)
    d_kv = d_kv.reshape(2, 2, ranks * half, 2 * HEAD_DIM)
    d_kv = d_kv[0] + net.across(d_kv[1].astype(low)).astype(wide)
    d_kv = d_kv[0] + net.swap(d_kv[1].astype(low)).astype(wide)
    d_query_low = by_token(turn(d_queries, cosine_heads, -sine_heads).astype(low))
    d_key_low = turn(d_kv[:, :HEAD_DIM], cosine, -sine_part).astype(low)
    if share != 1:
        blocks = jnp.zeros((ranks, half, repeat * HEAD_DIM), low)
        d_query_low = blocks.at[jnp.array(asked)].set(
            d_query_low.reshape(len(asked), half, repeat * HEAD_DIM)
        )
        d_query_low = d_query_low.reshape(-1, repeat * HEAD_DIM)
    d_value_low = d_kv[:, HEAD_DIM:].astype(low)
    d_front_low = jnp.concatenate([d_query_low, d_key_low], axis=1)
    d_normed_part = product_right_t(d_front_low, front_weights)
    d_normed_part = d_normed_part + product_right_t(d_value_low, w_value_head)
    grad_attn_in = jnp.sum(d_normed_part * units_in, axis=0)
    d_normed_low = d_normed_part.astype(low).reshape(ranks, half, width)
    down_grad, d_normed_low, d_front_low, d_value_low = hold(
        down_grad, d_normed_low, d_front_low, d_value_low
    )
    d_normed = net.returned(list(d_normed_low))
    front_grads = product_left_t(normed_low, d_front_low)
    back_grads = jnp.concatenate(
        [
            product_left_t(d_projected_asked, mixed_low),
            product_left_t(normed_low, d_value_low),
        ],
        axis=1,
    )
    head_grads = net.heads_by_square([front_grads, back_grads], rows)
    d_normed, pair_grad, head_grads = hold(d_normed, pair_grad, head_grads)
    head_grads = net.head_grads_out(head_grads, rows)
    pair_grad = net.to_ranks(pair_grad)
    gain_grads = jnp.stack([grad_attn_in, grad_attn_out, grad_ffw_in, grad_ffw_out])
    gain_grads = gain_grads + net.swap(gain_grads)
    gain_grads = jnp.transpose(gain_grads.reshape(4, net.dp, ranks, 2, rows), (1, 2, 3, 0, 4))
    gain_grads = pick(gain_grads, net.line, 0) + net.over(pick(gain_grads, 1 - net.line, 0))
    gain_grads = pick(gain_grads, net.side, 1) + net.across(pick(gain_grads, 1 - net.side, 1))
    gain_got = pick(gain_grads, net.rank, 0)
    for step in range(1, ranks):
        gain_got = gain_got + net.along(pick(gain_grads, (net.rank + step) % ranks, 0), step)
    own_inverse = inverse_size(own_inputs)
    own_grad = d_middle + norm_back(own_inputs * own_inverse, own_inverse, scale_in, d_normed)
    layer_output = jnp.concatenate(net.ordered(own_output, net.swap(own_output)))
    input_grad = jnp.concatenate(net.ordered(own_grad, net.swap(own_grad)))
    pair_grad, head_grads = hold(pair_grad, head_grads)
    got = net.to_ranks(head_grads)
    got = got.astype(wide).reshape(kv_heads, share, rows, lanes).sum(axis=1)
    got = jnp.transpose(got, (1, 0, 2)).reshape(rows, 2, kv_heads // 2, lanes)
    cut = repeat * HEAD_DIM
    total = jnp.concatenate(
        [got[..., :cut].reshape(rows, 2, -1), got[..., cut:].reshape(rows, 2, -1)], axis=2
    )
    kept = pick(total, core, 1)
    given = pick(total, 1 - core, 1)
    front, back = net.ordered(kept, net.swap(given.astype(low)).astype(wide))
    grad_query, grad_key = front[:, :q_cols], front[:, q_cols:]
    grad_out, grad_value = back[:, :q_cols], back[:, q_cols:]

    def by_units(pieces):
        return jnp.transpose(pieces, (1, 0, 2)).reshape(rows, ranks * units).astype(wide)

    return (
        layer_output[None],
        input_grad[None],
        grad_query,
        grad_key,
        grad_value,
        grad_out,
        by_units(pair_grad[:, :, :units]),
        by_units(pair_grad[:, :, units:]),
        by_units(down_grad),
        gain_got[0],
        gain_got[1],
        gain_got[2],
        gain_got[3],
    )


def solution(mesh):
    tokens_spec = P("dp", "context", None)
    weight_spec = P(("dp", "context"), "tensor")
    gain_spec = P(("dp", "context"))
    return jax.shard_map(
        body,
        mesh=mesh,
        in_specs=(tokens_spec,) + (weight_spec,) * 7 + (gain_spec,) * 4 + (tokens_spec,),
        out_specs=(tokens_spec,) * 2 + (weight_spec,) * 7 + (gain_spec,) * 4,
        check_vma=False,
    )
```

time: 764 us -> 671 us (0.88)
  waiting for transfers between devices: 388 us -> 320 us
  starting transfers between devices: 113 us -> 103 us
    ppermute x31 -> x35, waiting for transfers between devices: 300 us -> 187 us  [send(): return lax.ppermute(block, chip_axes, pairs)]
    all_to_all x6 -> x7, waiting for transfers between devices: 36.7 us -> 106 us  [to_ranks(): lax.all_to_all(array, 'context', 0, 0, tiled=True, axis_index_groups=groups)]
    all_to_all x2 -> x0, waiting for transfers between devices: 21.2 us -> none  [the longest x1 21.2 us: body(): got = lax.all_to_all(head_grads, 'context', 0, 0, tiled=True)]
    all_to_all x2 -> x0, starting transfers between devices: 11.6 us -> none  [the longest x1 6.66 us: body(): part = lax.all_to_all(head_sets, 'context', 0, 0, tiled=True)]
    all_gather x3 -> x4, waiting for transfers between devices: 20.9 us -> 11.5 us  [the longest x3 11.5 us: others_in(): lax.all_gather(around, chip_axes, axis=0, tiled=False, axis_index_groups=...]
    another operation x0 -> x7, local copies, waits for them, and re-layouts: none -> 8.85 us  [the longest x1 3.45 us: heads_by_square(): return jnp.stack(parts, axis=2).reshape(-1, lanes)]
    reshape x10 -> x7, local copies, waits for them, and re-layouts: 18.4 us -> 9.81 us  [the longest x2 7.43 us: by_square(): parts = grad.astype(low).reshape(self.dp, self.ranks, 2, rows, -1)]
    convert_element_type x7 -> x4, other arithmetic: 9.41 us -> 1.62 us  [the longest x1 0.95 us: attend(): jnp.transpose(gains.reshape(chips, 4, rows), (1, 0, 2)).reshape(4, width)]
  transfers between devices with their start and end apart: 59 -> 60, of which waited for: 32 -> 29; matrix products, arithmetic and copies ran while one was open for 25% -> 28% of each run, Pallas kernels for 0% -> 0%
where the time goes in v3:
time: 671 us; the launch traced here: 664 us
  waiting for transfers between devices  320 us (48%)
  starting transfers between devices  103 us (15%)
  local copies, waits for them, and re-layouts  97.4 us (15%)
  other arithmetic  63.2 us (9%)
  matrix products  60.1 us (9%)
  between operations  16.1 us (2%)
    ppermute x35, waiting for transfers between devices, send(): return lax.ppermute(block, chip_axes, pairs)  187 us
    all_to_all x7, waiting for transfers between devices, to_ranks(): lax.all_to_all(array, 'context', 0, 0, tiled=True, axis_index_groups=groups)  106 us
    ppermute x35, starting transfers between devices, send(): return lax.ppermute(block, chip_axes, pairs)  57.9 us
    all_to_all x7, starting transfers between devices, to_ranks(): lax.all_to_all(array, 'context', 0, 0, tiled=True, axis_index_groups=groups)  28.5 us
    dot_general x7, matrix products, product(): return jnp.dot(left_side, right_side, preferred_element_type=wide)  23.4 us
    dot_general x7, matrix products, product_right_t(): lax.dot_general(left_side, right_side, (((1,), (1,)), ((), ())), preferre...  22.4 us
    unnamed x188, local copies, waits for them, and re-layouts  20.1 us
    ppermute x11, starting transfers between devices, swap(): return lax.ppermute(block, 'tensor', [(0, 1), (1, 0)])  15.8 us
  transfers between devices with their start and end apart: 60, of which 29 were waited for; matrix products, arithmetic and copies ran while one was open for 28% of the time, Pallas kernels for 0%

profile of v3, /device:TPU:1, one launch (start us, length us, event | category | flops | bytes accessed | tf_op | source)
XLA Modules:
  0.0 663.8 jit_solution(13265552642906443541)
XLA Ops:
  48.8 8.9 %all-to-all-done = bf16[4,145,768]{2,1,0:T(8,128)(2,1)} async-done(((bf16[4,145,768]{2,1,0:T(8,128)(2,1)}), bf16[4,145,768]{2,1,0:T(8,128)(2,1)}, u32[]{:S(2)}, u32[]{:S(2)}) %all-to-all-start) | async-done | bytes 890912 | tf_op jit(solution)/shard_map/all_to_all | solution.py:164
  63.9 31.2 %all-to-all-done.1 = bf16[4,144,1152]{2,1,0:T(8,128)(2,1)S(1)} async-done(((bf16[4,144,1152]{2,1,0:T(8,128)(2,1)}), bf16[4,144,1152]{2,1,0:T(8,128)(2,1)S(1)}, u32[]{:S(2)}, u32[]{:S(2)}) %all-to-all-start.1) | async-done | bytes 1327136 | tf_op jit(solution)/shard_map/all_to_all | solution.py:164
  104.0 29.9 %all-to-all-done.2 = bf16[4,144,1152]{2,1,0:T(8,128)(2,1)S(1)} async-done(((bf16[4,144,1152]{2,1,0:T(8,128)(2,1)}), bf16[4,144,1152]{2,1,0:T(8,128)(2,1)S(1)}, u32[]{:S(2)}, u32[]{:S(2)}) %all-to-all-start.2) | async-done | bytes 1327136 | tf_op jit(solution)/shard_map/all_to_all | solution.py:164
  136.4 6.5 slice_bitcast_fusion.1
  191.1 19.6 %all-to-all-done.3 = bf16[4,144,1152]{2,1,0:T(8,128)(2,1)S(1)} async-done(((bf16[4,144,1152]{2,1,0:T(8,128)(2,1)}), bf16[4,144,1152]{2,1,0:T(8,128)(2,1)S(1)}, u32[]{:S(2)}, u32[]{:S(2)}) %all-to-all-start.3) | async-done | bytes 1327136 | tf_op jit(solution)/shard_map/all_to_all | solution.py:164
  219.1 7.2 %collective-permute-start.13 = (bf16[64,2304]{1,0:T(8,128)(2,1)S(1)}, bf16[64,2304]{1,0:T(8,128)(2,1)S(1)}, u32[]{:S(2)}, u32[]{:S(2)}) collective-permute-start(bf16[64,2304]{1,0:T(8,128)(2,1)S(1)} %multiply_convert_fusion.7), channel_id=1, source_target_pairs={{0,12},{2,14},{4,0},{6,2},{8,4},{10,6},{12,8},{14,10},{16,28},{18,... | collective-permute-start | bytes 884744 | tf_op jit(solution)/shard_map/ppermute | solution.py:128
  231.7 19.8 %collective-permute-done.12 = bf16[64,2304]{1,0:T(8,128)(2,1)S(1)} collective-permute-done((bf16[64,2304]{1,0:T(8,128)(2,1)S(1)}, bf16[64,2304]{1,0:T(8,128)(2,1)S(1)}, u32[]{:S(2)}, u32[]{:S(2)}) %collective-permute-start.12) | collective-permute-done | bytes 294944 | tf_op jit(solution)/shard_map/ppermute | solution.py:128
  277.0 11.5 %all-gather.15.cloned.1.call-done = bf16[12,144,1152]{2,1,0:T(8,128)(2,1)} async-done(((bf16[3,144,1152]{2,1,0:T(8,128)(2,1)}), bf16[12,144,1152]{2,1,0:T(8,128)(2,1)}) %all-gather.15.cloned.1.call-update) | async-done | bytes 3981328 | tf_op jit(solution)/shard_map/all_gather | solution.py:206
  306.1 5.7 collective-permute-done.20
  311.8 13.3 %collective-permute-done.19 = bf16[64,2304]{1,0:T(8,128)(2,1)S(1)} collective-permute-done((bf16[64,2304]{1,0:T(8,128)(2,1)}, bf16[64,2304]{1,0:T(8,128)(2,1)S(1)}, u32[]{:S(2)}, u32[]{:S(2)}) %collective-permute-start.19) | collective-permute-done | bytes 294944 | tf_op jit(solution)/shard_map/ppermute | solution.py:128
  328.3 6.8 %collective-permute-start.24 = (bf16[64,2304]{1,0:T(8,128)(2,1)S(1)}, bf16[64,2304]{1,0:T(8,128)(2,1)S(1)}, u32[]{:S(2)}, u32[]{:S(2)}) collective-permute-start(bf16[64,2304]{1,0:T(8,128)(2,1)S(1)} %get-tuple-element.134), channel_id=1, source_target_pairs={{0,12},{2,14},{4,0},{6,2},{8,4},{10,6},{12,8},{14,10},{16,28},{18,... | collective-permute-start | bytes 884744 | tf_op jit(solution)/shard_map/ppermute | solution.py:128
  342.0 19.8 %collective-permute-done.23 = bf16[64,2304]{1,0:T(8,128)(2,1)S(1)} collective-permute-done((bf16[64,2304]{1,0:T(8,128)(2,1)S(1)}, bf16[64,2304]{1,0:T(8,128)(2,1)S(1)}, u32[]{:S(2)}, u32[]{:S(2)}) %collective-permute-start.23) | collective-permute-done | bytes 294944 | tf_op jit(solution)/shard_map/ppermute | solution.py:128
  373.7 9.3 %fusion.6 = (bf16[512,1152]{1,0:T(8,128)(2,1)S(1)}, bf16[512,1152]{1,0:T(8,128)(2,1)S(1)}) fusion(f32[512,2304]{1,0:T(8,128)} %copy-done.30, bf16[512,2304]{1,0:T(8,128)(2,1)} %pad_maximum_fusion.1, bf16[2304,1152]{1,0:T(8,128)(2,1)} %bitcast.229), kind=kOutput, calls=%fused_computation.22 | convolution fusion | flops 2732064768 | bytes 14745600 | tf_op jit(solution)/shard_map/dot_general | solution.py:23
  383.0 10.7 %convolution_convert_fusion.4 = bf16[512,2304]{1,0:T(8,128)(2,1)S(1)} fusion(bf16[2304,2304]{1,0:T(8,128)(2,1)} %bitcast.227, bf16[512,1152]{1,0:T(8,128)(2,1)S(1)} %get-tuple-element.93, bf16[512,1152]{1,0:T(8,128)(2,1)S(1)} %get-tuple-element.92), kind=kOutput, calls=%fused_computation.5 | convolution fusion | flops 5441716224 | bytes 15335424 | tf_op jit(solution)/shard_map/dot_general | solution.py:27
  400.7 5.9 convolution_convert_fusion
  411.4 7.9 %collective-permute-done.28 = bf16[64,2304]{1,0:T(8,128)(2,1)S(1)} collective-permute-done((bf16[64,2304]{1,0:T(8,128)(2,1)S(1)}, bf16[64,2304]{1,0:T(8,128)(2,1)S(1)}, u32[]{:S(2)}, u32[]{:S(2)}) %collective-permute-start.28) | collective-permute-done | bytes 294944 | tf_op jit(solution)/shard_map/ppermute | solution.py:128
  425.3 6.4 collective-permute-start.32
  438.6 19.8 %collective-permute-done.31 = bf16[64,2304]{1,0:T(8,128)(2,1)} collective-permute-done((bf16[64,2304]{1,0:T(8,128)(2,1)}, bf16[64,2304]{1,0:T(8,128)(2,1)}, u32[]{:S(2)}, u32[]{:S(2)}) %collective-permute-start.31) | collective-permute-done | bytes 294944 | tf_op jit(solution)/shard_map/ppermute | solution.py:128
  485.3 20.0 %collective-permute-done.33 = bf16[2,256,512]{2,1,0:T(8,128)(2,1)S(1)} collective-permute-done((bf16[2,256,512]{2,1,0:T(8,128)(2,1)}, bf16[2,256,512]{2,1,0:T(8,128)(2,1)S(1)}, u32[]{:S(2)}, u32[]{:S(2)}) %collective-permute-start.33) | collective-permute-done | bytes 524320 | tf_op jit(solution)/shard_map/ppermute | solution.py:128
  533.6 9.3 %collective-permute-done.36 = bf16[64,2304]{1,0:T(8,128)(2,1)} collective-permute-done((bf16[64,2304]{1,0:T(8,128)(2,1)}, bf16[64,2304]{1,0:T(8,128)(2,1)}, u32[]{:S(2)}, u32[]{:S(2)}) %collective-permute-start.36) | collective-permute-done | bytes 294944 | tf_op jit(solution)/shard_map/ppermute | solution.py:128
  544.2 7.5 %reduce-scatter.6.cloned.1.call-done = bf16[576,2304]{1,0:T(8,128)(2,1)} async-done(((bf16[2304,2304]{1,0:T(8,128)(2,1)}), bf16[576,2304]{1,0:T(8,128)(2,1)}) %reduce-scatter.6.cloned.1.call-update) | async-done | bytes 2654224 | tf_op jit(solution)/shard_map/reduce_scatter | solution.py:218
  575.1 26.6 %collective-permute-done.45 = f32[4,144]{1,0:T(4,128)S(1)} collective-permute-done((f32[4,144]{1,0:T(4,128)S(1)}, f32[4,144]{1,0:T(4,128)S(1)}, u32[]{:S(2)}, u32[]{:S(2)}) %collective-permute-start.45) | collective-permute-done | bytes 2336 | tf_op jit(solution)/shard_map/ppermute | solution.py:128
  601.8 17.2 %collective-permute-done.44 = f32[4,144]{1,0:T(4,128)S(1)} collective-permute-done((f32[4,144]{1,0:T(4,128)S(1)}, f32[4,144]{1,0:T(4,128)S(1)}, u32[]{:S(2)}, u32[]{:S(2)}) %collective-permute-start.44) | collective-permute-done | bytes 2336 | tf_op jit(solution)/shard_map/ppermute | solution.py:128
  631.2 16.1 %all-to-all-done.6 = bf16[4,144,768]{2,1,0:T(8,128)(2,1)S(1)} async-done(((bf16[4,144,768]{2,1,0:T(8,128)(2,1)}), bf16[4,144,768]{2,1,0:T(8,128)(2,1)S(1)}, u32[]{:S(2)}, u32[]{:S(2)}) %all-to-all-start.6) | async-done | bytes 884768 | tf_op jit(solution)/shard_map/all_to_all | solution.py:164
  (488 shorter events, 310.7 us)
Async XLA Ops:
  8.9 33.0 %collective-permute-start.3 = (bf16[64,2304]{1,0:T(8,128)(2,1)S(1)}, bf16[64,2304]{1,0:T(8,128)(2,1)}, u32[]{:S(2)}, u32[]{:S(2)}) collective-permute-start(bf16[64,2304]{1,0:T(8,128)(2,1)S(1)} %bitcast.241), channel_id=1, source_target_pairs={{0,12},{2,14},{4,0},{6,2},{8,4},{10,6},{12,8},{14,10},{16,28},{18,... | collective-permute-start | bytes 884744 | tf_op jit(solution)/shard_map/ppermute | solution.py:128
  13.0 29.9 %collective-permute-start.2 = (bf16[64,2304]{1,0:T(8,128)(2,1)S(1)}, bf16[64,2304]{1,0:T(8,128)(2,1)}, u32[]{:S(2)}, u32[]{:S(2)}) collective-permute-start(bf16[64,2304]{1,0:T(8,128)(2,1)S(1)} %bitcast.242), channel_id=1, source_target_pairs={{0,8},{2,10},{4,12},{6,14},{8,0},{10,2},{12,4},{14,6},{16,24},{18,... | collective-permute-start | bytes 884744 | tf_op jit(solution)/shard_map/ppermute | solution.py:128
  13.0 29.9 %collective-permute-start.1 = (bf16[64,2304]{1,0:T(8,128)(2,1)S(1)}, bf16[64,2304]{1,0:T(8,128)(2,1)}, u32[]{:S(2)}, u32[]{:S(2)}) collective-permute-start(bf16[64,2304]{1,0:T(8,128)(2,1)S(1)} %bitcast.243), channel_id=1, source_target_pairs={{0,4},{2,6},{4,8},{6,10},{8,12},{10,14},{12,0},{14,2},{16,20},{18,... | collective-permute-start | bytes 884744 | tf_op jit(solution)/shard_map/ppermute | solution.py:128
  22.7 35.0 %all-to-all-start = ((bf16[4,145,768]{2,1,0:T(8,128)(2,1)}), bf16[4,145,768]{2,1,0:T(8,128)(2,1)}, u32[]{:S(2)}, u32[]{:S(2)}) async-start(bf16[4,145,768]{2,1,0:T(8,128)(2,1)} %copy.150), calls=%async_computation | async-start | bytes 1867776 | tf_op jit(solution)/shard_map/all_to_all | solution.py:164
  26.9 108.5 %all-gather.9.cloned.1.call-start = ((), (), s32[]{:S(2)}) async-start(), calls=%async_computation.13 | async-start | bytes 8404992 | tf_op jit(solution)/shard_map/all_gather | solution.py:176
  59.0 36.2 %all-to-all-start.1 = ((bf16[4,144,1152]{2,1,0:T(8,128)(2,1)}), bf16[4,144,1152]{2,1,0:T(8,128)(2,1)S(1)}, u32[]{:S(2)}, u32[]{:S(2)}) async-start(bf16[4,144,1152]{2,1,0:T(8,128)(2,1)} %copy.157), calls=%async_computation.1 | async-start | bytes 2654208 | tf_op jit(solution)/shard_map/all_to_all | solution.py:164
  63.9 188.7 %all-gather.11.cloned.1.call-start = ((), (), s32[]{:S(2)}) async-start(), calls=%async_computation.14 | async-start | bytes 4976640 | tf_op jit(solution)/shard_map/all_gather | solution.py:206
  99.2 34.7 %all-to-all-start.2 = ((bf16[4,144,1152]{2,1,0:T(8,128)(2,1)}), bf16[4,144,1152]{2,1,0:T(8,128)(2,1)S(1)}, u32[]{:S(2)}, u32[]{:S(2)}) async-start(bf16[4,144,1152]{2,1,0:T(8,128)(2,1)} %copy.158), calls=%async_computation.2 | async-start | bytes 2654208 | tf_op jit(solution)/shard_map/all_to_all | solution.py:164
  102.8 149.9 %all-gather.13.cloned.1.call-start = ((), (), s32[]{:S(2)}) async-start(), calls=%async_computation.15 | async-start | bytes 4976640 | tf_op jit(solution)/shard_map/all_gather | solution.py:206
  161.4 95.1 %collective-permute-start.16 = (bf16[2,3,144,512]{3,2,1,0:T(8,128)(2,1)}, bf16[2,3,144,512]{3,2,1,0:T(8,128)(2,1)}, u32[]{:S(2)}, u32[]{:S(2)}) collective-permute-start(bf16[2,3,144,512]{3,2,1,0:T(8,128)(2,1)} %pad_maximum_fusion.15), channel_id=1, source_target_pairs={{0,2},{2,0},{4,6},{6,4},{8,10},{10,8},{12,14},{14,12},{16,18},{18,... | collective-permute-start | bytes 2654216 | tf_op jit(solution)/shard_map/ppermute | solution.py:128
  163.2 47.5 %all-to-all-start.3 = ((bf16[4,144,1152]{2,1,0:T(8,128)(2,1)}), bf16[4,144,1152]{2,1,0:T(8,128)(2,1)S(1)}, u32[]{:S(2)}, u32[]{:S(2)}) async-start(bf16[4,144,1152]{2,1,0:T(8,128)(2,1)} %copy.159), calls=%async_computation.3 | async-start | bytes 2654208 | tf_op jit(solution)/shard_map/all_to_all | solution.py:164
  166.9 121.6 %all-gather.15.cloned.1.call-start = ((), (), s32[]{:S(2)}) async-start(), calls=%async_computation.16 | async-start | bytes 4976640 | tf_op jit(solution)/shard_map/all_gather | solution.py:206
  183.2 29.2 %collective-permute-start.10 = (bf16[64,2304]{1,0:T(8,128)(2,1)}, bf16[64,2304]{1,0:T(8,128)(2,1)}, u32[]{:S(2)}, u32[]{:S(2)}) collective-permute-start(bf16[64,2304]{1,0:T(8,128)(2,1)} %get-tuple-element.118), channel_id=1, source_target_pairs={{0,4},{2,6},{4,8},{6,10},{8,12},{10,14},{12,0},{14,2},{16,20},{18,... | collective-permute-start | bytes 884744 | tf_op jit(solution)/shard_map/ppermute | solution.py:128
  184.5 32.6 %collective-permute-start.9 = (bf16[64,2304]{1,0:T(8,128)(2,1)}, bf16[64,2304]{1,0:T(8,128)(2,1)}, u32[]{:S(2)}, u32[]{:S(2)}) collective-permute-start(bf16[64,2304]{1,0:T(8,128)(2,1)} %get-tuple-element.119), channel_id=1, source_target_pairs={{0,8},{2,10},{4,12},{6,14},{8,0},{10,2},{12,4},{14,6},{16,24},{18,... | collective-permute-start | bytes 884744 | tf_op jit(solution)/shard_map/ppermute | solution.py:128
  186.6 30.5 %collective-permute-start.8 = (bf16[64,2304]{1,0:T(8,128)(2,1)}, bf16[64,2304]{1,0:T(8,128)(2,1)}, u32[]{:S(2)}, u32[]{:S(2)}) collective-permute-start(bf16[64,2304]{1,0:T(8,128)(2,1)} %get-tuple-element.117), channel_id=1, source_target_pairs={{0,12},{2,14},{4,0},{6,2},{8,4},{10,6},{12,8},{14,10},{16,28},{18,... | collective-permute-start | bytes 884744 | tf_op jit(solution)/shard_map/ppermute | solution.py:128
  189.9 68.9 %collective-permute-start.15 = (bf16[2,3,144,640]{3,2,1,0:T(8,128)(2,1)}, bf16[2,3,144,640]{3,2,1,0:T(8,128)(2,1)}, u32[]{:S(2)}, u32[]{:S(2)}) collective-permute-start(bf16[2,3,144,640]{3,2,1,0:T(8,128)(2,1)} %pad_maximum_fusion.10), channel_id=1, source_target_pairs={{0,16},{2,18},{4,20},{6,22},{8,24},{10,26},{12,28},{14,30},{16,0},... | collective-permute-start | bytes 3317768 | tf_op jit(solution)/shard_map/ppermute | solution.py:128
  212.2 248.7 %reduce-scatter.4.cloned.1.call-start = ((), (), s32[]{:S(2)}) async-start(), calls=%async_computation.10 | async-start | bytes 6635520 | tf_op jit(solution)/shard_map/reduce_scatter | solution.py:218
  373.6 178.0 %reduce-scatter.6.cloned.1.call-start = ((), (), s32[]{:S(2)}) async-start(), calls=%async_computation.11 | async-start | bytes 13271040 | tf_op jit(solution)/shard_map/reduce_scatter | solution.py:218
  460.8 56.0 %all-to-all-start.4 = ((bf16[4,144,1152]{2,1,0:T(8,128)(2,1)}), bf16[4,144,1152]{2,1,0:T(8,128)(2,1)}, u32[]{:S(2)}, u32[]{:S(2)}) async-start(bf16[4,144,1152]{2,1,0:T(8,128)(2,1)} %bitcast.277), calls=%async_computation.5 | async-start | bytes 2654208 | tf_op jit(solution)/shard_map/all_to_all | solution.py:164
  465.2 156.8 %reduce-scatter.8.cloned.1.call-start = ((), (), s32[]{:S(2)}) async-start(), calls=%async_computation.12 | async-start | bytes 7962624 | tf_op jit(solution)/shard_map/reduce_scatter | solution.py:188
  554.3 67.6 %all-to-all-start.5 = ((bf16[4,144,2304]{2,1,0:T(8,128)(2,1)}), bf16[4,144,2304]{2,1,0:T(8,128)(2,1)S(1)}, u32[]{:S(2)}, u32[]{:S(2)}) async-start(bf16[4,144,2304]{2,1,0:T(8,128)(2,1)} %bitcast.271), calls=%async_computation.7 | async-start | bytes 5308416 | tf_op jit(solution)/shard_map/all_to_all | solution.py:164
  570.3 31.5 %collective-permute-start.45 = (f32[4,144]{1,0:T(4,128)S(1)}, f32[4,144]{1,0:T(4,128)S(1)}, u32[]{:S(2)}, u32[]{:S(2)}) collective-permute-start(f32[4,144]{1,0:T(4,128)S(1)} %bitcast.293), channel_id=1, source_target_pairs={{0,12},{2,14},{4,0},{6,2},{8,4},{10,6},{12,8},{14,10},{16,28},{18,... | collective-permute-start | bytes 6920 | tf_op jit(solution)/shard_map/ppermute | solution.py:128
  573.6 45.4 %collective-permute-start.44 = (f32[4,144]{1,0:T(4,128)S(1)}, f32[4,144]{1,0:T(4,128)S(1)}, u32[]{:S(2)}, u32[]{:S(2)}) collective-permute-start(f32[4,144]{1,0:T(4,128)S(1)} %bitcast.294), channel_id=1, source_target_pairs={{0,8},{2,10},{4,12},{6,14},{8,0},{10,2},{12,4},{14,6},{16,24},{18,... | collective-permute-start | bytes 6920 | tf_op jit(solution)/shard_map/ppermute | solution.py:128
  573.6 45.4 %collective-permute-start.43 = (f32[4,144]{1,0:T(4,128)S(1)}, f32[4,144]{1,0:T(4,128)S(1)}, u32[]{:S(2)}, u32[]{:S(2)}) collective-permute-start(f32[4,144]{1,0:T(4,128)S(1)} %bitcast.295), channel_id=1, source_target_pairs={{0,4},{2,6},{4,8},{6,10},{8,12},{10,14},{12,0},{14,2},{16,20},{18,... | collective-permute-start | bytes 6920 | tf_op jit(solution)/shard_map/ppermute | solution.py:128
  (124 other events, 1395.8 us)
Sparse Core Ops, SparseCore 0:
  57.9 53.1 all-gather.8
  112.9 50.5 all-gather.10
  166.0 72.1 all-gather.12
  240.4 47.9 all-gather.14
  373.7 59.1 reduce-scatter.3
  435.9 115.7 reduce-scatter.5
  555.1 65.4 reduce-scatter.7

commit v4 on v3

--- a/solution.py
+++ b/solution.py
@@ -73,6 +73,9 @@
             out[0, own, 0, :, begin + parts[0] : begin + units] = lower_ref[0, at]
             for step in range(1, ranks):
                 out[0, (own + step) % ranks, 0, :, begin : begin + units] = refs[at][0, step - 1]
+
+    def around(line, side, place):
+        return (line * 2 + (side ^ line), 0, 0, 0)
 
     def relative(line, side, place):
         return ((line ^ place[0]) * 2 + (side ^ place[1]), 0, 0, 0)
@@ -86,12 +89,7 @@
                 pl.BlockSpec((1, count, rows, parts[0]), relative),
                 pl.BlockSpec((1, count, rows, parts[1]), relative),
             ]
-            + [
-                pl.BlockSpec(
-                    (1, ranks - 1, rows, units), lambda line, side, place: (line * 2 + side, 0, 0, 0)
-                )
-            ]
-            * count,
+            + [pl.BlockSpec((1, ranks - 1, rows, units), around)] * count,
             out_specs=pl.BlockSpec(
                 (1, ranks, 1, rows, count * units), lambda line, side, place: (line, 0, side, 0, 0)
             ),
@@ -105,6 +103,65 @@
     return whole.reshape(-1, count * units)
 
 
+def by_part(place, whole, rows):
+    ranks, some, lanes = whole.shape[2], whole.shape[3], whole.shape[4]
+
+    def kernel(place_ref, whole_ref, *outs):
+        for core in range(2):
+            for step in range(ranks):
+                outs[core][0, (place_ref[2] + step) % ranks, 0] = whole_ref[0, core, step, :rows]
+        for step in range(ranks):
+            outs[2][0, (place_ref[2] + step) % ranks, 0] = whole_ref[0, 0, step, rows:]
+
+    def to(count):
+        return pl.BlockSpec(
+            (1, ranks, 1, count, lanes), lambda line, side, place: (line, 0, side, 0, 0)
+        )
+
+    front, back, after = pl.pallas_call(
+        kernel,
+        grid_spec=pltpu.PrefetchScalarGridSpec(
+            num_scalar_prefetch=1,
+            grid=(2, 2),
+            in_specs=[
+                pl.BlockSpec(
+                    (1,) + whole.shape[1:],
+                    lambda line, side, place: (line * 2 + (side ^ line), 0, 0, 0, 0),
+                )
+            ],
+            out_specs=[to(rows), to(rows), to(some - rows)],
+        ),
+        out_shape=[
+            jax.ShapeDtypeStruct((2, ranks, 2, count, lanes), low)
+            for count in (rows, rows, some - rows)
+        ],
+        compiler_params=pltpu.CompilerParams(vmem_limit_bytes=32 * 2**20),
+        cost_estimate=pl.CostEstimate(
+            flops=0, transcendentals=0, bytes_accessed=32 * ranks * rows * lanes
+        ),
+    )(place, whole)
+    return front.reshape(-1, lanes), back.reshape(-1, lanes), after
+
+
+def side_by_side(pieces):
+    ranks, rows, units = pieces.shape
+
+    def kernel(in_ref, out):
+        for rank in range(ranks):
+            out[:, rank * units : (rank + 1) * units] = in_ref[rank].astype(wide)
+
+    return pl.pallas_call(
+        kernel,
+        in_specs=[pl.BlockSpec(memory_space=pltpu.VMEM)],
+        out_specs=pl.BlockSpec(memory_space=pltpu.VMEM),
+        out_shape=jax.ShapeDtypeStruct((rows, ranks * units), wide),
+        compiler_params=pltpu.CompilerParams(vmem_limit_bytes=32 * 2**20),
+        cost_estimate=pl.CostEstimate(
+            flops=0, transcendentals=0, bytes_accessed=6 * ranks * rows * units
+        ),
+    )(pieces)
+
+
 class Slice:
     def __init__(self):
         self.dp = lax.axis_size("dp")
@@ -153,19 +210,33 @@
 
     def returned(self, blocks):
         total = 0.0
-        for step, block in enumerate(blocks):
+        for step, block in zip(range(0, self.ranks, self.ranks // len(blocks)), blocks, strict=True):
             if step:
                 block = self.along(block.astype(low), -step)
             total = total + block.astype(wide)
         return total
 
     def to_ranks(self, array):
+        if self.ranks != 4:
+            return self.turned(self.exchanged(array), self.rank)
+        own, after, far, before = [pick(array, (self.rank + step) % 4, 0) for step in range(4)]
+        cut = far.shape[0] // 32 * 16
+        back, ahead = self.along(far[:cut], -1), self.along(far[cut:], 2)
+        from_before, from_after = self.along(after, 1), self.along(before, -1)
+        back, ahead, from_before, from_after = hold(back, ahead, from_before, from_after)
+        far = jnp.concatenate([self.along(back, -1), ahead])
+        return jnp.stack([own, from_after, far, from_before])
+
+    def exchanged(self, array):
         groups = [[rank * 2 + side for rank in range(self.ranks)] for side in range(2)]
         return lax.all_to_all(array, "context", 0, 0, tiled=True, axis_index_groups=groups)
 
+    def turned(self, array, first):
+        return lax.dynamic_slice_in_dim(jnp.concatenate([array, array]), first, array.shape[0], 0)
+
     def square(self):
         return [
-            [self.index(dp, rank, side) for dp in range(self.dp) for side in range(2)]
+            [self.index(dp, rank, side ^ dp) for dp in range(self.dp) for side in range(2)]
             for rank in range(self.ranks)
         ]
 
@@ -176,13 +247,16 @@
         whole = lax.all_gather(
             array, all_axes, axis=0, tiled=False, axis_index_groups=self.square_cores()
         )
-        return whole.reshape((self.dp, 2, 2) + array.shape)
+        return whole.reshape((4, 2) + array.shape)
 
     def heads_by_square(self, grads, rows):
         lanes = grads[0].shape[1]
         parts = [g.astype(low).reshape(self.dp, self.ranks, 2, rows, lanes) for g in grads]
-        parts = [jnp.transpose(part, (0, 2, 1, 3, 4)) for part in parts]
-        return jnp.stack(parts, axis=2).reshape(-1, lanes)
+        parts = [self.round_square(part) for part in parts]
+        return jnp.stack(parts, axis=1).reshape(-1, lanes)
+
+    def round_square(self, parts):
+        return jnp.stack([parts[line, :, side ^ line] for line in range(2) for side in range(2)])
 
     def head_grads_out(self, parts, rows):
         total = lax.psum_scatter(
@@ -196,23 +270,19 @@
 
     def weights_in(self, array):
         ranks, rows, units = array.shape
-        whole = lax.all_gather(array, chip_axes, axis=0, tiled=False, axis_index_groups=self.square())
-        return whole.reshape(self.dp, 2, ranks, rows, units)
-
-    def others_in(self, array):
-        ranks = array.shape[0]
-        around = jnp.concatenate([array, array[: ranks - 1]])
-        around = lax.dynamic_slice_in_dim(around, self.rank + 1, ranks - 1, 0)
-        return lax.all_gather(
-            around, chip_axes, axis=0, tiled=False, axis_index_groups=self.square()
-        )
+        return lax.all_gather(array, chip_axes, axis=0, tiled=False, axis_index_groups=self.square())
 
     def by_model_row(self, whole):
+        ranks = whole.shape[1]
+        whole = self.turned(jnp.moveaxis(whole, 1, 0), ranks - self.rank)
+        whole = jnp.stack(
+            [whole[:, line * 2 + (side ^ line)] for line in range(2) for side in range(2)]
+        ).reshape((2, 2, ranks) + whole.shape[2:])
         return jnp.transpose(whole, (0, 2, 1, 3, 4)).reshape(-1, whole.shape[-1])
 
     def by_square(self, grad, rows):
         parts = grad.astype(low).reshape(self.dp, self.ranks, 2, rows, -1)
-        return jnp.transpose(parts, (0, 2, 1, 3, 4)).reshape(-1, grad.shape[1])
+        return self.round_square(parts).reshape(-1, grad.shape[1])
 
     def grads_out(self, parts, rows):
         total = lax.psum_scatter(
@@ -279,38 +349,6 @@
     gate_set, up_set, down_set = by_rank(w_gate), by_rank(w_up), by_rank(w_down)
     token_blocks = jnp.stack(net.moves(own_tokens))
 
-    by_parts = rows % 16 == 0 and units % LANES == 0
-    if by_parts:
-        own_units = jnp.stack(
-            [lax.dynamic_slice_in_dim(w, net.rank * units, units, 1) for w in (w_gate, w_up, w_down)]
-        )
-        middle_lane = (units // LANES + 1) // 2 * LANES
-        upper, lower = own_units[:, :, :middle_lane], own_units[:, :, middle_lane:]
-        upper = jnp.stack([upper, net.across(upper)])
-        lower = jnp.stack([lower, net.over(lower)])
-        part, token_blocks, upper, lower, gate_set, up_set, down_set = hold(
-            part, token_blocks, upper, lower, gate_set, up_set, down_set
-        )
-        upper = jnp.concatenate([upper, net.over(upper)])
-        lower_side = net.across(lower)
-        lower = jnp.stack([lower[0], lower_side[0], lower[1], lower_side[1]])
-        place = jnp.stack([net.line, net.side, net.rank]).astype(jnp.int32)
-    else:
-        part, token_blocks, gate_set, up_set, down_set = hold(
-            part, token_blocks, gate_set, up_set, down_set
-        )
-    weights_in = net.others_in if by_parts else net.weights_in
-
-    gate_set = net.to_ranks(gate_set)
-    head_all = net.heads_in(part)
-    gate_units = weights_in(gate_set)
-    gate_set, up_set = hold(gate_set, up_set)
-    up_set = net.to_ranks(up_set)
-    up_units = weights_in(up_set)
-    up_set, down_set = hold(up_set, down_set)
-    down_set = net.to_ranks(down_set)
-    down_units = weights_in(down_set)
-
     own_inputs = own_tokens.astype(wide)
     block_places = (net.rank - jnp.arange(ranks)) % ranks * 2 * span
     offsets = jnp.arange(half, dtype=jnp.int32)
@@ -319,13 +357,45 @@
     key_places = jnp.concatenate(
         [
             line_places + side * span + of * half
+            for of in (core, 1 - core)
             for side in (net.side, 1 - net.side)
-            for of in (core, 1 - core)
         ]
     )
     exponent = jnp.arange(HEAD_DIM // 2, dtype=wide) * (-2.0 / HEAD_DIM)
     angles = places.astype(wide)[:, None] * (theta**exponent)[None, :]
     cosine, sine_part = jnp.cos(angles), jnp.sin(angles)
+
+    by_parts = rows % 16 == 0 and units % LANES == 0
+    place = jnp.stack([net.line, net.side, net.rank]).astype(jnp.int32)
+    if by_parts:
+        own_units = jnp.stack(
+            [lax.dynamic_slice_in_dim(w, net.rank * units, units, 1) for w in (w_gate, w_up, w_down)]
+        )
+        middle_lane = (units // LANES + 1) // 2 * LANES
+        upper, lower = own_units[:, :, :middle_lane], own_units[:, :, middle_lane:]
+        upper = jnp.stack([upper, net.across(upper)])
+        lower = jnp.stack([lower, net.over(lower)])
+        part, token_blocks, upper, lower, gate_set, up_set, down_set, cosine, sine_part = hold(
+            part, token_blocks, upper, lower, gate_set, up_set, down_set, cosine, sine_part
+        )
+        upper = jnp.concatenate([upper, net.over(upper)])
+        lower_side = net.across(lower)
+        lower = jnp.stack([lower[0], lower_side[0], lower[1], lower_side[1]])
+    else:
+        part, token_blocks, gate_set, up_set, down_set = hold(
+            part, token_blocks, gate_set, up_set, down_set
+        )
+    kept = 1 if by_parts else 0
+    head_all = net.heads_in(part)
+    gate_set = net.to_ranks(gate_set)
+    gate_units = net.weights_in(gate_set[kept:])
+    gate_set, up_set = hold(gate_set, up_set)
+    up_set = net.to_ranks(up_set)
+    up_units = net.weights_in(up_set[kept:])
+    up_set, down_set = hold(up_set, down_set)
+    down_set = net.to_ranks(down_set)
+    down_units = net.weights_in(down_set[kept:])
+
     asked = tuple(range(0, ranks, share))
 
     def asked_rows(array):
@@ -345,10 +415,15 @@
     head_cols = repeat * HEAD_DIM
 
     def attend(head_all, token_blocks):
-        front_weights = net.by_model_row(head_all[:, :, 0, :, :rows])
-        back_weights = net.by_model_row(head_all[:, :, 1, :, :rows])
-        gains = jnp.transpose(head_all[:, :, 0, :, rows, : 4 * rows], (0, 2, 1, 3))
-        gains = jnp.transpose(gains.reshape(chips, 4, rows), (1, 0, 2)).reshape(4, width).astype(wide)
+        if by_parts:
+            front_weights, back_weights, gain_rows = by_part(place, head_all, rows)
+        else:
+            front_weights, back_weights = [
+                net.by_model_row(head_all[:, of, :, :rows]) for of in range(2)
+            ]
+            gain_rows = net.by_model_row(head_all[:, 0, :, rows:])
+        gains = gain_rows.reshape(chips, lanes)[:, : 4 * rows].reshape(chips, 4, rows)
+        gains = jnp.transpose(gains, (1, 0, 2)).reshape(4, width).astype(wide)
         inputs = token_blocks.reshape(-1, width).astype(wide)
         normed_low = (inputs * inverse_size(inputs) * gains[0]).astype(low)
         query_key = product(normed_low, front_weights)
@@ -357,8 +432,8 @@
         keys = turn(query_key[:, head_cols:], cosine, sine_part).astype(low)
         values = product(normed_low, back_weights[:, head_cols:]).astype(low)
         own_kv = jnp.concatenate([keys, values], axis=1)
-        side_kv = jnp.stack([own_kv, net.swap(own_kv)])
-        all_kv = jnp.concatenate([side_kv, net.across(side_kv)]).reshape(-1, 2 * HEAD_DIM)
+        side_kv = jnp.concatenate([own_kv, net.across(own_kv)])
+        all_kv = jnp.concatenate([side_kv, net.swap(side_kv)])
         allowed = key_places[None, :] <= jnp.concatenate([asked_rows(places)] * repeat)[:, None]
         scores = product_right_t(queries, all_kv[:, :HEAD_DIM]) * score_scale
         bent = jnp.tanh(scores / softcap)
@@ -418,7 +493,9 @@
     two_blocks = jnp.stack(net.moves(normed_two_low)).reshape(-1, width)
     two_blocks, gate_units, up_units = hold(two_blocks, gate_units, up_units)
     if by_parts:
-        pair_units = assembled(place, ranks, rows, upper[:, :2], lower[:, :2], [gate_units, up_units])
+        pair_units = assembled(
+            place, ranks, rows, upper[:, :2], lower[:, :2], [gate_units, up_units]
+        )
     else:
         pair_units = jnp.concatenate(
             [net.by_model_row(gate_units), net.by_model_row(up_units)], axis=1
@@ -458,19 +535,27 @@
     d_hidden = product(all_branch, down_units)
     _, pull = jax.vjp(geglu, gate_in, upward)
     d_gate, d_up = pull(d_hidden)
-    d_pair_low = jnp.concatenate([d_gate.astype(low), d_up.astype(low)], axis=1)
-    d_two = core_total(product_right_t(d_pair_low, pair_units))
+    d_gate_low, d_up_low = d_gate.astype(low), d_up.astype(low)
+    d_two = product_right_t(jnp.concatenate([d_gate_low, d_up_low], axis=1), pair_units)
+    d_two, d_gate_low, d_up_low, all_two = hold(
+        core_total(d_two), d_gate_low, d_up_low, all_two
+    )
     d_normed_two = line_total(d_two)
-    pair_grad = net.by_square(product_left_t(all_two, d_pair_low), rows)
-    d_normed_two, pair_grad = hold(d_normed_two, pair_grad)
-    pair_grad = net.grads_out(pair_grad, rows)
+    gate_grad = net.by_square(product_left_t(all_two, d_gate_low), rows)
+    up_grad = net.by_square(product_left_t(all_two, d_up_low), rows)
+    d_normed_two, gate_grad, up_grad, down_grad = hold(
+        d_normed_two, gate_grad, up_grad, down_grad
+    )
+    gate_grad = net.grads_out(gate_grad, rows)
     grad_ffw_in = jnp.sum(d_normed_two * unit_pre, axis=0)
     d_middle = upstream + norm_back(unit_pre, inverse_pre, scale_pre, d_normed_two)
     grad_attn_out = jnp.sum(d_middle * unit_mid, axis=0)
     d_projected_low = norm_back(unit_mid, inverse_mid, scale_mid, d_middle).astype(low)
+    d_projected_low, up_grad = hold(d_projected_low, up_grad)
+    up_grad = net.grads_out(up_grad, rows)
     d_projected_all = jnp.stack(net.moves(d_projected_low))
     d_projected_all, down_grad = hold(d_projected_all, down_grad)
-    down_grad = net.to_ranks(down_grad)
+    down_grad = net.exchanged(down_grad)
     d_projected_asked = asked_rows(d_projected_all.reshape(-1, width))
     d_mixed_low = by_head(product(d_projected_asked, w_out_head).astype(low))
     d_prob = product_right_t(d_mixed_low, all_values)
@@ -480,27 +565,34 @@
     d_queries = product(d_scores, all_keys) * score_scale
     d_keys = product_left_t(d_scores, queries) * score_scale
     d_values = product_left_t(probabilities_low, d_mixed_low)
-    d_kv = jnp.concatenate([d_keys, d_values], axis=1)
-    d_kv = d_kv.reshape(2, 2, ranks * half, 2 * HEAD_DIM)
-    d_kv = d_kv[0] + net.across(d_kv[1].astype(low)).astype(wide)
-    d_kv = d_kv[0] + net.swap(d_kv[1].astype(low)).astype(wide)
+    count = all_keys.shape[0] // 2
+    given = jnp.concatenate([d_keys[count:].astype(low), d_values[count:].astype(low)], axis=1)
+    given = net.swap(given).astype(wide)
+    d_keys = d_keys[:count] + given[:, :HEAD_DIM]
+    d_values = d_values[:count] + given[:, HEAD_DIM:]
+    count = count // 2
+    given = jnp.concatenate([d_keys[count:].astype(low), d_values[count:].astype(low)], axis=1)
+    given = net.across(given).astype(wide)
+    d_keys = d_keys[:count] + given[:, :HEAD_DIM]
+    d_values = d_values[:count] + given[:, HEAD_DIM:]
     d_query_low = by_token(turn(d_queries, cosine_heads, -sine_heads).astype(low))
-    d_key_low = turn(d_kv[:, :HEAD_DIM], cosine, -sine_part).astype(low)
+    d_key_low = turn(d_keys, cosine, -sine_part).astype(low)
     if share != 1:
         blocks = jnp.zeros((ranks, half, repeat * HEAD_DIM), low)
         d_query_low = blocks.at[jnp.array(asked)].set(
             d_query_low.reshape(len(asked), half, repeat * HEAD_DIM)
         )
         d_query_low = d_query_low.reshape(-1, repeat * HEAD_DIM)
-    d_value_low = d_kv[:, HEAD_DIM:].astype(low)
+    d_value_low = d_values.astype(low)
     d_front_low = jnp.concatenate([d_query_low, d_key_low], axis=1)
     d_normed_part = product_right_t(d_front_low, front_weights)
     d_normed_part = d_normed_part + product_right_t(d_value_low, w_value_head)
     grad_attn_in = jnp.sum(d_normed_part * units_in, axis=0)
     d_normed_low = d_normed_part.astype(low).reshape(ranks, half, width)
-    down_grad, d_normed_low, d_front_low, d_value_low = hold(
-        down_grad, d_normed_low, d_front_low, d_value_low
-    )
+    d_normed_low, d_front_low, d_value_low, down_grad, gate_grad = hold(
+        d_normed_low, d_front_low, d_value_low, down_grad, gate_grad
+    )
+    gate_grad = net.exchanged(gate_grad)
     d_normed = net.returned(list(d_normed_low))
     front_grads = product_left_t(normed_low, d_front_low)
     back_grads = jnp.concatenate(
@@ -511,9 +603,11 @@
         axis=1,
     )
     head_grads = net.heads_by_square([front_grads, back_grads], rows)
-    d_normed, pair_grad, head_grads = hold(d_normed, pair_grad, head_grads)
+    head_grads, gate_grad = hold(head_grads, gate_grad)
     head_grads = net.head_grads_out(head_grads, rows)
-    pair_grad = net.to_ranks(pair_grad)
+    up_grad, gate_grad = hold(up_grad, gate_grad)
+    up_grad = net.exchanged(up_grad)
+    up_grad, head_grads = hold(up_grad, head_grads)
     gain_grads = jnp.stack([grad_attn_in, grad_attn_out, grad_ffw_in, grad_ffw_out])
     gain_grads = gain_grads + net.swap(gain_grads)
     gain_grads = jnp.transpose(gain_grads.reshape(4, net.dp, ranks, 2, rows), (1, 2, 3, 0, 4))
@@ -526,8 +620,7 @@
     own_grad = d_middle + norm_back(own_inputs * own_inverse, own_inverse, scale_in, d_normed)
     layer_output = jnp.concatenate(net.ordered(own_output, net.swap(own_output)))
     input_grad = jnp.concatenate(net.ordered(own_grad, net.swap(own_grad)))
-    pair_grad, head_grads = hold(pair_grad, head_grads)
-    got = net.to_ranks(head_grads)
+    got = net.exchanged(head_grads)
     got = got.astype(wide).reshape(kv_heads, share, rows, lanes).sum(axis=1)
     got = jnp.transpose(got, (1, 0, 2)).reshape(rows, 2, kv_heads // 2, lanes)
     cut = repeat * HEAD_DIM
@@ -541,6 +634,8 @@
     grad_out, grad_value = back[:, :q_cols], back[:, q_cols:]
 
     def by_units(pieces):
+        if by_parts:
+            return side_by_side(pieces)
         return jnp.transpose(pieces, (1, 0, 2)).reshape(rows, ranks * units).astype(wide)
 
     return (
@@ -550,8 +645,8 @@
         grad_key,
         grad_value,
         grad_out,
-        by_units(pair_grad[:, :, :units]),
-        by_units(pair_grad[:, :, units:]),
+        by_units(gate_grad),
+        by_units(up_grad),
         by_units(down_grad),
         gain_got[0],
         gain_got[1],

time: 671 us -> 657 us (0.979)
  waiting for transfers between devices: 320 us -> 269 us
  starting transfers between devices: 103 us -> 135 us
  local copies, waits for them, and re-layouts: 97.4 us -> 84.7 us
  Pallas kernels: 3.54 us -> 11.5 us
  other arithmetic: 63.2 us -> 70.6 us
    all_to_all x7 -> x4, waiting for transfers between devices: 106 us -> 35.4 us  [exchanged(): lax.all_to_all(array, 'context', 0, 0, tiled=True, axis_index_groups=groups)]
    ppermute x35 -> x55, starting transfers between devices: 57.9 us -> 98.6 us  [send(): return lax.ppermute(block, chip_axes, pairs)]
    ppermute x35 -> x55, waiting for transfers between devices: 187 us -> 224 us  [send(): return lax.ppermute(block, chip_axes, pairs)]
    another operation x10 -> x20, other arithmetic: 8.76 us -> 22.2 us  [the longest x4 9.41 us: round_square(): jnp.stack([parts[line, :, side ^ line] for line in range(2) for side in r...]
    transpose x3 -> x0, local copies, waits for them, and re-layouts: 12.9 us -> none  [by_model_row(): return jnp.transpose(whole, (0, 2, 1, 3, 4)).reshape(-1, whole.shape[-1])]
    unnamed x188 -> x245, local copies, waits for them, and re-layouts: 20.1 us -> 32 us
    all_gather x3, waiting for transfers between devices: 11.5 us -> 0.01 us  [weights_in(): lax.all_gather(array, chip_axes, axis=0, tiled=False, axis_index_groups=s...]
    pallas_call x0 -> x4, Pallas kernels: none -> 8 us  [the longest x3 6.34 us: side_by_side(): pl.pallas_call(kernel, in_specs=[pl.BlockSpec(memory_space=pltpu.VMEM)],...]
  transfers between devices with their start and end apart: 60 -> 78, of which waited for: 29 -> 35; matrix products, arithmetic and copies ran while one was open for 28% -> 26% of each run, Pallas kernels for 0% -> 2%
where the time goes in v4:
time: 657 us; the launch traced here: 646 us
  waiting for transfers between devices  269 us (41%)
  starting transfers between devices  135 us (21%)
  local copies, waits for them, and re-layouts  84.7 us (13%)
  other arithmetic  70.6 us (11%)
  matrix products  58.7 us (9%)
  between operations  16.8 us (3%)
  Pallas kernels  11.5 us (2%)
    ppermute x55, waiting for transfers between devices, send(): return lax.ppermute(block, chip_axes, pairs)  224 us
    ppermute x55, starting transfers between devices, send(): return lax.ppermute(block, chip_axes, pairs)  98.6 us
    all_to_all x4, waiting for transfers between devices, exchanged(): lax.all_to_all(array, 'context', 0, 0, tiled=True, axis_index_groups=groups)  35.4 us
    unnamed x245, local copies, waits for them, and re-layouts  32 us
    all_to_all x4, starting transfers between devices, exchanged(): lax.all_to_all(array, 'context', 0, 0, tiled=True, axis_index_groups=groups)  21.1 us
    dot_general x7, matrix products, product(): return jnp.dot(left_side, right_side, preferred_element_type=wide)  21.1 us
    dot_general x7, matrix products, product_right_t(): lax.dot_general(left_side, right_side, (((1,), (1,)), ((), ())), preferre...  20.9 us
    dot_general x8, matrix products, product_left_t(): lax.dot_general(left_side, right_side, (((0,), (0,)), ((), ())), preferre...  16.7 us
  transfers between devices with their start and end apart: 78, of which 35 were waited for; matrix products, arithmetic and copies ran while one was open for 26% of the time, Pallas kernels for 2%

profile of v4, /device:TPU:1, one launch (start us, length us, event | category | flops | bytes accessed | tf_op | source)
XLA Modules:
  0.0 646.4 jit_solution(11128478373875653848)
XLA Ops:
  50.3 8.1 %collective-permute-done.1 = bf16[64,768]{1,0:T(8,128)(2,1)S(1)} collective-permute-done((bf16[64,768]{1,0:T(8,128)(2,1)S(1)}, bf16[64,768]{1,0:T(8,128)(2,1)S(1)}, u32[]{:S(2)}, u32[]{:S(2)}) %collective-permute-start.1) | collective-permute-done | bytes 98336 | tf_op jit(solution)/shard_map/ppermute | solution.py:185
  76.4 13.9 %collective-permute-done.24 = bf16[64,1152]{1,0:T(8,128)(2,1)S(1)} collective-permute-done((bf16[64,1152]{1,0:T(8,128)(2,1)S(1)}, bf16[64,1152]{1,0:T(8,128)(2,1)S(1)}, u32[]{:S(2)}, u32[]{:S(2)}) %collective-permute-start.24) | collective-permute-done | bytes 147488 | tf_op jit(solution)/shard_map/ppermute | solution.py:185
  90.3 7.1 %collective-permute-done.25 = bf16[80,1152]{1,0:T(8,128)(2,1)S(1)} collective-permute-done((bf16[80,1152]{1,0:T(8,128)(2,1)S(1)}, bf16[80,1152]{1,0:T(8,128)(2,1)S(1)}, u32[]{:S(2)}, u32[]{:S(2)}) %collective-permute-start.25) | collective-permute-done | bytes 184352 | tf_op jit(solution)/shard_map/ppermute | solution.py:185
  97.9 7.2 %collective-permute-done.28 = bf16[64,1152]{1,0:T(8,128)(2,1)S(1)} collective-permute-done((bf16[64,1152]{1,0:T(8,128)(2,1)S(1)}, bf16[64,1152]{1,0:T(8,128)(2,1)S(1)}, u32[]{:S(2)}, u32[]{:S(2)}) %collective-permute-start.28) | collective-permute-done | bytes 147488 | tf_op jit(solution)/shard_map/ppermute | solution.py:185
  117.9 13.0 %collective-permute-done.19 = bf16[64,1152]{1,0:T(8,128)(2,1)S(1)} collective-permute-done((bf16[64,1152]{1,0:T(8,128)(2,1)S(1)}, bf16[64,1152]{1,0:T(8,128)(2,1)S(1)}, u32[]{:S(2)}, u32[]{:S(2)}) %collective-permute-start.19) | collective-permute-done | bytes 147488 | tf_op jit(solution)/shard_map/ppermute | solution.py:185
  179.0 5.8 collective-permute-done.11
  188.8 7.1 %collective-permute-done.32 = bf16[64,1152]{1,0:T(8,128)(2,1)S(1)} collective-permute-done((bf16[64,1152]{1,0:T(8,128)(2,1)S(1)}, bf16[64,1152]{1,0:T(8,128)(2,1)S(1)}, u32[]{:S(2)}, u32[]{:S(2)}) %collective-permute-start.32) | collective-permute-done | bytes 147488 | tf_op jit(solution)/shard_map/ppermute | solution.py:185
  216.8 21.2 %collective-permute-done.14 = bf16[64,2304]{1,0:T(8,128)(2,1)} collective-permute-done((bf16[64,2304]{1,0:T(8,128)(2,1)S(1)}, bf16[64,2304]{1,0:T(8,128)(2,1)}, u32[]{:S(2)}, u32[]{:S(2)}) %collective-permute-start.14) | collective-permute-done | bytes 294944 | tf_op jit(solution)/shard_map/ppermute | solution.py:185
  248.8 14.2 %collective-permute-done.17 = bf16[64,2304]{1,0:T(8,128)(2,1)S(1)} collective-permute-done((bf16[64,2304]{1,0:T(8,128)(2,1)S(1)}, bf16[64,2304]{1,0:T(8,128)(2,1)S(1)}, u32[]{:S(2)}, u32[]{:S(2)}) %collective-permute-start.17) | collective-permute-done | bytes 294944 | tf_op jit(solution)/shard_map/ppermute | solution.py:185
  299.3 7.9 %collective-permute-start.38 = (bf16[64,2304]{1,0:T(8,128)(2,1)}, bf16[64,2304]{1,0:T(8,128)(2,1)S(1)}, u32[]{:S(2)}, u32[]{:S(2)}) collective-permute-start(bf16[64,2304]{1,0:T(8,128)(2,1)} %get-tuple-element.192), channel_id=1, source_target_pairs={{0,12},{2,14},{4,0},{6,2},{8,4},{10,6},{12,8},{14,10},{16,28},{18,... | collective-permute-start | bytes 884744 | tf_op jit(solution)/shard_map/ppermute | solution.py:185
  307.6 6.3 collective-permute-done.38
  313.9 19.0 %collective-permute-done.39 = bf16[64,2304]{1,0:T(8,128)(2,1)S(1)} collective-permute-done((bf16[64,2304]{1,0:T(8,128)(2,1)}, bf16[64,2304]{1,0:T(8,128)(2,1)S(1)}, u32[]{:S(2)}, u32[]{:S(2)}) %collective-permute-start.39) | collective-permute-done | bytes 294944 | tf_op jit(solution)/shard_map/ppermute | solution.py:185
  345.4 12.5 %collective-permute-done.43 = bf16[64,2304]{1,0:T(8,128)(2,1)S(1)} collective-permute-done((bf16[64,2304]{1,0:T(8,128)(2,1)S(1)}, bf16[64,2304]{1,0:T(8,128)(2,1)S(1)}, u32[]{:S(2)}, u32[]{:S(2)}) %collective-permute-start.43) | collective-permute-done | bytes 294944 | tf_op jit(solution)/shard_map/ppermute | solution.py:185
  371.4 9.1 %fusion.6 = (bf16[512,1152]{1,0:T(8,128)(2,1)S(1)}, bf16[512,1152]{1,0:T(8,128)(2,1)S(1)}) fusion(f32[512,2304]{1,0:T(8,128)} %copy-done.31, bf16[512,2304]{1,0:T(8,128)(2,1)} %pad_maximum_fusion.4, bf16[2304,1152]{1,0:T(8,128)(2,1)} %bitcast.340), kind=kOutput, calls=%fused_computation.28 | convolution fusion | flops 2732064768 | bytes 14745600 | tf_op jit(solution)/shard_map/dot_general | solution.py:23
  380.4 10.9 %convolution_convert_fusion.5 = bf16[512,2304]{1,0:T(8,128)(2,1)S(1)} fusion(bf16[2304,2304]{1,0:T(8,128)(2,1)} %bitcast.337, bf16[512,1152]{1,0:T(8,128)(2,1)S(1)} %get-tuple-element.108, bf16[512,1152]{1,0:T(8,128)(2,1)S(1)} %get-tuple-element.107), kind=kOutput, calls=%fused_computation.12 | convolution fusion | flops 5441716224 | bytes 15335424 | tf_op jit(solution)/shard_map/dot_general | solution.py:27
  394.8 6.3 collective-permute-start.47
  415.6 11.0 %collective-permute-done.48 = bf16[64,2304]{1,0:T(8,128)(2,1)S(1)} collective-permute-done((bf16[64,2304]{1,0:T(8,128)(2,1)S(1)}, bf16[64,2304]{1,0:T(8,128)(2,1)S(1)}, u32[]{:S(2)}, u32[]{:S(2)}) %collective-permute-start.48) | collective-permute-done | bytes 294944 | tf_op jit(solution)/shard_map/ppermute | solution.py:185
  443.3 13.6 %collective-permute-done.51 = bf16[64,2304]{1,0:T(8,128)(2,1)} collective-permute-done((bf16[64,2304]{1,0:T(8,128)(2,1)}, bf16[64,2304]{1,0:T(8,128)(2,1)}, u32[]{:S(2)}, u32[]{:S(2)}) %collective-permute-start.51) | collective-permute-done | bytes 294944 | tf_op jit(solution)/shard_map/ppermute | solution.py:185
  467.0 9.0 %all-to-all-start = ((bf16[4,144,1152]{2,1,0:T(8,128)(2,1)}), bf16[4,144,1152]{2,1,0:T(8,128)(2,1)S(1)}, u32[]{:S(2)}, u32[]{:S(2)}) async-start(bf16[4,144,1152]{2,1,0:T(8,128)(2,1)} %bitcast.388), calls=%async_computation.1 | async-start | bytes 2654208 | tf_op jit(solution)/shard_map/all_to_all | solution.py:232
  493.5 13.9 %all-to-all-done.in_ref = bf16[4,144,1152]{2,1,0:T(8,128)(2,1)S(1)} async-done(((bf16[4,144,1152]{2,1,0:T(8,128)(2,1)}), bf16[4,144,1152]{2,1,0:T(8,128)(2,1)S(1)}, u32[]{:S(2)}, u32[]{:S(2)}) %all-to-all-start) | async-done | bytes 1327136 | tf_op jit(solution)/shard_map/all_to_all | solution.py:232
  524.5 17.6 %all-to-all-done.1.in_ref = bf16[4,144,1152]{2,1,0:T(8,128)(2,1)S(1)} async-done(((bf16[4,144,1152]{2,1,0:T(8,128)(2,1)}), bf16[4,144,1152]{2,1,0:T(8,128)(2,1)S(1)}, u32[]{:S(2)}, u32[]{:S(2)}) %all-to-all-start.1) | async-done | bytes 1327136 | tf_op jit(solution)/shard_map/all_to_all | solution.py:232
  561.3 14.3 %collective-permute-done.63 = f32[4,144]{1,0:T(4,128)S(1)} collective-permute-done((f32[4,144]{1,0:T(4,128)S(1)}, f32[4,144]{1,0:T(4,128)S(1)}, u32[]{:S(2)}, u32[]{:S(2)}) %collective-permute-start.63) | collective-permute-done | bytes 2336 | tf_op jit(solution)/shard_map/ppermute | solution.py:185
  575.7 17.5 %collective-permute-start.57 = (bf16[64,2304]{1,0:T(8,128)(2,1)}, bf16[64,2304]{1,0:T(8,128)(2,1)}, u32[]{:S(2)}, u32[]{:S(2)}) collective-permute-start(bf16[64,2304]{1,0:T(8,128)(2,1)} %get-tuple-element.187), channel_id=1, source_target_pairs={{0,4},{2,6},{4,8},{6,10},{8,12},{10,14},{12,0},{14,2},{16,20},{18,... | collective-permute-start | bytes 884744 | tf_op jit(solution)/shard_map/ppermute | solution.py:185
  599.7 17.4 %collective-permute-done.56 = bf16[64,2304]{1,0:T(8,128)(2,1)} collective-permute-done((bf16[64,2304]{1,0:T(8,128)(2,1)}, bf16[64,2304]{1,0:T(8,128)(2,1)}, u32[]{:S(2)}, u32[]{:S(2)}) %collective-permute-start.56) | collective-permute-done | bytes 294944 | tf_op jit(solution)/shard_map/ppermute | solution.py:185
  (599 shorter events, 345.8 us)
Async XLA Ops:
  7.2 137.3 %all-gather.9.cloned.1.call-start = ((), (), s32[]{:S(2)}) async-start(), calls=%async_computation.12 | async-start | bytes 8404992 | tf_op jit(solution)/shard_map/all_gather | solution.py:247
  8.9 28.4 %collective-permute-start.6 = (bf16[64,2304]{1,0:T(8,128)(2,1)S(1)}, bf16[64,2304]{1,0:T(8,128)(2,1)}, u32[]{:S(2)}, u32[]{:S(2)}) collective-permute-start(bf16[64,2304]{1,0:T(8,128)(2,1)S(1)} %bitcast.365), channel_id=1, source_target_pairs={{0,4},{2,6},{4,8},{6,10},{8,12},{10,14},{12,0},{14,2},{16,20},{18,... | collective-permute-start | bytes 884744 | tf_op jit(solution)/shard_map/ppermute | solution.py:185
  11.0 27.6 %collective-permute-start.7 = (bf16[64,2304]{1,0:T(8,128)(2,1)S(1)}, bf16[64,2304]{1,0:T(8,128)(2,1)}, u32[]{:S(2)}, u32[]{:S(2)}) collective-permute-start(bf16[64,2304]{1,0:T(8,128)(2,1)S(1)} %bitcast.366), channel_id=1, source_target_pairs={{0,8},{2,10},{4,12},{6,14},{8,0},{10,2},{12,4},{14,6},{16,24},{18,... | collective-permute-start | bytes 884744 | tf_op jit(solution)/shard_map/ppermute | solution.py:185
  23.8 40.4 %collective-permute-start.9 = (bf16[3,144,640]{2,1,0:T(8,128)(2,1)}, bf16[3,144,640]{2,1,0:T(8,128)(2,1)}, u32[]{:S(2)}, u32[]{:S(2)}) collective-permute-start(bf16[3,144,640]{2,1,0:T(8,128)(2,1)} %get-tuple-element.207), channel_id=1, source_target_pairs={{0,2},{2,0},{4,6},{6,4},{8,10},{10,8},{12,14},{14,12},{16,18},{18,... | collective-permute-start | bytes 1658888 | tf_op jit(solution)/shard_map/ppermute | solution.py:185
  67.5 196.7 %all-gather.13.cloned.1.call-start = ((), (), s32[]{:S(2)}) async-start(), calls=%async_computation.14 | async-start | bytes 4976640 | tf_op jit(solution)/shard_map/all_gather | solution.py:273
  70.8 26.6 %collective-permute-start.26 = (bf16[144,1152]{1,0:T(8,128)(2,1)S(1)}, bf16[144,1152]{1,0:T(8,128)(2,1)S(1)}, u32[]{:S(2)}, u32[]{:S(2)}) collective-permute-start(bf16[144,1152]{1,0:T(8,128)(2,1)S(1)} %bitcast.400), channel_id=1, source_target_pairs={{0,4},{2,6},{4,8},{6,10},{8,12},{10,14},{12,0},{14,2},{16,20},{18,... | collective-permute-start | bytes 995336 | tf_op jit(solution)/shard_map/ppermute | solution.py:185
  106.2 158.1 %all-gather.11.cloned.1.call-start = ((), (), s32[]{:S(2)}) async-start(), calls=%async_computation.13 | async-start | bytes 4976640 | tf_op jit(solution)/shard_map/all_gather | solution.py:273
  144.5 142.1 %all-gather.15.cloned.1.call-start = ((), (), s32[]{:S(2)}) async-start(), calls=%async_computation.15 | async-start | bytes 4976640 | tf_op jit(solution)/shard_map/all_gather | solution.py:273
  173.4 27.7 %collective-permute-start.34 = (bf16[144,1152]{1,0:T(8,128)(2,1)S(1)}, bf16[144,1152]{1,0:T(8,128)(2,1)S(1)}, u32[]{:S(2)}, u32[]{:S(2)}) collective-permute-start(bf16[144,1152]{1,0:T(8,128)(2,1)S(1)} %bitcast.396), channel_id=1, source_target_pairs={{0,4},{2,6},{4,8},{6,10},{8,12},{10,14},{12,0},{14,2},{16,20},{18,... | collective-permute-start | bytes 995336 | tf_op jit(solution)/shard_map/ppermute | solution.py:185
  195.9 71.0 %collective-permute-start.31 = (bf16[2,3,144,512]{3,2,1,0:T(8,128)(2,1)}, bf16[2,3,144,512]{3,2,1,0:T(8,128)(2,1)}, u32[]{:S(2)}, u32[]{:S(2)}) collective-permute-start(bf16[2,3,144,512]{3,2,1,0:T(8,128)(2,1)} %pad_maximum_fusion.19), channel_id=1, source_target_pairs={{0,2},{2,0},{4,6},{6,4},{8,10},{10,8},{12,14},{14,12},{16,18},{18,... | collective-permute-start | bytes 2654216 | tf_op jit(solution)/shard_map/ppermute | solution.py:185
  200.0 68.5 %collective-permute-start.30 = (bf16[2,3,144,640]{3,2,1,0:T(8,128)(2,1)}, bf16[2,3,144,640]{3,2,1,0:T(8,128)(2,1)}, u32[]{:S(2)}, u32[]{:S(2)}) collective-permute-start(bf16[2,3,144,640]{3,2,1,0:T(8,128)(2,1)} %pad_maximum_fusion.10), channel_id=1, source_target_pairs={{0,16},{2,18},{4,20},{6,22},{8,24},{10,26},{12,28},{14,30},{16,0},... | collective-permute-start | bytes 3317768 | tf_op jit(solution)/shard_map/ppermute | solution.py:185
  215.2 212.7 %reduce-scatter.5.cloned.1.call-start = ((), (), s32[]{:S(2)}) async-start(), calls=%async_computation.8 | async-start | bytes 6635520 | tf_op jit(solution)/shard_map/reduce_scatter | solution.py:288
  371.3 136.1 %reduce-scatter.7.cloned.1.call-start = ((), (), s32[]{:S(2)}) async-start(), calls=%async_computation.9 | async-start | bytes 6635520 | tf_op jit(solution)/shard_map/reduce_scatter | solution.py:288
  427.9 118.5 %reduce-scatter.9.cloned.1.call-start = ((), (), s32[]{:S(2)}) async-start(), calls=%async_computation.10 | async-start | bytes 6635520 | tf_op jit(solution)/shard_map/reduce_scatter | solution.py:288
  467.0 40.4 %all-to-all-start = ((bf16[4,144,1152]{2,1,0:T(8,128)(2,1)}), bf16[4,144,1152]{2,1,0:T(8,128)(2,1)S(1)}, u32[]{:S(2)}, u32[]{:S(2)}) async-start(bf16[4,144,1152]{2,1,0:T(8,128)(2,1)} %bitcast.388), calls=%async_computation.1 | async-start | bytes 2654208 | tf_op jit(solution)/shard_map/all_to_all | solution.py:232
  507.4 34.7 %all-to-all-start.1 = ((bf16[4,144,1152]{2,1,0:T(8,128)(2,1)}), bf16[4,144,1152]{2,1,0:T(8,128)(2,1)S(1)}, u32[]{:S(2)}, u32[]{:S(2)}) async-start(bf16[4,144,1152]{2,1,0:T(8,128)(2,1)} %bitcast.389), calls=%async_computation.4 | async-start | bytes 2654208 | tf_op jit(solution)/shard_map/all_to_all | solution.py:232
  510.9 82.3 %reduce-scatter.11.cloned.1.call-start = ((), (), s32[]{:S(2)}) async-start(), calls=%async_computation.11 | async-start | bytes 7962624 | tf_op jit(solution)/shard_map/reduce_scatter | solution.py:262
  546.5 46.7 %all-to-all-start.2 = ((bf16[4,144,1152]{2,1,0:T(8,128)(2,1)}), bf16[4,144,1152]{2,1,0:T(8,128)(2,1)}, u32[]{:S(2)}, u32[]{:S(2)}) async-start(bf16[4,144,1152]{2,1,0:T(8,128)(2,1)} %bitcast.387), calls=%async_computation.5 | async-start | bytes 2654208 | tf_op jit(solution)/shard_map/all_to_all | solution.py:232
  555.6 37.5 %collective-permute-start.64 = (f32[4,144]{1,0:T(4,128)S(1)}, f32[4,144]{1,0:T(4,128)S(1)}, u32[]{:S(2)}, u32[]{:S(2)}) collective-permute-start(f32[4,144]{1,0:T(4,128)S(1)} %bitcast.424), channel_id=1, source_target_pairs={{0,8},{2,10},{4,12},{6,14},{8,0},{10,2},{12,4},{14,6},{16,24},{18,... | collective-permute-start | bytes 6920 | tf_op jit(solution)/shard_map/ppermute | solution.py:185
  557.7 35.4 %collective-permute-start.65 = (f32[4,144]{1,0:T(4,128)S(1)}, f32[4,144]{1,0:T(4,128)S(1)}, u32[]{:S(2)}, u32[]{:S(2)}) collective-permute-start(f32[4,144]{1,0:T(4,128)S(1)} %bitcast.425), channel_id=1, source_target_pairs={{0,12},{2,14},{4,0},{6,2},{8,4},{10,6},{12,8},{14,10},{16,28},{18,... | collective-permute-start | bytes 6920 | tf_op jit(solution)/shard_map/ppermute | solution.py:185
  559.8 39.9 %collective-permute-start.55 = (bf16[64,2304]{1,0:T(8,128)(2,1)}, bf16[64,2304]{1,0:T(8,128)(2,1)}, u32[]{:S(2)}, u32[]{:S(2)}) collective-permute-start(bf16[64,2304]{1,0:T(8,128)(2,1)} %get-tuple-element.186), channel_id=1, source_target_pairs={{0,12},{2,14},{4,0},{6,2},{8,4},{10,6},{12,8},{14,10},{16,28},{18,... | collective-permute-start | bytes 884744 | tf_op jit(solution)/shard_map/ppermute | solution.py:185
  560.1 57.0 %collective-permute-start.56 = (bf16[64,2304]{1,0:T(8,128)(2,1)}, bf16[64,2304]{1,0:T(8,128)(2,1)}, u32[]{:S(2)}, u32[]{:S(2)}) collective-permute-start(bf16[64,2304]{1,0:T(8,128)(2,1)} %get-tuple-element.188), channel_id=1, source_target_pairs={{0,8},{2,10},{4,12},{6,14},{8,0},{10,2},{12,4},{14,6},{16,24},{18,... | collective-permute-start | bytes 884744 | tf_op jit(solution)/shard_map/ppermute | solution.py:185
  575.7 41.5 %collective-permute-start.57 = (bf16[64,2304]{1,0:T(8,128)(2,1)}, bf16[64,2304]{1,0:T(8,128)(2,1)}, u32[]{:S(2)}, u32[]{:S(2)}) collective-permute-start(bf16[64,2304]{1,0:T(8,128)(2,1)} %get-tuple-element.187), channel_id=1, source_target_pairs={{0,4},{2,6},{4,8},{6,10},{8,12},{10,14},{12,0},{14,2},{16,20},{18,... | collective-permute-start | bytes 884744 | tf_op jit(solution)/shard_map/ppermute | solution.py:185
  593.2 33.3 %all-to-all-start.3 = ((bf16[4,144,768]{2,1,0:T(8,128)(2,1)}), bf16[4,144,768]{2,1,0:T(8,128)(2,1)S(1)}, u32[]{:S(2)}, u32[]{:S(2)}) async-start(bf16[4,144,768]{2,1,0:T(8,128)(2,1)} %bitcast.394), calls=%async_computation.7 | async-start | bytes 1769472 | tf_op jit(solution)/shard_map/all_to_all | solution.py:232
  (164 other events, 1845.5 us)
Sparse Core Ops, SparseCore 0:
  67.6 45.7 all-gather.8
  114.9 42.8 all-gather.12
  159.4 57.5 all-gather.10
  218.5 44.3 all-gather.14
  371.4 56.4 reduce-scatter.4
  430.2 52.3 reduce-scatter.6
  484.9 52.3 reduce-scatter.8
  542.2 42.2 reduce-scatter.10

commit v5 on v4

--- a/solution.py
+++ b/solution.py
@@ -217,15 +217,8 @@
         return total
 
     def to_ranks(self, array):
-        if self.ranks != 4:
-            return self.turned(self.exchanged(array), self.rank)
-        own, after, far, before = [pick(array, (self.rank + step) % 4, 0) for step in range(4)]
-        cut = far.shape[0] // 32 * 16
-        back, ahead = self.along(far[:cut], -1), self.along(far[cut:], 2)
-        from_before, from_after = self.along(after, 1), self.along(before, -1)
-        back, ahead, from_before, from_after = hold(back, ahead, from_before, from_after)
-        far = jnp.concatenate([self.along(back, -1), ahead])
-        return jnp.stack([own, from_after, far, from_before])
+        pieces = [self.along(pick(array, (self.rank - step) % self.ranks, 0), -step) for step in range(self.ranks)]
+        return jnp.stack(pieces)
 
     def exchanged(self, array):
         groups = [[rank * 2 + side for rank in range(self.ranks)] for side in range(2)]
@@ -426,14 +419,13 @@
         gains = jnp.transpose(gains, (1, 0, 2)).reshape(4, width).astype(wide)
         inputs = token_blocks.reshape(-1, width).astype(wide)
         normed_low = (inputs * inverse_size(inputs) * gains[0]).astype(low)
-        query_key = product(normed_low, front_weights)
-        queries = turn(by_head(asked_rows(query_key[:, :head_cols])), cosine_heads, sine_heads)
-        queries = queries.astype(low)
-        keys = turn(query_key[:, head_cols:], cosine, sine_part).astype(low)
+        keys = turn(product(normed_low, front_weights[:, head_cols:]), cosine, sine_part).astype(low)
         values = product(normed_low, back_weights[:, head_cols:]).astype(low)
         own_kv = jnp.concatenate([keys, values], axis=1)
         side_kv = jnp.concatenate([own_kv, net.across(own_kv)])
         all_kv = jnp.concatenate([side_kv, net.swap(side_kv)])
+        queries = product(asked_rows(normed_low), front_weights[:, :head_cols])
+        queries = turn(by_head(queries), cosine_heads, sine_heads).astype(low)
         allowed = key_places[None, :] <= jnp.concatenate([asked_rows(places)] * repeat)[:, None]
         scores = product_right_t(queries, all_kv[:, :HEAD_DIM]) * score_scale
         bent = jnp.tanh(scores / softcap)

time: 657 us -> 643 us (0.979)
  starting transfers between devices: 135 us -> 118 us
  waiting for transfers between devices: 269 us -> 276 us
    ppermute x55 -> x47, starting transfers between devices: 98.6 us -> 81.4 us  [send(): return lax.ppermute(block, chip_axes, pairs)]
    ppermute x55 -> x47, waiting for transfers between devices: 224 us -> 230 us  [send(): return lax.ppermute(block, chip_axes, pairs)]
    dot_general x7 -> x8, matrix products: 21.1 us -> 21.4 us  [product(): return jnp.dot(left_side, right_side, preferred_element_type=wide)]
    unnamed x245 -> x228, local copies, waits for them, and re-layouts: 32 us -> 32.1 us
  transfers between devices with their start and end apart: 78 -> 70, of which waited for: 35 -> 32; matrix products, arithmetic and copies ran while one was open for 26% -> 26% of each run, Pallas kernels for 2% -> 2%
where the time goes in v5:
time: 643 us; the launch traced here: 633 us
  waiting for transfers between devices  276 us (43%)
  starting transfers between devices  118 us (18%)
  local copies, waits for them, and re-layouts  84.6 us (13%)
  other arithmetic  67.6 us (11%)
  matrix products  58.9 us (9%)
  between operations  16.6 us (3%)
  Pallas kernels  11.5 us (2%)
    ppermute x47, waiting for transfers between devices, send(): return lax.ppermute(block, chip_axes, pairs)  230 us
    ppermute x47, starting transfers between devices, send(): return lax.ppermute(block, chip_axes, pairs)  81.4 us
    all_to_all x4, waiting for transfers between devices, exchanged(): lax.all_to_all(array, 'context', 0, 0, tiled=True, axis_index_groups=groups)  35.4 us
    unnamed x228, local copies, waits for them, and re-layouts  32.1 us
    dot_general x8, matrix products, product(): return jnp.dot(left_side, right_side, preferred_element_type=wide)  21.4 us
    all_to_all x4, starting transfers between devices, exchanged(): lax.all_to_all(array, 'context', 0, 0, tiled=True, axis_index_groups=groups)  21.1 us
    dot_general x7, matrix products, product_right_t(): lax.dot_general(left_side, right_side, (((1,), (1,)), ((), ())), preferre...  20.8 us
    dot_general x8, matrix products, product_left_t(): lax.dot_general(left_side, right_side, (((0,), (0,)), ((), ())), preferre...  16.7 us
  transfers between devices with their start and end apart: 70, of which 32 were waited for; matrix products, arithmetic and copies ran while one was open for 26% of the time, Pallas kernels for 2%

profile of v5, /device:TPU:1, one launch (start us, length us, event | category | flops | bytes accessed | tf_op | source)
XLA Modules:
  0.0 632.8 jit_solution(11681715594332208184)
XLA Ops:
  51.4 13.9 %collective-permute-done.2 = bf16[145,768]{1,0:T(8,128)(2,1)S(1)} collective-permute-done((bf16[145,768]{1,0:T(8,128)(2,1)S(1)}, bf16[145,768]{1,0:T(8,128)(2,1)S(1)}, u32[]{:S(2)}, u32[]{:S(2)}) %collective-permute-start.2) | collective-permute-done | bytes 222752 | tf_op jit(solution)/shard_map/ppermute | solution.py:185
  79.5 22.7 %collective-permute-done.21 = bf16[144,1152]{1,0:T(8,128)(2,1)S(1)} collective-permute-done((bf16[144,1152]{1,0:T(8,128)(2,1)S(1)}, bf16[144,1152]{1,0:T(8,128)(2,1)S(1)}, u32[]{:S(2)}, u32[]{:S(2)}) %collective-permute-start.21) | collective-permute-done | bytes 331808 | tf_op jit(solution)/shard_map/ppermute | solution.py:185
  115.4 21.7 %collective-permute-done.18 = bf16[144,1152]{1,0:T(8,128)(2,1)} collective-permute-done((bf16[144,1152]{1,0:T(8,128)(2,1)S(1)}, bf16[144,1152]{1,0:T(8,128)(2,1)}, u32[]{:S(2)}, u32[]{:S(2)}) %collective-permute-start.18) | collective-permute-done | bytes 331808 | tf_op jit(solution)/shard_map/ppermute | solution.py:185
  172.7 7.3 %collective-permute-done.9 = bf16[256,512]{0,1:T(8,128)(2,1)S(1)} collective-permute-done((bf16[256,512]{0,1:T(8,128)(2,1)S(1)}, bf16[256,512]{0,1:T(8,128)(2,1)S(1)}, u32[]{:S(2)}, u32[]{:S(2)}) %collective-permute-start.9) | collective-permute-done | bytes 262176 | tf_op jit(solution)/shard_map/ppermute | solution.py:185
  193.3 6.7 %collective-permute-done.27 = bf16[144,1152]{1,0:T(8,128)(2,1)S(1)} collective-permute-done((bf16[144,1152]{1,0:T(8,128)(2,1)S(1)}, bf16[144,1152]{1,0:T(8,128)(2,1)S(1)}, u32[]{:S(2)}, u32[]{:S(2)}) %collective-permute-start.27) | collective-permute-done | bytes 331808 | tf_op jit(solution)/shard_map/ppermute | solution.py:185
  207.2 18.0 %collective-permute-done.12 = bf16[64,2304]{1,0:T(8,128)(2,1)S(1)} collective-permute-done((bf16[64,2304]{1,0:T(8,128)(2,1)S(1)}, bf16[64,2304]{1,0:T(8,128)(2,1)S(1)}, u32[]{:S(2)}, u32[]{:S(2)}) %collective-permute-start.12) | collective-permute-done | bytes 294944 | tf_op jit(solution)/shard_map/ppermute | solution.py:185
  236.5 12.5 %collective-permute-done.15 = bf16[64,2304]{1,0:T(8,128)(2,1)S(1)} collective-permute-done((bf16[64,2304]{1,0:T(8,128)(2,1)S(1)}, bf16[64,2304]{1,0:T(8,128)(2,1)S(1)}, u32[]{:S(2)}, u32[]{:S(2)}) %collective-permute-start.15) | collective-permute-done | bytes 294944 | tf_op jit(solution)/shard_map/ppermute | solution.py:185
  264.0 5.6 fusion.99
  286.5 7.3 %collective-permute-start.30 = (bf16[64,2304]{1,0:T(8,128)(2,1)}, bf16[64,2304]{1,0:T(8,128)(2,1)S(1)}, u32[]{:S(2)}, u32[]{:S(2)}) collective-permute-start(bf16[64,2304]{1,0:T(8,128)(2,1)} %get-tuple-element.163), channel_id=1, source_target_pairs={{0,12},{2,14},{4,0},{6,2},{8,4},{10,6},{12,8},{14,10},{16,28},{18,... | collective-permute-start | bytes 884744 | tf_op jit(solution)/shard_map/ppermute | solution.py:185
  294.1 6.3 collective-permute-done.30
  300.4 19.1 %collective-permute-done.31 = bf16[64,2304]{1,0:T(8,128)(2,1)S(1)} collective-permute-done((bf16[64,2304]{1,0:T(8,128)(2,1)}, bf16[64,2304]{1,0:T(8,128)(2,1)S(1)}, u32[]{:S(2)}, u32[]{:S(2)}) %collective-permute-start.31) | collective-permute-done | bytes 294944 | tf_op jit(solution)/shard_map/ppermute | solution.py:185
  327.0 5.0 collective-permute-done.34
  332.0 12.3 %collective-permute-done.35 = bf16[64,2304]{1,0:T(8,128)(2,1)S(1)} collective-permute-done((bf16[64,2304]{1,0:T(8,128)(2,1)S(1)}, bf16[64,2304]{1,0:T(8,128)(2,1)S(1)}, u32[]{:S(2)}, u32[]{:S(2)}) %collective-permute-start.35) | collective-permute-done | bytes 294944 | tf_op jit(solution)/shard_map/ppermute | solution.py:185
  358.0 9.1 %fusion.6 = (bf16[512,1152]{1,0:T(8,128)(2,1)S(1)}, bf16[512,1152]{1,0:T(8,128)(2,1)S(1)}) fusion(f32[512,2304]{1,0:T(8,128)} %copy-done.30, bf16[512,2304]{1,0:T(8,128)(2,1)} %pad_maximum_fusion.4, bf16[2304,1152]{1,0:T(8,128)(2,1)} %bitcast.324), kind=kOutput, calls=%fused_computation.28 | convolution fusion | flops 2732064768 | bytes 14745600 | tf_op jit(solution)/shard_map/dot_general | solution.py:23
  367.0 10.9 %convolution_convert_fusion.5 = bf16[512,2304]{1,0:T(8,128)(2,1)S(1)} fusion(bf16[2304,2304]{1,0:T(8,128)(2,1)} %bitcast.321, bf16[512,1152]{1,0:T(8,128)(2,1)S(1)} %get-tuple-element.76, bf16[512,1152]{1,0:T(8,128)(2,1)S(1)} %get-tuple-element.75), kind=kOutput, calls=%fused_computation.12 | convolution fusion | flops 5441716224 | bytes 15335424 | tf_op jit(solution)/shard_map/dot_general | solution.py:27
  381.4 6.2 collective-permute-start.39
  402.1 11.0 %collective-permute-done.40 = bf16[64,2304]{1,0:T(8,128)(2,1)S(1)} collective-permute-done((bf16[64,2304]{1,0:T(8,128)(2,1)S(1)}, bf16[64,2304]{1,0:T(8,128)(2,1)S(1)}, u32[]{:S(2)}, u32[]{:S(2)}) %collective-permute-start.40) | collective-permute-done | bytes 294944 | tf_op jit(solution)/shard_map/ppermute | solution.py:185
  429.8 13.6 %collective-permute-done.43 = bf16[64,2304]{1,0:T(8,128)(2,1)} collective-permute-done((bf16[64,2304]{1,0:T(8,128)(2,1)}, bf16[64,2304]{1,0:T(8,128)(2,1)}, u32[]{:S(2)}, u32[]{:S(2)}) %collective-permute-start.43) | collective-permute-done | bytes 294944 | tf_op jit(solution)/shard_map/ppermute | solution.py:185
  453.4 9.0 %all-to-all-start = ((bf16[4,144,1152]{2,1,0:T(8,128)(2,1)}), bf16[4,144,1152]{2,1,0:T(8,128)(2,1)S(1)}, u32[]{:S(2)}, u32[]{:S(2)}) async-start(bf16[4,144,1152]{2,1,0:T(8,128)(2,1)} %bitcast.367), calls=%async_computation.1 | async-start | bytes 2654208 | tf_op jit(solution)/shard_map/all_to_all | solution.py:225
  479.8 14.0 %all-to-all-done.in_ref = bf16[4,144,1152]{2,1,0:T(8,128)(2,1)S(1)} async-done(((bf16[4,144,1152]{2,1,0:T(8,128)(2,1)}), bf16[4,144,1152]{2,1,0:T(8,128)(2,1)S(1)}, u32[]{:S(2)}, u32[]{:S(2)}) %all-to-all-start) | async-done | bytes 1327136 | tf_op jit(solution)/shard_map/all_to_all | solution.py:225
  511.0 17.5 %all-to-all-done.1.in_ref = bf16[4,144,1152]{2,1,0:T(8,128)(2,1)S(1)} async-done(((bf16[4,144,1152]{2,1,0:T(8,128)(2,1)}), bf16[4,144,1152]{2,1,0:T(8,128)(2,1)S(1)}, u32[]{:S(2)}, u32[]{:S(2)}) %all-to-all-start.1) | async-done | bytes 1327136 | tf_op jit(solution)/shard_map/all_to_all | solution.py:225
  547.8 14.3 %collective-permute-done.55 = f32[4,144]{1,0:T(4,128)S(1)} collective-permute-done((f32[4,144]{1,0:T(4,128)S(1)}, f32[4,144]{1,0:T(4,128)S(1)}, u32[]{:S(2)}, u32[]{:S(2)}) %collective-permute-start.55) | collective-permute-done | bytes 2336 | tf_op jit(solution)/shard_map/ppermute | solution.py:185
  562.1 17.5 %collective-permute-start.49 = (bf16[64,2304]{1,0:T(8,128)(2,1)}, bf16[64,2304]{1,0:T(8,128)(2,1)}, u32[]{:S(2)}, u32[]{:S(2)}) collective-permute-start(bf16[64,2304]{1,0:T(8,128)(2,1)} %get-tuple-element.158), channel_id=1, source_target_pairs={{0,4},{2,6},{4,8},{6,10},{8,12},{10,14},{12,0},{14,2},{16,20},{18,... | collective-permute-start | bytes 884744 | tf_op jit(solution)/shard_map/ppermute | solution.py:185
  586.2 17.4 %collective-permute-done.48 = bf16[64,2304]{1,0:T(8,128)(2,1)} collective-permute-done((bf16[64,2304]{1,0:T(8,128)(2,1)}, bf16[64,2304]{1,0:T(8,128)(2,1)}, u32[]{:S(2)}, u32[]{:S(2)}) %collective-permute-start.48) | collective-permute-done | bytes 294944 | tf_op jit(solution)/shard_map/ppermute | solution.py:185
  (554 shorter events, 317.2 us)
Async XLA Ops:
  7.2 132.4 %all-gather.9.cloned.1.call-start = ((), (), s32[]{:S(2)}) async-start(), calls=%async_computation.12 | async-start | bytes 8404992 | tf_op jit(solution)/shard_map/all_gather | solution.py:240
  66.4 183.8 %all-gather.13.cloned.1.call-start = ((), (), s32[]{:S(2)}) async-start(), calls=%async_computation.14 | async-start | bytes 4976640 | tf_op jit(solution)/shard_map/all_gather | solution.py:266
  70.9 31.3 %collective-permute-start.21 = (bf16[144,1152]{1,0:T(8,128)(2,1)S(1)}, bf16[144,1152]{1,0:T(8,128)(2,1)S(1)}, u32[]{:S(2)}, u32[]{:S(2)}) collective-permute-start(bf16[144,1152]{1,0:T(8,128)(2,1)S(1)} %bitcast.381), channel_id=1, source_target_pairs={{0,8},{2,10},{4,12},{6,14},{8,0},{10,2},{12,4},{14,6},{16,24},{18,... | collective-permute-start | bytes 995336 | tf_op jit(solution)/shard_map/ppermute | solution.py:185
  103.4 146.9 %all-gather.11.cloned.1.call-start = ((), (), s32[]{:S(2)}) async-start(), calls=%async_computation.13 | async-start | bytes 4976640 | tf_op jit(solution)/shard_map/all_gather | solution.py:266
  107.2 30.0 %collective-permute-start.18 = (bf16[144,1152]{1,0:T(8,128)(2,1)S(1)}, bf16[144,1152]{1,0:T(8,128)(2,1)}, u32[]{:S(2)}, u32[]{:S(2)}) collective-permute-start(bf16[144,1152]{1,0:T(8,128)(2,1)S(1)} %bitcast.378), channel_id=1, source_target_pairs={{0,8},{2,10},{4,12},{6,14},{8,0},{10,2},{12,4},{14,6},{16,24},{18,... | collective-permute-start | bytes 995336 | tf_op jit(solution)/shard_map/ppermute | solution.py:185
  139.3 134.4 %all-gather.15.cloned.1.call-start = ((), (), s32[]{:S(2)}) async-start(), calls=%async_computation.15 | async-start | bytes 4976640 | tf_op jit(solution)/shard_map/all_gather | solution.py:266
  169.9 30.0 %collective-permute-start.27 = (bf16[144,1152]{1,0:T(8,128)(2,1)S(1)}, bf16[144,1152]{1,0:T(8,128)(2,1)S(1)}, u32[]{:S(2)}, u32[]{:S(2)}) collective-permute-start(bf16[144,1152]{1,0:T(8,128)(2,1)S(1)} %bitcast.375), channel_id=1, source_target_pairs={{0,8},{2,10},{4,12},{6,14},{8,0},{10,2},{12,4},{14,6},{16,24},{18,... | collective-permute-start | bytes 995336 | tf_op jit(solution)/shard_map/ppermute | solution.py:185
  188.8 36.4 %collective-permute-start.12 = (bf16[64,2304]{1,0:T(8,128)(2,1)S(1)}, bf16[64,2304]{1,0:T(8,128)(2,1)S(1)}, u32[]{:S(2)}, u32[]{:S(2)}) collective-permute-start(bf16[64,2304]{1,0:T(8,128)(2,1)S(1)} %get-tuple-element.168), channel_id=1, source_target_pairs={{0,8},{2,10},{4,12},{6,14},{8,0},{10,2},{12,4},{14,6},{16,24},{18,... | collective-permute-start | bytes 884744 | tf_op jit(solution)/shard_map/ppermute | solution.py:185
  190.7 34.5 %collective-permute-start.13 = (bf16[64,2304]{1,0:T(8,128)(2,1)S(1)}, bf16[64,2304]{1,0:T(8,128)(2,1)}, u32[]{:S(2)}, u32[]{:S(2)}) collective-permute-start(bf16[64,2304]{1,0:T(8,128)(2,1)S(1)} %get-tuple-element.167), channel_id=1, source_target_pairs={{0,4},{2,6},{4,8},{6,10},{8,12},{10,14},{12,0},{14,2},{16,20},{18,... | collective-permute-start | bytes 884744 | tf_op jit(solution)/shard_map/ppermute | solution.py:185
  199.9 54.0 %collective-permute-start.25 = (bf16[2,3,144,512]{3,2,1,0:T(8,128)(2,1)}, bf16[2,3,144,512]{3,2,1,0:T(8,128)(2,1)}, u32[]{:S(2)}, u32[]{:S(2)}) collective-permute-start(bf16[2,3,144,512]{3,2,1,0:T(8,128)(2,1)} %pad_maximum_fusion.19), channel_id=1, source_target_pairs={{0,2},{2,0},{4,6},{6,4},{8,10},{10,8},{12,14},{14,12},{16,18},{18,... | collective-permute-start | bytes 2654216 | tf_op jit(solution)/shard_map/ppermute | solution.py:185
  201.2 54.4 %collective-permute-start.24 = (bf16[2,3,144,640]{3,2,1,0:T(8,128)(2,1)}, bf16[2,3,144,640]{3,2,1,0:T(8,128)(2,1)}, u32[]{:S(2)}, u32[]{:S(2)}) collective-permute-start(bf16[2,3,144,640]{3,2,1,0:T(8,128)(2,1)} %pad_maximum_fusion.10), channel_id=1, source_target_pairs={{0,16},{2,18},{4,20},{6,22},{8,24},{10,26},{12,28},{14,30},{16,0},... | collective-permute-start | bytes 3317768 | tf_op jit(solution)/shard_map/ppermute | solution.py:185
  202.6 211.8 %reduce-scatter.5.cloned.1.call-start = ((), (), s32[]{:S(2)}) async-start(), calls=%async_computation.8 | async-start | bytes 6635520 | tf_op jit(solution)/shard_map/reduce_scatter | solution.py:281
  357.9 135.9 %reduce-scatter.7.cloned.1.call-start = ((), (), s32[]{:S(2)}) async-start(), calls=%async_computation.9 | async-start | bytes 6635520 | tf_op jit(solution)/shard_map/reduce_scatter | solution.py:281
  414.5 118.4 %reduce-scatter.9.cloned.1.call-start = ((), (), s32[]{:S(2)}) async-start(), calls=%async_computation.10 | async-start | bytes 6635520 | tf_op jit(solution)/shard_map/reduce_scatter | solution.py:281
  453.4 40.4 %all-to-all-start = ((bf16[4,144,1152]{2,1,0:T(8,128)(2,1)}), bf16[4,144,1152]{2,1,0:T(8,128)(2,1)S(1)}, u32[]{:S(2)}, u32[]{:S(2)}) async-start(bf16[4,144,1152]{2,1,0:T(8,128)(2,1)} %bitcast.367), calls=%async_computation.1 | async-start | bytes 2654208 | tf_op jit(solution)/shard_map/all_to_all | solution.py:225
  493.8 34.7 %all-to-all-start.1 = ((bf16[4,144,1152]{2,1,0:T(8,128)(2,1)}), bf16[4,144,1152]{2,1,0:T(8,128)(2,1)S(1)}, u32[]{:S(2)}, u32[]{:S(2)}) async-start(bf16[4,144,1152]{2,1,0:T(8,128)(2,1)} %bitcast.368), calls=%async_computation.4 | async-start | bytes 2654208 | tf_op jit(solution)/shard_map/all_to_all | solution.py:225
  497.4 82.3 %reduce-scatter.11.cloned.1.call-start = ((), (), s32[]{:S(2)}) async-start(), calls=%async_computation.11 | async-start | bytes 7962624 | tf_op jit(solution)/shard_map/reduce_scatter | solution.py:255
  532.9 46.7 %all-to-all-start.2 = ((bf16[4,144,1152]{2,1,0:T(8,128)(2,1)}), bf16[4,144,1152]{2,1,0:T(8,128)(2,1)}, u32[]{:S(2)}, u32[]{:S(2)}) async-start(bf16[4,144,1152]{2,1,0:T(8,128)(2,1)} %bitcast.366), calls=%async_computation.5 | async-start | bytes 2654208 | tf_op jit(solution)/shard_map/all_to_all | solution.py:225
  542.1 37.5 %collective-permute-start.56 = (f32[4,144]{1,0:T(4,128)S(1)}, f32[4,144]{1,0:T(4,128)S(1)}, u32[]{:S(2)}, u32[]{:S(2)}) collective-permute-start(f32[4,144]{1,0:T(4,128)S(1)} %bitcast.402), channel_id=1, source_target_pairs={{0,8},{2,10},{4,12},{6,14},{8,0},{10,2},{12,4},{14,6},{16,24},{18,... | collective-permute-start | bytes 6920 | tf_op jit(solution)/shard_map/ppermute | solution.py:185
  544.2 35.4 %collective-permute-start.57 = (f32[4,144]{1,0:T(4,128)S(1)}, f32[4,144]{1,0:T(4,128)S(1)}, u32[]{:S(2)}, u32[]{:S(2)}) collective-permute-start(f32[4,144]{1,0:T(4,128)S(1)} %bitcast.403), channel_id=1, source_target_pairs={{0,12},{2,14},{4,0},{6,2},{8,4},{10,6},{12,8},{14,10},{16,28},{18,... | collective-permute-start | bytes 6920 | tf_op jit(solution)/shard_map/ppermute | solution.py:185
  546.3 39.9 %collective-permute-start.47 = (bf16[64,2304]{1,0:T(8,128)(2,1)}, bf16[64,2304]{1,0:T(8,128)(2,1)}, u32[]{:S(2)}, u32[]{:S(2)}) collective-permute-start(bf16[64,2304]{1,0:T(8,128)(2,1)} %get-tuple-element.157), channel_id=1, source_target_pairs={{0,12},{2,14},{4,0},{6,2},{8,4},{10,6},{12,8},{14,10},{16,28},{18,... | collective-permute-start | bytes 884744 | tf_op jit(solution)/shard_map/ppermute | solution.py:185
  546.6 57.0 %collective-permute-start.48 = (bf16[64,2304]{1,0:T(8,128)(2,1)}, bf16[64,2304]{1,0:T(8,128)(2,1)}, u32[]{:S(2)}, u32[]{:S(2)}) collective-permute-start(bf16[64,2304]{1,0:T(8,128)(2,1)} %get-tuple-element.159), channel_id=1, source_target_pairs={{0,8},{2,10},{4,12},{6,14},{8,0},{10,2},{12,4},{14,6},{16,24},{18,... | collective-permute-start | bytes 884744 | tf_op jit(solution)/shard_map/ppermute | solution.py:185
  562.1 41.5 %collective-permute-start.49 = (bf16[64,2304]{1,0:T(8,128)(2,1)}, bf16[64,2304]{1,0:T(8,128)(2,1)}, u32[]{:S(2)}, u32[]{:S(2)}) collective-permute-start(bf16[64,2304]{1,0:T(8,128)(2,1)} %get-tuple-element.158), channel_id=1, source_target_pairs={{0,4},{2,6},{4,8},{6,10},{8,12},{10,14},{12,0},{14,2},{16,20},{18,... | collective-permute-start | bytes 884744 | tf_op jit(solution)/shard_map/ppermute | solution.py:185
  579.7 33.3 %all-to-all-start.3 = ((bf16[4,144,768]{2,1,0:T(8,128)(2,1)}), bf16[4,144,768]{2,1,0:T(8,128)(2,1)S(1)}, u32[]{:S(2)}, u32[]{:S(2)}) async-start(bf16[4,144,768]{2,1,0:T(8,128)(2,1)} %bitcast.372), calls=%async_computation.7 | async-start | bytes 1769472 | tf_op jit(solution)/shard_map/all_to_all | solution.py:225
  (149 other events, 1548.6 us)
Sparse Core Ops, SparseCore 0:
  66.5 41.7 all-gather.8
  109.9 42.8 all-gather.12
  154.4 48.9 all-gather.10
  204.8 58.7 all-gather.14
  358.1 56.3 reduce-scatter.4
  416.7 52.3 reduce-scatter.6
  471.4 52.3 reduce-scatter.8
  528.7 42.2 reduce-scatter.10

commit v6 on v5

--- a/solution.py
+++ b/solution.py
@@ -334,6 +334,7 @@
     head_sets = jnp.concatenate(
         [head_sets, jnp.broadcast_to(gain_row, (kv_heads, 1, lanes))], axis=1
     )
+    head_sets, w_gate, w_up, w_down = hold(head_sets, w_gate, w_up, w_down)
     part = net.to_ranks(jnp.repeat(head_sets, share, axis=0))
 
     def by_rank(w):
@@ -361,19 +362,14 @@
     by_parts = rows % 16 == 0 and units % LANES == 0
     place = jnp.stack([net.line, net.side, net.rank]).astype(jnp.int32)
     if by_parts:
-        own_units = jnp.stack(
-            [lax.dynamic_slice_in_dim(w, net.rank * units, units, 1) for w in (w_gate, w_up, w_down)]
-        )
+        part, token_blocks, gate_set, up_set, down_set, cosine, sine_part = hold(
+            part, token_blocks, gate_set, up_set, down_set, cosine, sine_part
+        )
+        own_units = jnp.stack([pick(w, net.rank, 0) for w in (gate_set, up_set, down_set)])
         middle_lane = (units // LANES + 1) // 2 * LANES
         upper, lower = own_units[:, :, :middle_lane], own_units[:, :, middle_lane:]
         upper = jnp.stack([upper, net.across(upper)])
         lower = jnp.stack([lower, net.over(lower)])
-        part, token_blocks, upper, lower, gate_set, up_set, down_set, cosine, sine_part = hold(
-            part, token_blocks, upper, lower, gate_set, up_set, down_set, cosine, sine_part
-        )
-        upper = jnp.concatenate([upper, net.over(upper)])
-        lower_side = net.across(lower)
-        lower = jnp.stack([lower[0], lower_side[0], lower[1], lower_side[1]])
     else:
         part, token_blocks, gate_set, up_set, down_set = hold(
             part, token_blocks, gate_set, up_set, down_set
@@ -385,7 +381,13 @@
     gate_set, up_set = hold(gate_set, up_set)
     up_set = net.to_ranks(up_set)
     up_units = net.weights_in(up_set[kept:])
-    up_set, down_set = hold(up_set, down_set)
+    if by_parts:
+        up_set, down_set, upper, lower = hold(up_set, down_set, upper, lower)
+        upper = jnp.concatenate([upper, net.over(upper)])
+        lower_side = net.across(lower)
+        lower = jnp.stack([lower[0], lower_side[0], lower[1], lower_side[1]])
+    else:
+        up_set, down_set = hold(up_set, down_set)
     down_set = net.to_ranks(down_set)
     down_units = net.weights_in(down_set[kept:])
 

time: 643 us -> 635 us (0.988)
  starting transfers between devices: 118 us -> 149 us
  waiting for transfers between devices: 276 us -> 257 us
  local copies, waits for them, and re-layouts: 84.6 us -> 70.3 us
    ppermute x47, waiting for transfers between devices: 230 us -> 211 us  [send(): return lax.ppermute(block, chip_axes, pairs)]
    ppermute x47, starting transfers between devices: 81.4 us -> 100 us  [send(): return lax.ppermute(block, chip_axes, pairs)]
    ppermute x11, starting transfers between devices: 14.6 us -> 26.9 us  [swap(): return lax.ppermute(block, 'tensor', [(0, 1), (1, 0)])]
    reshape x3, local copies, waits for them, and re-layouts: 9.8 us -> 2.43 us  [by_rank(): return jnp.transpose(w.reshape(rows, ranks, units), (1, 0, 2))]
    unnamed x228 -> x221, local copies, waits for them, and re-layouts: 32.1 us -> 31.4 us
  transfers between devices with their start and end apart: 70 -> 70, of which waited for: 32 -> 32; matrix products, arithmetic and copies ran while one was open for 26% -> 23% of each run, Pallas kernels for 2% -> 2%
where the time goes in v6:
time: 635 us; the launch traced here: 627 us
  waiting for transfers between devices  257 us (40%)
  starting transfers between devices  149 us (23%)
  local copies, waits for them, and re-layouts  70.3 us (11%)
  other arithmetic  64.1 us (10%)
  matrix products  58.7 us (9%)
  between operations  16.3 us (3%)
  Pallas kernels  11.5 us (2%)
    ppermute x47, waiting for transfers between devices, send(): return lax.ppermute(block, chip_axes, pairs)  211 us
    ppermute x47, starting transfers between devices, send(): return lax.ppermute(block, chip_axes, pairs)  100 us
    all_to_all x4, waiting for transfers between devices, exchanged(): lax.all_to_all(array, 'context', 0, 0, tiled=True, axis_index_groups=groups)  35.5 us
    unnamed x221, local copies, waits for them, and re-layouts  31.4 us
    ppermute x11, starting transfers between devices, swap(): return lax.ppermute(block, 'tensor', [(0, 1), (1, 0)])  26.9 us
    dot_general x8, matrix products, product(): return jnp.dot(left_side, right_side, preferred_element_type=wide)  21.3 us
    all_to_all x4, starting transfers between devices, exchanged(): lax.all_to_all(array, 'context', 0, 0, tiled=True, axis_index_groups=groups)  21.1 us
    dot_general x7, matrix products, product_right_t(): lax.dot_general(left_side, right_side, (((1,), (1,)), ((), ())), preferre...  20.7 us
  transfers between devices with their start and end apart: 70, of which 32 were waited for; matrix products, arithmetic and copies ran while one was open for 23% of the time, Pallas kernels for 2%

profile of v6, /device:TPU:1, one launch (start us, length us, event | category | flops | bytes accessed | tf_op | source)
XLA Modules:
  0.0 627.0 jit_solution(15041158363745128346)
XLA Ops:
  25.2 8.0 %collective-permute-start.3 = (bf16[145,768]{1,0:T(8,128)(2,1)S(1)}, bf16[145,768]{1,0:T(8,128)(2,1)S(1)}, u32[]{:S(2)}, u32[]{:S(2)}) collective-permute-start(bf16[145,768]{1,0:T(8,128)(2,1)S(1)} %get-tuple-element.189), channel_id=1, source_target_pairs={{0,4},{2,6},{4,8},{6,10},{8,12},{10,14},{12,0},{14,2},{16,20},{18,... | collective-permute-start | bytes 668168 | tf_op jit(solution)/shard_map/ppermute | solution.py:185
  37.4 20.4 %collective-permute-done.2 = bf16[145,768]{1,0:T(8,128)(2,1)S(1)} collective-permute-done((bf16[145,768]{1,0:T(8,128)(2,1)S(1)}, bf16[145,768]{1,0:T(8,128)(2,1)S(1)}, u32[]{:S(2)}, u32[]{:S(2)}) %collective-permute-start.2) | collective-permute-done | bytes 222752 | tf_op jit(solution)/shard_map/ppermute | solution.py:185
  68.3 24.1 %collective-permute-done.19 = bf16[144,1152]{1,0:T(8,128)(2,1)S(1)} collective-permute-done((bf16[144,1152]{1,0:T(8,128)(2,1)S(1)}, bf16[144,1152]{1,0:T(8,128)(2,1)S(1)}, u32[]{:S(2)}, u32[]{:S(2)}) %collective-permute-start.19) | collective-permute-done | bytes 331808 | tf_op jit(solution)/shard_map/ppermute | solution.py:185
  111.2 19.7 %collective-permute-done.16 = bf16[144,1152]{1,0:T(8,128)(2,1)} collective-permute-done((bf16[144,1152]{1,0:T(8,128)(2,1)}, bf16[144,1152]{1,0:T(8,128)(2,1)}, u32[]{:S(2)}, u32[]{:S(2)}) %collective-permute-start.16) | collective-permute-done | bytes 331808 | tf_op jit(solution)/shard_map/ppermute | solution.py:185
  169.6 6.1 collective-permute-start.8
  192.2 16.8 %collective-permute-done.27 = bf16[144,1152]{1,0:T(8,128)(2,1)S(1)} collective-permute-done((bf16[144,1152]{1,0:T(8,128)(2,1)S(1)}, bf16[144,1152]{1,0:T(8,128)(2,1)S(1)}, u32[]{:S(2)}, u32[]{:S(2)}) %collective-permute-start.27) | collective-permute-done | bytes 331808 | tf_op jit(solution)/shard_map/ppermute | solution.py:185
  217.4 6.8 %collective-permute-start.12 = (bf16[64,2304]{1,0:T(8,128)(2,1)S(1)}, bf16[64,2304]{1,0:T(8,128)(2,1)S(1)}, u32[]{:S(2)}, u32[]{:S(2)}) collective-permute-start(bf16[64,2304]{1,0:T(8,128)(2,1)S(1)} %multiply_convert_fusion.6), channel_id=1, source_target_pairs={{0,4},{2,6},{4,8},{6,10},{8,12},{10,14},{12,0},{14,2},{16,20},{18,... | collective-permute-start | bytes 884744 | tf_op jit(solution)/shard_map/ppermute | solution.py:185
  227.8 7.2 %collective-permute-done.13 = bf16[64,2304]{1,0:T(8,128)(2,1)S(1)} collective-permute-done((bf16[64,2304]{1,0:T(8,128)(2,1)S(1)}, bf16[64,2304]{1,0:T(8,128)(2,1)S(1)}, u32[]{:S(2)}, u32[]{:S(2)}) %collective-permute-start.13) | collective-permute-done | bytes 294944 | tf_op jit(solution)/shard_map/ppermute | solution.py:185
  236.1 11.3 %collective-permute-start.21 = (bf16[256,2304]{1,0:T(8,128)(2,1)}, bf16[256,2304]{1,0:T(8,128)(2,1)S(1)}, u32[]{:S(2)}, u32[]{:S(2)}) collective-permute-start(bf16[256,2304]{1,0:T(8,128)(2,1)} %bitcast.27), channel_id=1, source_target_pairs={{0,1},{1,0},{2,3},{3,2},{4,5},{5,4},{6,7},{7,6},{8,9},{9,8},{10,11... | collective-permute-start | bytes 3538952 | tf_op jit(solution)/shard_map/ppermute | solution.py:202
  282.0 6.2 collective-permute-start.30
  288.6 6.3 %collective-permute-done.30 = bf16[64,2304]{1,0:T(8,128)(2,1)S(1)} collective-permute-done((bf16[64,2304]{1,0:T(8,128)(2,1)}, bf16[64,2304]{1,0:T(8,128)(2,1)S(1)}, u32[]{:S(2)}, u32[]{:S(2)}) %collective-permute-start.30) | collective-permute-done | bytes 294944 | tf_op jit(solution)/shard_map/ppermute | solution.py:185
  294.9 17.9 %collective-permute-done.31 = bf16[64,2304]{1,0:T(8,128)(2,1)S(1)} collective-permute-done((bf16[64,2304]{1,0:T(8,128)(2,1)}, bf16[64,2304]{1,0:T(8,128)(2,1)S(1)}, u32[]{:S(2)}, u32[]{:S(2)}) %collective-permute-start.31) | collective-permute-done | bytes 294944 | tf_op jit(solution)/shard_map/ppermute | solution.py:185
  325.3 14.0 %collective-permute-done.35 = bf16[64,2304]{1,0:T(8,128)(2,1)S(1)} collective-permute-done((bf16[64,2304]{1,0:T(8,128)(2,1)S(1)}, bf16[64,2304]{1,0:T(8,128)(2,1)S(1)}, u32[]{:S(2)}, u32[]{:S(2)}) %collective-permute-start.35) | collective-permute-done | bytes 294944 | tf_op jit(solution)/shard_map/ppermute | solution.py:185
  351.2 9.1 %fusion.6 = (bf16[512,1152]{1,0:T(8,128)(2,1)S(1)}, bf16[512,1152]{1,0:T(8,128)(2,1)S(1)}) fusion(f32[512,2304]{1,0:T(8,128)} %copy-done.30, bf16[512,2304]{1,0:T(8,128)(2,1)} %pad_maximum_fusion.4, bf16[2304,1152]{1,0:T(8,128)(2,1)} %bitcast.327), kind=kOutput, calls=%fused_computation.28 | convolution fusion | flops 2732064768 | bytes 14745600 | tf_op jit(solution)/shard_map/dot_general | solution.py:23
  360.3 10.9 %convolution_convert_fusion.5 = bf16[512,2304]{1,0:T(8,128)(2,1)S(1)} fusion(bf16[2304,2304]{1,0:T(8,128)(2,1)} %bitcast.324, bf16[512,1152]{1,0:T(8,128)(2,1)S(1)} %get-tuple-element.86, bf16[512,1152]{1,0:T(8,128)(2,1)S(1)} %get-tuple-element.85), kind=kOutput, calls=%fused_computation.12 | convolution fusion | flops 5441716224 | bytes 15335424 | tf_op jit(solution)/shard_map/dot_general | solution.py:27
  374.6 7.5 %collective-permute-start.39 = (bf16[64,2304]{1,0:T(8,128)(2,1)S(1)}, bf16[64,2304]{1,0:T(8,128)(2,1)S(1)}, u32[]{:S(2)}, u32[]{:S(2)}) collective-permute-start(bf16[64,2304]{1,0:T(8,128)(2,1)S(1)} %get-tuple-element.171), channel_id=1, source_target_pairs={{0,12},{2,14},{4,0},{6,2},{8,4},{10,6},{12,8},{14,10},{16,28},{18,... | collective-permute-start | bytes 884744 | tf_op jit(solution)/shard_map/ppermute | solution.py:185
  396.8 10.3 %collective-permute-done.40 = bf16[64,2304]{1,0:T(8,128)(2,1)S(1)} collective-permute-done((bf16[64,2304]{1,0:T(8,128)(2,1)S(1)}, bf16[64,2304]{1,0:T(8,128)(2,1)S(1)}, u32[]{:S(2)}, u32[]{:S(2)}) %collective-permute-start.40) | collective-permute-done | bytes 294944 | tf_op jit(solution)/shard_map/ppermute | solution.py:185
  424.2 13.6 %collective-permute-done.43 = bf16[64,2304]{1,0:T(8,128)(2,1)} collective-permute-done((bf16[64,2304]{1,0:T(8,128)(2,1)}, bf16[64,2304]{1,0:T(8,128)(2,1)}, u32[]{:S(2)}, u32[]{:S(2)}) %collective-permute-start.43) | collective-permute-done | bytes 294944 | tf_op jit(solution)/shard_map/ppermute | solution.py:185
  447.9 8.9 %all-to-all-start = ((bf16[4,144,1152]{2,1,0:T(8,128)(2,1)}), bf16[4,144,1152]{2,1,0:T(8,128)(2,1)S(1)}, u32[]{:S(2)}, u32[]{:S(2)}) async-start(bf16[4,144,1152]{2,1,0:T(8,128)(2,1)} %bitcast.375), calls=%async_computation.1 | async-start | bytes 2654208 | tf_op jit(solution)/shard_map/all_to_all | solution.py:225
  474.1 14.1 %all-to-all-done.in_ref = bf16[4,144,1152]{2,1,0:T(8,128)(2,1)S(1)} async-done(((bf16[4,144,1152]{2,1,0:T(8,128)(2,1)}), bf16[4,144,1152]{2,1,0:T(8,128)(2,1)S(1)}, u32[]{:S(2)}, u32[]{:S(2)}) %all-to-all-start) | async-done | bytes 1327136 | tf_op jit(solution)/shard_map/all_to_all | solution.py:225
  505.4 17.5 %all-to-all-done.1.in_ref = bf16[4,144,1152]{2,1,0:T(8,128)(2,1)S(1)} async-done(((bf16[4,144,1152]{2,1,0:T(8,128)(2,1)}), bf16[4,144,1152]{2,1,0:T(8,128)(2,1)S(1)}, u32[]{:S(2)}, u32[]{:S(2)}) %all-to-all-start.1) | async-done | bytes 1327136 | tf_op jit(solution)/shard_map/all_to_all | solution.py:225
  542.1 14.3 %collective-permute-done.55 = f32[4,144]{1,0:T(4,128)S(1)} collective-permute-done((f32[4,144]{1,0:T(4,128)S(1)}, f32[4,144]{1,0:T(4,128)S(1)}, u32[]{:S(2)}, u32[]{:S(2)}) %collective-permute-start.55) | collective-permute-done | bytes 2336 | tf_op jit(solution)/shard_map/ppermute | solution.py:185
  556.5 17.5 %collective-permute-start.49 = (bf16[64,2304]{1,0:T(8,128)(2,1)}, bf16[64,2304]{1,0:T(8,128)(2,1)}, u32[]{:S(2)}, u32[]{:S(2)}) collective-permute-start(bf16[64,2304]{1,0:T(8,128)(2,1)} %get-tuple-element.169), channel_id=1, source_target_pairs={{0,4},{2,6},{4,8},{6,10},{8,12},{10,14},{12,0},{14,2},{16,20},{18,... | collective-permute-start | bytes 884744 | tf_op jit(solution)/shard_map/ppermute | solution.py:185
  580.6 17.4 %collective-permute-done.48 = bf16[64,2304]{1,0:T(8,128)(2,1)} collective-permute-done((bf16[64,2304]{1,0:T(8,128)(2,1)}, bf16[64,2304]{1,0:T(8,128)(2,1)}, u32[]{:S(2)}, u32[]{:S(2)}) %collective-permute-start.48) | collective-permute-done | bytes 294944 | tf_op jit(solution)/shard_map/ppermute | solution.py:185
  (547 shorter events, 304.7 us)
Async XLA Ops:
  7.2 129.2 %all-gather.9.cloned.1.call-start = ((), (), s32[]{:S(2)}) async-start(), calls=%async_computation.12 | async-start | bytes 8404992 | tf_op jit(solution)/shard_map/all_gather | solution.py:240
  23.2 34.6 %collective-permute-start.2 = (bf16[145,768]{1,0:T(8,128)(2,1)S(1)}, bf16[145,768]{1,0:T(8,128)(2,1)S(1)}, u32[]{:S(2)}, u32[]{:S(2)}) collective-permute-start(bf16[145,768]{1,0:T(8,128)(2,1)S(1)} %get-tuple-element.190), channel_id=1, source_target_pairs={{0,8},{2,10},{4,12},{6,14},{8,0},{10,2},{12,4},{14,6},{16,24},{18,... | collective-permute-start | bytes 668168 | tf_op jit(solution)/shard_map/ppermute | solution.py:185
  58.9 177.2 %all-gather.13.cloned.1.call-start = ((), (), s32[]{:S(2)}) async-start(), calls=%async_computation.14 | async-start | bytes 4976640 | tf_op jit(solution)/shard_map/all_gather | solution.py:266
  93.6 142.6 %all-gather.11.cloned.1.call-start = ((), (), s32[]{:S(2)}) async-start(), calls=%async_computation.13 | async-start | bytes 4976640 | tf_op jit(solution)/shard_map/all_gather | solution.py:266
  98.9 34.4 %collective-permute-start.23 = (bf16[3,144,512]{2,1,0:T(8,128)(2,1)}, bf16[3,144,512]{2,1,0:T(8,128)(2,1)}, u32[]{:S(2)}, u32[]{:S(2)}) collective-permute-start(bf16[3,144,512]{2,1,0:T(8,128)(2,1)} %pad_maximum_fusion.24), channel_id=1, source_target_pairs={{0,16},{2,18},{4,20},{6,22},{8,24},{10,26},{12,28},{14,30},{16,0},... | collective-permute-start | bytes 1327112 | tf_op jit(solution)/shard_map/ppermute | solution.py:185
  101.4 34.0 %collective-permute-start.22 = (bf16[3,144,640]{2,1,0:T(8,128)(2,1)}, bf16[3,144,640]{2,1,0:T(8,128)(2,1)S(1)}, u32[]{:S(2)}, u32[]{:S(2)}) collective-permute-start(bf16[3,144,640]{2,1,0:T(8,128)(2,1)} %get-tuple-element.187), channel_id=1, source_target_pairs={{0,2},{2,0},{4,6},{6,4},{8,10},{10,8},{12,14},{14,12},{16,18},{18,... | collective-permute-start | bytes 1658888 | tf_op jit(solution)/shard_map/ppermute | solution.py:185
  133.2 135.9 %all-gather.15.cloned.1.call-start = ((), (), s32[]{:S(2)}) async-start(), calls=%async_computation.15 | async-start | bytes 4976640 | tf_op jit(solution)/shard_map/all_gather | solution.py:266
  163.6 45.4 %collective-permute-start.27 = (bf16[144,1152]{1,0:T(8,128)(2,1)S(1)}, bf16[144,1152]{1,0:T(8,128)(2,1)S(1)}, u32[]{:S(2)}, u32[]{:S(2)}) collective-permute-start(bf16[144,1152]{1,0:T(8,128)(2,1)S(1)} %get-tuple-element.156), channel_id=1, source_target_pairs={{0,8},{2,10},{4,12},{6,14},{8,0},{10,2},{12,4},{14,6},{16,24},{18,... | collective-permute-start | bytes 995336 | tf_op jit(solution)/shard_map/ppermute | solution.py:185
  167.6 42.5 %collective-permute-start.28 = (bf16[144,1152]{1,0:T(8,128)(2,1)S(1)}, bf16[144,1152]{1,0:T(8,128)(2,1)S(1)}, u32[]{:S(2)}, u32[]{:S(2)}) collective-permute-start(bf16[144,1152]{1,0:T(8,128)(2,1)S(1)} %get-tuple-element.155), channel_id=1, source_target_pairs={{0,4},{2,6},{4,8},{6,10},{8,12},{10,14},{12,0},{14,2},{16,20},{18,... | collective-permute-start | bytes 995336 | tf_op jit(solution)/shard_map/ppermute | solution.py:185
  209.0 39.9 %collective-permute-start.25 = (bf16[2,3,144,512]{3,2,1,0:T(8,128)(2,1)}, bf16[2,3,144,512]{3,2,1,0:T(8,128)(2,1)}, u32[]{:S(2)}, u32[]{:S(2)}) collective-permute-start(bf16[2,3,144,512]{3,2,1,0:T(8,128)(2,1)} %pad_maximum_fusion.19), channel_id=1, source_target_pairs={{0,2},{2,0},{4,6},{6,4},{8,10},{10,8},{12,14},{14,12},{16,18},{18,... | collective-permute-start | bytes 2654216 | tf_op jit(solution)/shard_map/ppermute | solution.py:185
  210.2 40.3 %collective-permute-start.24 = (bf16[2,3,144,640]{3,2,1,0:T(8,128)(2,1)}, bf16[2,3,144,640]{3,2,1,0:T(8,128)(2,1)}, u32[]{:S(2)}, u32[]{:S(2)}) collective-permute-start(bf16[2,3,144,640]{3,2,1,0:T(8,128)(2,1)} %pad_maximum_fusion.10), channel_id=1, source_target_pairs={{0,16},{2,18},{4,20},{6,22},{8,24},{10,26},{12,28},{14,30},{16,0},... | collective-permute-start | bytes 3317768 | tf_op jit(solution)/shard_map/ppermute | solution.py:185
  211.7 197.2 %reduce-scatter.5.cloned.1.call-start = ((), (), s32[]{:S(2)}) async-start(), calls=%async_computation.8 | async-start | bytes 6635520 | tf_op jit(solution)/shard_map/reduce_scatter | solution.py:281
  351.1 137.0 %reduce-scatter.7.cloned.1.call-start = ((), (), s32[]{:S(2)}) async-start(), calls=%async_computation.9 | async-start | bytes 6635520 | tf_op jit(solution)/shard_map/reduce_scatter | solution.py:281
  408.9 118.4 %reduce-scatter.9.cloned.1.call-start = ((), (), s32[]{:S(2)}) async-start(), calls=%async_computation.10 | async-start | bytes 6635520 | tf_op jit(solution)/shard_map/reduce_scatter | solution.py:281
  447.9 40.3 %all-to-all-start = ((bf16[4,144,1152]{2,1,0:T(8,128)(2,1)}), bf16[4,144,1152]{2,1,0:T(8,128)(2,1)S(1)}, u32[]{:S(2)}, u32[]{:S(2)}) async-start(bf16[4,144,1152]{2,1,0:T(8,128)(2,1)} %bitcast.375), calls=%async_computation.1 | async-start | bytes 2654208 | tf_op jit(solution)/shard_map/all_to_all | solution.py:225
  488.2 34.7 %all-to-all-start.1 = ((bf16[4,144,1152]{2,1,0:T(8,128)(2,1)}), bf16[4,144,1152]{2,1,0:T(8,128)(2,1)S(1)}, u32[]{:S(2)}, u32[]{:S(2)}) async-start(bf16[4,144,1152]{2,1,0:T(8,128)(2,1)} %bitcast.376), calls=%async_computation.4 | async-start | bytes 2654208 | tf_op jit(solution)/shard_map/all_to_all | solution.py:225
  491.7 82.3 %reduce-scatter.11.cloned.1.call-start = ((), (), s32[]{:S(2)}) async-start(), calls=%async_computation.11 | async-start | bytes 7962624 | tf_op jit(solution)/shard_map/reduce_scatter | solution.py:255
  527.3 46.7 %all-to-all-start.2 = ((bf16[4,144,1152]{2,1,0:T(8,128)(2,1)}), bf16[4,144,1152]{2,1,0:T(8,128)(2,1)}, u32[]{:S(2)}, u32[]{:S(2)}) async-start(bf16[4,144,1152]{2,1,0:T(8,128)(2,1)} %bitcast.374), calls=%async_computation.5 | async-start | bytes 2654208 | tf_op jit(solution)/shard_map/all_to_all | solution.py:225
  536.5 37.5 %collective-permute-start.56 = (f32[4,144]{1,0:T(4,128)S(1)}, f32[4,144]{1,0:T(4,128)S(1)}, u32[]{:S(2)}, u32[]{:S(2)}) collective-permute-start(f32[4,144]{1,0:T(4,128)S(1)} %bitcast.403), channel_id=1, source_target_pairs={{0,8},{2,10},{4,12},{6,14},{8,0},{10,2},{12,4},{14,6},{16,24},{18,... | collective-permute-start | bytes 6920 | tf_op jit(solution)/shard_map/ppermute | solution.py:185
  538.6 35.4 %collective-permute-start.57 = (f32[4,144]{1,0:T(4,128)S(1)}, f32[4,144]{1,0:T(4,128)S(1)}, u32[]{:S(2)}, u32[]{:S(2)}) collective-permute-start(f32[4,144]{1,0:T(4,128)S(1)} %bitcast.404), channel_id=1, source_target_pairs={{0,12},{2,14},{4,0},{6,2},{8,4},{10,6},{12,8},{14,10},{16,28},{18,... | collective-permute-start | bytes 6920 | tf_op jit(solution)/shard_map/ppermute | solution.py:185
  540.7 39.9 %collective-permute-start.47 = (bf16[64,2304]{1,0:T(8,128)(2,1)}, bf16[64,2304]{1,0:T(8,128)(2,1)}, u32[]{:S(2)}, u32[]{:S(2)}) collective-permute-start(bf16[64,2304]{1,0:T(8,128)(2,1)} %get-tuple-element.168), channel_id=1, source_target_pairs={{0,12},{2,14},{4,0},{6,2},{8,4},{10,6},{12,8},{14,10},{16,28},{18,... | collective-permute-start | bytes 884744 | tf_op jit(solution)/shard_map/ppermute | solution.py:185
  541.0 57.0 %collective-permute-start.48 = (bf16[64,2304]{1,0:T(8,128)(2,1)}, bf16[64,2304]{1,0:T(8,128)(2,1)}, u32[]{:S(2)}, u32[]{:S(2)}) collective-permute-start(bf16[64,2304]{1,0:T(8,128)(2,1)} %get-tuple-element.170), channel_id=1, source_target_pairs={{0,8},{2,10},{4,12},{6,14},{8,0},{10,2},{12,4},{14,6},{16,24},{18,... | collective-permute-start | bytes 884744 | tf_op jit(solution)/shard_map/ppermute | solution.py:185
  556.5 41.5 %collective-permute-start.49 = (bf16[64,2304]{1,0:T(8,128)(2,1)}, bf16[64,2304]{1,0:T(8,128)(2,1)}, u32[]{:S(2)}, u32[]{:S(2)}) collective-permute-start(bf16[64,2304]{1,0:T(8,128)(2,1)} %get-tuple-element.169), channel_id=1, source_target_pairs={{0,4},{2,6},{4,8},{6,10},{8,12},{10,14},{12,0},{14,2},{16,20},{18,... | collective-permute-start | bytes 884744 | tf_op jit(solution)/shard_map/ppermute | solution.py:185
  574.0 33.3 %all-to-all-start.3 = ((bf16[4,144,768]{2,1,0:T(8,128)(2,1)}), bf16[4,144,768]{2,1,0:T(8,128)(2,1)S(1)}, u32[]{:S(2)}, u32[]{:S(2)}) async-start(bf16[4,144,768]{2,1,0:T(8,128)(2,1)} %bitcast.380), calls=%async_computation.7 | async-start | bytes 1769472 | tf_op jit(solution)/shard_map/all_to_all | solution.py:225
  (150 other events, 1459.8 us)
Sparse Core Ops, SparseCore 0:
  59.0 44.3 all-gather.8
  104.9 51.9 all-gather.12
  158.5 45.3 all-gather.10
  211.8 57.3 all-gather.14
  351.3 57.5 reduce-scatter.4
  411.1 52.3 reduce-scatter.6
  465.9 52.3 reduce-scatter.8
  523.1 42.2 reduce-scatter.10

commit v7 on v6

--- a/solution.py
+++ b/solution.py
@@ -524,7 +524,6 @@
     all_branch = jnp.concatenate([branch_blocks, net.swap(branch_blocks)])
 
     down_grad = net.by_square(product_left_t(all_branch, hidden_low), rows)
-    down_grad, all_branch = hold(down_grad, all_branch)
     down_grad = net.grads_out(down_grad, rows)
     d_hidden = product(all_branch, down_units)
     _, pull = jax.vjp(geglu, gate_in, upward)

time: 635 us -> 628 us (0.989)
  starting transfers between devices: 149 us -> 120 us
  waiting for transfers between devices: 257 us -> 282 us
    ppermute x47, waiting for transfers between devices: 211 us -> 227 us  [send(): return lax.ppermute(block, chip_axes, pairs)]
    ppermute x11, starting transfers between devices: 26.9 us -> 13.3 us  [swap(): return lax.ppermute(block, 'tensor', [(0, 1), (1, 0)])]
    ppermute x47, starting transfers between devices: 100 us -> 91.7 us  [send(): return lax.ppermute(block, chip_axes, pairs)]
  transfers between devices with their start and end apart: 70 -> 70, of which waited for: 32 -> 33; matrix products, arithmetic and copies ran while one was open for 23% -> 23% of each run, Pallas kernels for 2% -> 2%
where the time goes in v7:
time: 628 us; the launch traced here: 620 us
  waiting for transfers between devices  282 us (45%)
  starting transfers between devices  120 us (19%)
  local copies, waits for them, and re-layouts  69.6 us (11%)
  other arithmetic  61.9 us (10%)
  matrix products  58.4 us (9%)
  between operations  16.5 us (3%)
  Pallas kernels  11.5 us (2%)
    ppermute x47, waiting for transfers between devices, send(): return lax.ppermute(block, chip_axes, pairs)  227 us
    ppermute x47, starting transfers between devices, send(): return lax.ppermute(block, chip_axes, pairs)  91.7 us
    all_to_all x4, waiting for transfers between devices, exchanged(): lax.all_to_all(array, 'context', 0, 0, tiled=True, axis_index_groups=groups)  40.8 us
    unnamed x221, local copies, waits for them, and re-layouts  32.6 us
    dot_general x8, matrix products, product(): return jnp.dot(left_side, right_side, preferred_element_type=wide)  21.7 us
    dot_general x7, matrix products, product_right_t(): lax.dot_general(left_side, right_side, (((1,), (1,)), ((), ())), preferre...  20 us
    dot_general x8, matrix products, product_left_t(): lax.dot_general(left_side, right_side, (((0,), (0,)), ((), ())), preferre...  16.8 us
    all_to_all x4, starting transfers between devices, exchanged(): lax.all_to_all(array, 'context', 0, 0, tiled=True, axis_index_groups=groups)  15.1 us
  transfers between devices with their start and end apart: 70, of which 33 were waited for; matrix products, arithmetic and copies ran while one was open for 23% of the time, Pallas kernels for 2%

profile of v7, /device:TPU:1, one launch (start us, length us, event | category | flops | bytes accessed | tf_op | source)
XLA Modules:
  0.0 619.9 jit_solution(15427940384283361749)
XLA Ops:
  24.7 23.0 %collective-permute-done.5 = bf16[64,2304]{1,0:T(8,128)(2,1)S(1)} collective-permute-done((bf16[64,2304]{1,0:T(8,128)(2,1)S(1)}, bf16[64,2304]{1,0:T(8,128)(2,1)S(1)}, u32[]{:S(2)}, u32[]{:S(2)}) %collective-permute-start.5) | collective-permute-done | bytes 294944 | tf_op jit(solution)/shard_map/ppermute | solution.py:185
  54.0 5.9 collective-permute-start.17
  63.0 6.6 %collective-permute-done.17 = bf16[144,1152]{1,0:T(8,128)(2,1)S(1)} collective-permute-done((bf16[144,1152]{1,0:T(8,128)(2,1)S(1)}, bf16[144,1152]{1,0:T(8,128)(2,1)S(1)}, u32[]{:S(2)}, u32[]{:S(2)}) %collective-permute-start.17) | collective-permute-done | bytes 331808 | tf_op jit(solution)/shard_map/ppermute | solution.py:185
  69.7 15.6 %collective-permute-done.16 = bf16[144,1152]{1,0:T(8,128)(2,1)S(1)} collective-permute-done((bf16[144,1152]{1,0:T(8,128)(2,1)S(1)}, bf16[144,1152]{1,0:T(8,128)(2,1)S(1)}, u32[]{:S(2)}, u32[]{:S(2)}) %collective-permute-start.16) | collective-permute-done | bytes 331808 | tf_op jit(solution)/shard_map/ppermute | solution.py:185
  89.0 7.5 %collective-permute-start.20 = (bf16[144,1152]{1,0:T(8,128)(2,1)}, bf16[144,1152]{1,0:T(8,128)(2,1)}, u32[]{:S(2)}, u32[]{:S(2)}) collective-permute-start(bf16[144,1152]{1,0:T(8,128)(2,1)} %get-tuple-element.158), channel_id=1, source_target_pairs={{0,4},{2,6},{4,8},{6,10},{8,12},{10,14},{12,0},{14,2},{16,20},{18,... | collective-permute-start | bytes 995336 | tf_op jit(solution)/shard_map/ppermute | solution.py:185
  106.4 10.2 %collective-permute-done.19 = bf16[144,1152]{1,0:T(8,128)(2,1)} collective-permute-done((bf16[144,1152]{1,0:T(8,128)(2,1)}, bf16[144,1152]{1,0:T(8,128)(2,1)}, u32[]{:S(2)}, u32[]{:S(2)}) %collective-permute-start.19) | collective-permute-done | bytes 331808 | tf_op jit(solution)/shard_map/ppermute | solution.py:185
  150.5 7.4 %collective-permute-start.28 = (bf16[144,1152]{1,0:T(8,128)(2,1)S(1)}, bf16[144,1152]{1,0:T(8,128)(2,1)S(1)}, u32[]{:S(2)}, u32[]{:S(2)}) collective-permute-start(bf16[144,1152]{1,0:T(8,128)(2,1)S(1)} %get-tuple-element.151), channel_id=1, source_target_pairs={{0,4},{2,6},{4,8},{6,10},{8,12},{10,14},{12,0},{14,2},{16,20},{18,... | collective-permute-start | bytes 995336 | tf_op jit(solution)/shard_map/ppermute | solution.py:185
  170.4 5.8 collective-permute-start.11
  188.3 21.0 %collective-permute-done.10 = bf16[64,2304]{1,0:T(8,128)(2,1)S(1)} collective-permute-done((bf16[64,2304]{1,0:T(8,128)(2,1)S(1)}, bf16[64,2304]{1,0:T(8,128)(2,1)S(1)}, u32[]{:S(2)}, u32[]{:S(2)}) %collective-permute-start.10) | collective-permute-done | bytes 294944 | tf_op jit(solution)/shard_map/ppermute | solution.py:185
  225.0 19.7 %collective-permute-done.13 = bf16[64,2304]{1,0:T(8,128)(2,1)S(1)} collective-permute-done((bf16[64,2304]{1,0:T(8,128)(2,1)S(1)}, bf16[64,2304]{1,0:T(8,128)(2,1)S(1)}, u32[]{:S(2)}, u32[]{:S(2)}) %collective-permute-start.13) | collective-permute-done | bytes 294944 | tf_op jit(solution)/shard_map/ppermute | solution.py:185
  258.6 5.6 fusion.102
  284.4 7.2 %collective-permute-done.32 = bf16[64,2304]{1,0:T(8,128)(2,1)S(1)} collective-permute-done((bf16[64,2304]{1,0:T(8,128)(2,1)}, bf16[64,2304]{1,0:T(8,128)(2,1)S(1)}, u32[]{:S(2)}, u32[]{:S(2)}) %collective-permute-start.32) | collective-permute-done | bytes 294944 | tf_op jit(solution)/shard_map/ppermute | solution.py:185
  291.6 11.7 %collective-permute-done.31 = bf16[64,2304]{1,0:T(8,128)(2,1)S(1)} collective-permute-done((bf16[64,2304]{1,0:T(8,128)(2,1)}, bf16[64,2304]{1,0:T(8,128)(2,1)S(1)}, u32[]{:S(2)}, u32[]{:S(2)}) %collective-permute-start.31) | collective-permute-done | bytes 294944 | tf_op jit(solution)/shard_map/ppermute | solution.py:185
  306.4 5.6 collective-permute-start.36
  319.4 19.8 %collective-permute-done.35 = bf16[64,2304]{1,0:T(8,128)(2,1)S(1)} collective-permute-done((bf16[64,2304]{1,0:T(8,128)(2,1)S(1)}, bf16[64,2304]{1,0:T(8,128)(2,1)S(1)}, u32[]{:S(2)}, u32[]{:S(2)}) %collective-permute-start.35) | collective-permute-done | bytes 294944 | tf_op jit(solution)/shard_map/ppermute | solution.py:185
  350.9 9.4 %fusion.6 = (bf16[512,1152]{1,0:T(8,128)(2,1)S(1)}, bf16[512,1152]{1,0:T(8,128)(2,1)S(1)}) fusion(f32[512,2304]{1,0:T(8,128)} %copy-done.31, bf16[2304,1152]{1,0:T(8,128)(2,1)} %bitcast.326, bf16[256,2304]{1,0:T(8,128)(2,1)} %copy-done.103, bf16[256,2304]{1,0:T(8,128)(2,1)S(1)} %bitcast.377), kind=kOutput, calls=%fused_computation.28 | convolution fusion | flops 2736783360 | bytes 14745600 | tf_op jit(solution)/shard_map/dot_general | solution.py:23
  360.4 10.1 %convolution_convert_fusion.5 = bf16[512,2304]{1,0:T(8,128)(2,1)S(1)} fusion(bf16[2304,2304]{1,0:T(8,128)(2,1)} %bitcast.323, bf16[512,1152]{1,0:T(8,128)(2,1)S(1)} %get-tuple-element.83, bf16[512,1152]{1,0:T(8,128)(2,1)S(1)} %get-tuple-element.82), kind=kOutput, calls=%fused_computation.12 | convolution fusion | flops 5441716224 | bytes 15335424 | tf_op jit(solution)/shard_map/dot_general | solution.py:27
  414.4 19.3 %collective-permute-done.43 = bf16[64,2304]{1,0:T(8,128)(2,1)} collective-permute-done((bf16[64,2304]{1,0:T(8,128)(2,1)}, bf16[64,2304]{1,0:T(8,128)(2,1)}, u32[]{:S(2)}, u32[]{:S(2)}) %collective-permute-start.43) | collective-permute-done | bytes 294944 | tf_op jit(solution)/shard_map/ppermute | solution.py:185
  467.5 13.6 %all-to-all-done.in_ref = bf16[4,144,1152]{2,1,0:T(8,128)(2,1)S(1)} async-done(((bf16[4,144,1152]{2,1,0:T(8,128)(2,1)}), bf16[4,144,1152]{2,1,0:T(8,128)(2,1)S(1)}, u32[]{:S(2)}, u32[]{:S(2)}) %all-to-all-start) | async-done | bytes 1327136 | tf_op jit(solution)/shard_map/all_to_all | solution.py:225
  498.2 17.6 %all-to-all-done.1.in_ref = bf16[4,144,1152]{2,1,0:T(8,128)(2,1)S(1)} async-done(((bf16[4,144,1152]{2,1,0:T(8,128)(2,1)}), bf16[4,144,1152]{2,1,0:T(8,128)(2,1)S(1)}, u32[]{:S(2)}, u32[]{:S(2)}) %all-to-all-start.1) | async-done | bytes 1327136 | tf_op jit(solution)/shard_map/all_to_all | solution.py:225
  535.7 10.2 %collective-permute-done.57 = f32[4,144]{1,0:T(4,128)S(1)} collective-permute-done((f32[4,144]{1,0:T(4,128)S(1)}, f32[4,144]{1,0:T(4,128)S(1)}, u32[]{:S(2)}, u32[]{:S(2)}) %collective-permute-start.57) | collective-permute-done | bytes 2336 | tf_op jit(solution)/shard_map/ppermute | solution.py:185
  549.6 19.2 %collective-permute-done.56 = f32[4,144]{1,0:T(4,128)S(1)} collective-permute-done((f32[4,144]{1,0:T(4,128)S(1)}, f32[4,144]{1,0:T(4,128)S(1)}, u32[]{:S(2)}, u32[]{:S(2)}) %collective-permute-start.56) | collective-permute-done | bytes 2336 | tf_op jit(solution)/shard_map/ppermute | solution.py:185
  575.1 11.9 %collective-permute-done.47 = bf16[64,2304]{1,0:T(8,128)(2,1)} collective-permute-done((bf16[64,2304]{1,0:T(8,128)(2,1)}, bf16[64,2304]{1,0:T(8,128)(2,1)}, u32[]{:S(2)}, u32[]{:S(2)}) %collective-permute-start.47) | collective-permute-done | bytes 294944 | tf_op jit(solution)/shard_map/ppermute | solution.py:185
  590.6 9.6 %all-to-all-done.3 = bf16[4,144,768]{2,1,0:T(8,128)(2,1)S(1)} async-done(((bf16[4,144,768]{2,1,0:T(8,128)(2,1)}), bf16[4,144,768]{2,1,0:T(8,128)(2,1)S(1)}, u32[]{:S(2)}, u32[]{:S(2)}) %all-to-all-start.3) | async-done | bytes 884768 | tf_op jit(solution)/shard_map/all_to_all | solution.py:225
  (546 shorter events, 309.6 us)
Async XLA Ops:
  7.2 115.2 %all-gather.9.cloned.1.call-start = ((), (), s32[]{:S(2)}) async-start(), calls=%async_computation.12 | async-start | bytes 8404992 | tf_op jit(solution)/shard_map/all_gather | solution.py:240
  13.1 34.6 %collective-permute-start.5 = (bf16[64,2304]{1,0:T(8,128)(2,1)S(1)}, bf16[64,2304]{1,0:T(8,128)(2,1)S(1)}, u32[]{:S(2)}, u32[]{:S(2)}) collective-permute-start(bf16[64,2304]{1,0:T(8,128)(2,1)S(1)} %bitcast.344), channel_id=1, source_target_pairs={{0,8},{2,10},{4,12},{6,14},{8,0},{10,2},{12,4},{14,6},{16,24},{18,... | collective-permute-start | bytes 884744 | tf_op jit(solution)/shard_map/ppermute | solution.py:185
  13.1 34.6 %collective-permute-start.4 = (bf16[64,2304]{1,0:T(8,128)(2,1)S(1)}, bf16[64,2304]{1,0:T(8,128)(2,1)S(1)}, u32[]{:S(2)}, u32[]{:S(2)}) collective-permute-start(bf16[64,2304]{1,0:T(8,128)(2,1)S(1)} %bitcast.345), channel_id=1, source_target_pairs={{0,4},{2,6},{4,8},{6,10},{8,12},{10,14},{12,0},{14,2},{16,20},{18,... | collective-permute-start | bytes 884744 | tf_op jit(solution)/shard_map/ppermute | solution.py:185
  20.3 31.5 %collective-permute-start.3 = (bf16[145,768]{1,0:T(8,128)(2,1)S(1)}, bf16[145,768]{1,0:T(8,128)(2,1)S(1)}, u32[]{:S(2)}, u32[]{:S(2)}) collective-permute-start(bf16[145,768]{1,0:T(8,128)(2,1)S(1)} %get-tuple-element.185), channel_id=1, source_target_pairs={{0,4},{2,6},{4,8},{6,10},{8,12},{10,14},{12,0},{14,2},{16,20},{18,... | collective-permute-start | bytes 668168 | tf_op jit(solution)/shard_map/ppermute | solution.py:185
  22.5 30.2 %collective-permute-start.2 = (bf16[145,768]{1,0:T(8,128)(2,1)S(1)}, bf16[145,768]{1,0:T(8,128)(2,1)S(1)}, u32[]{:S(2)}, u32[]{:S(2)}) collective-permute-start(bf16[145,768]{1,0:T(8,128)(2,1)S(1)} %get-tuple-element.186), channel_id=1, source_target_pairs={{0,8},{2,10},{4,12},{6,14},{8,0},{10,2},{12,4},{14,6},{16,24},{18,... | collective-permute-start | bytes 668168 | tf_op jit(solution)/shard_map/ppermute | solution.py:185
  53.8 192.0 %all-gather.11.cloned.1.call-start = ((), (), s32[]{:S(2)}) async-start(), calls=%async_computation.13 | async-start | bytes 4976640 | tf_op jit(solution)/shard_map/all_gather | solution.py:266
  86.4 159.5 %all-gather.13.cloned.1.call-start = ((), (), s32[]{:S(2)}) async-start(), calls=%async_computation.14 | async-start | bytes 4976640 | tf_op jit(solution)/shard_map/all_gather | solution.py:266
  120.2 148.1 %all-gather.15.cloned.1.call-start = ((), (), s32[]{:S(2)}) async-start(), calls=%async_computation.15 | async-start | bytes 4976640 | tf_op jit(solution)/shard_map/all_gather | solution.py:266
  176.2 33.2 %collective-permute-start.10 = (bf16[64,2304]{1,0:T(8,128)(2,1)S(1)}, bf16[64,2304]{1,0:T(8,128)(2,1)S(1)}, u32[]{:S(2)}, u32[]{:S(2)}) collective-permute-start(bf16[64,2304]{1,0:T(8,128)(2,1)S(1)} %get-tuple-element.175), channel_id=1, source_target_pairs={{0,8},{2,10},{4,12},{6,14},{8,0},{10,2},{12,4},{14,6},{16,24},{18,... | collective-permute-start | bytes 884744 | tf_op jit(solution)/shard_map/ppermute | solution.py:185
  184.5 64.0 %collective-permute-start.25 = (bf16[2,3,144,512]{3,2,1,0:T(8,128)(2,1)}, bf16[2,3,144,512]{3,2,1,0:T(8,128)(2,1)}, u32[]{:S(2)}, u32[]{:S(2)}) collective-permute-start(bf16[2,3,144,512]{3,2,1,0:T(8,128)(2,1)} %pad_maximum_fusion.21), channel_id=1, source_target_pairs={{0,2},{2,0},{4,6},{6,4},{8,10},{10,8},{12,14},{14,12},{16,18},{18,... | collective-permute-start | bytes 2654216 | tf_op jit(solution)/shard_map/ppermute | solution.py:185
  184.5 65.7 %collective-permute-start.24 = (bf16[2,3,144,640]{3,2,1,0:T(8,128)(2,1)}, bf16[2,3,144,640]{3,2,1,0:T(8,128)(2,1)}, u32[]{:S(2)}, u32[]{:S(2)}) collective-permute-start(bf16[2,3,144,640]{3,2,1,0:T(8,128)(2,1)} %pad_maximum_fusion.12), channel_id=1, source_target_pairs={{0,16},{2,18},{4,20},{6,22},{8,24},{10,26},{12,28},{14,30},{16,0},... | collective-permute-start | bytes 3317768 | tf_op jit(solution)/shard_map/ppermute | solution.py:185
  187.0 213.5 %reduce-scatter.5.cloned.1.call-start = ((), (), s32[]{:S(2)}) async-start(), calls=%async_computation.8 | async-start | bytes 6635520 | tf_op jit(solution)/shard_map/reduce_scatter | solution.py:281
  350.9 130.2 %reduce-scatter.7.cloned.1.call-start = ((), (), s32[]{:S(2)}) async-start(), calls=%async_computation.9 | async-start | bytes 6635520 | tf_op jit(solution)/shard_map/reduce_scatter | solution.py:281
  400.6 119.6 %reduce-scatter.9.cloned.1.call-start = ((), (), s32[]{:S(2)}) async-start(), calls=%async_computation.10 | async-start | bytes 6635520 | tf_op jit(solution)/shard_map/reduce_scatter | solution.py:281
  445.5 35.6 %all-to-all-start = ((bf16[4,144,1152]{2,1,0:T(8,128)(2,1)}), bf16[4,144,1152]{2,1,0:T(8,128)(2,1)S(1)}, u32[]{:S(2)}, u32[]{:S(2)}) async-start(bf16[4,144,1152]{2,1,0:T(8,128)(2,1)} %bitcast.371), calls=%async_computation.1 | async-start | bytes 2654208 | tf_op jit(solution)/shard_map/all_to_all | solution.py:225
  481.1 34.7 %all-to-all-start.1 = ((bf16[4,144,1152]{2,1,0:T(8,128)(2,1)}), bf16[4,144,1152]{2,1,0:T(8,128)(2,1)S(1)}, u32[]{:S(2)}, u32[]{:S(2)}) async-start(bf16[4,144,1152]{2,1,0:T(8,128)(2,1)} %bitcast.372), calls=%async_computation.4 | async-start | bytes 2654208 | tf_op jit(solution)/shard_map/all_to_all | solution.py:225
  484.7 84.2 %reduce-scatter.11.cloned.1.call-start = ((), (), s32[]{:S(2)}) async-start(), calls=%async_computation.11 | async-start | bytes 7962624 | tf_op jit(solution)/shard_map/reduce_scatter | solution.py:255
  520.2 48.6 %all-to-all-start.2 = ((bf16[4,144,1152]{2,1,0:T(8,128)(2,1)}), bf16[4,144,1152]{2,1,0:T(8,128)(2,1)}, u32[]{:S(2)}, u32[]{:S(2)}) async-start(bf16[4,144,1152]{2,1,0:T(8,128)(2,1)} %bitcast.370), calls=%async_computation.5 | async-start | bytes 2654208 | tf_op jit(solution)/shard_map/all_to_all | solution.py:225
  531.2 37.6 %collective-permute-start.56 = (f32[4,144]{1,0:T(4,128)S(1)}, f32[4,144]{1,0:T(4,128)S(1)}, u32[]{:S(2)}, u32[]{:S(2)}) collective-permute-start(f32[4,144]{1,0:T(4,128)S(1)} %bitcast.402), channel_id=1, source_target_pairs={{0,8},{2,10},{4,12},{6,14},{8,0},{10,2},{12,4},{14,6},{16,24},{18,... | collective-permute-start | bytes 6920 | tf_op jit(solution)/shard_map/ppermute | solution.py:185
  531.2 37.6 %collective-permute-start.55 = (f32[4,144]{1,0:T(4,128)S(1)}, f32[4,144]{1,0:T(4,128)S(1)}, u32[]{:S(2)}, u32[]{:S(2)}) collective-permute-start(f32[4,144]{1,0:T(4,128)S(1)} %bitcast.403), channel_id=1, source_target_pairs={{0,4},{2,6},{4,8},{6,10},{8,12},{10,14},{12,0},{14,2},{16,20},{18,... | collective-permute-start | bytes 6920 | tf_op jit(solution)/shard_map/ppermute | solution.py:185
  532.7 42.0 %collective-permute-start.49 = (bf16[64,2304]{1,0:T(8,128)(2,1)}, bf16[64,2304]{1,0:T(8,128)(2,1)}, u32[]{:S(2)}, u32[]{:S(2)}) collective-permute-start(bf16[64,2304]{1,0:T(8,128)(2,1)} %get-tuple-element.165), channel_id=1, source_target_pairs={{0,4},{2,6},{4,8},{6,10},{8,12},{10,14},{12,0},{14,2},{16,20},{18,... | collective-permute-start | bytes 884744 | tf_op jit(solution)/shard_map/ppermute | solution.py:185
  534.8 40.3 %collective-permute-start.48 = (bf16[64,2304]{1,0:T(8,128)(2,1)}, bf16[64,2304]{1,0:T(8,128)(2,1)}, u32[]{:S(2)}, u32[]{:S(2)}) collective-permute-start(bf16[64,2304]{1,0:T(8,128)(2,1)} %get-tuple-element.166), channel_id=1, source_target_pairs={{0,8},{2,10},{4,12},{6,14},{8,0},{10,2},{12,4},{14,6},{16,24},{18,... | collective-permute-start | bytes 884744 | tf_op jit(solution)/shard_map/ppermute | solution.py:185
  545.9 41.2 %collective-permute-start.47 = (bf16[64,2304]{1,0:T(8,128)(2,1)}, bf16[64,2304]{1,0:T(8,128)(2,1)}, u32[]{:S(2)}, u32[]{:S(2)}) collective-permute-start(bf16[64,2304]{1,0:T(8,128)(2,1)} %get-tuple-element.164), channel_id=1, source_target_pairs={{0,12},{2,14},{4,0},{6,2},{8,4},{10,6},{12,8},{14,10},{16,28},{18,... | collective-permute-start | bytes 884744 | tf_op jit(solution)/shard_map/ppermute | solution.py:185
  568.9 31.4 %all-to-all-start.3 = ((bf16[4,144,768]{2,1,0:T(8,128)(2,1)}), bf16[4,144,768]{2,1,0:T(8,128)(2,1)S(1)}, u32[]{:S(2)}, u32[]{:S(2)}) async-start(bf16[4,144,768]{2,1,0:T(8,128)(2,1)} %bitcast.379), calls=%async_computation.7 | async-start | bytes 1769472 | tf_op jit(solution)/shard_map/all_to_all | solution.py:225
  (150 other events, 1478.9 us)
Sparse Core Ops, SparseCore 0:
  54.0 50.6 all-gather.8
  106.2 42.8 all-gather.10
  150.7 46.4 all-gather.12
  198.6 50.7 all-gather.14
  351.0 49.4 reduce-scatter.4
  402.8 52.4 reduce-scatter.6
  457.6 52.3 reduce-scatter.8
  516.0 41.9 reduce-scatter.10
